TPU v7x, 256 devices: a whole 4x4x8 slice. The times are simulated.
256 devices in a mesh: dp: 16 (over x_lo, z), space: 16 (over y, x_hi, core).
Axes of the slice: x: 4 (x_hi: 2, x_lo: 2; x = x_hi * 2 + x_lo), y: 4, z: 8, core: 2. Of those that a mesh axis runs over, the one named last changes fastest.
Arguments:
- volume: bfloat16 [16, 32, 32, 8, 256], P('dp', None, 'space'), may hold values from -6 to 6
- conv_weight: bfloat16 [64, 864], replicated, may hold values from -0.21875 to 0.21875
- strided_weight: bfloat16 [128, 512], P('space'), may hold values from -0.25 to 0.25
- cotangent: bfloat16 [16, 128, 16, 4, 128], P('dp', 'space'), may hold values from -6 to 6
Outputs:
- output: bfloat16 [16, 128, 16, 4, 128], P('dp', 'space')
- vol_grad: bfloat16 [16, 32, 32, 8, 256], P('dp', None, 'space')
- conv_grad: float32 [64, 864], replicated
- strided_grad: float32 [128, 512], P('space')
All inputs are finite; a program needn't handle non-finite values.
Results may differ from a plain program's by a relative error of at most 0.0095.
Values may be sent and summed in bfloat16 or wider, within the bound.
No kernel may reach another device: no remote copies, remote signals or barrier semaphores. Data moves between devices by JAX's collectives and lax.ppermute only.
A program may use at most 128 MiB of HBM per device.

v0:
```python
import math

import jax
import jax.numpy as jnp
from jax import lax
from jax.sharding import PartitionSpec as P

root_two_pi = 0.7978845608028654


def extended(cells, sides, width):
    for axis, dim in sides:
        count = lax.axis_size(axis)
        ends = count - 1
        head = lax.slice_in_dim(cells, 0, width, axis=dim)
        tail = lax.slice_in_dim(cells, cells.shape[dim] - width, cells.shape[dim], axis=dim)
        cells = jnp.concatenate(
            [
                lax.ppermute(tail, axis, [(i, (i + 1) % count) for i in range(ends)]),
                cells,
                lax.ppermute(head, axis, [((i + 1) % count, i) for i in range(ends)]),
            ],
            axis=dim,
        )
    return cells


def gelu_value(field):
    inner = root_two_pi * (field + 0.044715 * field * field * field)
    return 0.5 * field * (1.0 + jnp.tanh(inner))


def gelu_slope(field):
    inner = root_two_pi * (field + 0.044715 * field * field * field)
    hyper = jnp.tanh(inner)
    return 0.5 * (1.0 + hyper) + 0.5 * field * (1.0 - hyper * hyper) * root_two_pi * (
        1.0 + 3.0 * 0.044715 * field * field
    )


def tap_stack(padded):
    depth_len = padded.shape[2] - 2
    row_count, col_count = (padded.shape[3], padded.shape[4])
    framed = jnp.pad(padded, ((0, 0), (0, 0), (0, 0), (1, 1), (1, 1)))
    pieces = [
        framed[:, :, a : a + depth_len, b : b + row_count, e : e + col_count]
        for a in range(3)
        for b in range(3)
        for e in range(3)
    ]
    return jnp.concatenate(pieces, axis=1)


def to_blocks(field):
    samples, channels = (field.shape[0], field.shape[1])
    row_count, col_count = (field.shape[-2], field.shape[-1])
    pairs = field.size // (samples * channels * row_count * col_count * 2)
    shaped = field.reshape(samples, channels, pairs, 2, row_count // 2, 2, col_count // 2, 2)
    return shaped.transpose(0, 3, 5, 7, 1, 2, 4, 6).reshape(
        samples, 8 * channels, pairs, row_count // 2, col_count // 2
    )


def from_blocks(blocked):
    samples, widened, pairs, half_rows, half_cols = blocked.shape
    channels = widened // 8
    shaped = blocked.reshape(samples, 2, 2, 2, channels, pairs, half_rows, half_cols)
    return shaped.transpose(0, 4, 5, 1, 6, 2, 7, 3).reshape(
        samples, channels, 2 * pairs, 2 * half_rows, 2 * half_cols
    )


def shards(volume, conv_weight, strided_weight, cotangent):
    sample_count, in_channels, depth_len, row_count, col_count = volume.shape
    mid_channels = conv_weight.shape[0]
    cells_total = (
        sample_count
        * lax.axis_size("dp")
        * depth_len
        * lax.axis_size("space")
        * row_count
        * col_count
    )
    padded = extended(volume, (("space", 2),), 1)
    vol_taps = tap_stack(padded)
    pre = jnp.einsum("ok,skdrw->sodrw", conv_weight, vol_taps, preferred_element_type=jnp.float32)
    hidden = gelu_value(pre).astype(jnp.bfloat16)
    all_filters = lax.all_gather(strided_weight, "space", axis=0, tiled=True)
    paired = hidden.reshape(sample_count, mid_channels, depth_len // 2, 2, row_count, col_count)
    piece_blocks = to_blocks(lax.all_gather(paired, "space", axis=2, tiled=True))
    piece_out = jnp.einsum(
        "ok,skdrw->sodrw", strided_weight, piece_blocks, preferred_element_type=jnp.float32
    ).astype(jnp.bfloat16)
    grad_total = jnp.einsum(
        "sodrw,skdrw->ok", cotangent, piece_blocks, preferred_element_type=jnp.float32
    )
    cot_slab = lax.all_to_all(cotangent, "space", split_axis=2, concat_axis=1, tiled=True)
    hidden_grad = from_blocks(
        jnp.einsum("ok,sodrw->skdrw", all_filters, cot_slab, preferred_element_type=jnp.float32)
    )
    pre_grad = (hidden_grad * gelu_slope(pre)).astype(jnp.bfloat16)
    grad_padded = extended(pre_grad, (("space", 2),), 1)
    conv_terms = jnp.einsum(
        "sodrw,skdrw->ok", pre_grad, vol_taps, preferred_element_type=jnp.float32
    )
    conv_grad = lax.psum(conv_terms, ("dp", "space")) / math.sqrt(cells_total)
    strided_grad = lax.psum(grad_total, "dp") / math.sqrt(cells_total / 8)
    flipped = (
        conv_weight.reshape(mid_channels, 27, in_channels)[:, ::-1, :]
        .transpose(2, 1, 0)
        .reshape(in_channels, 27 * mid_channels)
    )
    vol_grad = jnp.einsum(
        "ck,skdrw->scdrw", flipped, tap_stack(grad_padded), preferred_element_type=jnp.float32
    ).astype(jnp.bfloat16)
    return (piece_out, vol_grad, conv_grad, strided_grad)


def solution(mesh):
    return jax.shard_map(
        shards,
        mesh=mesh,
        in_specs=(
            P("dp", None, "space", None, None),
            P(),
            P("space", None),
            P("dp", "space", None, None, None),
        ),
        out_specs=(
            P("dp", "space", None, None, None),
            P("dp", None, "space", None, None),
            P(),
            P("space", None),
        ),
        check_vma=False,
    )
```

profile of v0, /device:TPU:8, one launch (start us, length us, event | category | flops | bytes accessed | tf_op | source)
XLA Modules:
  0.0 470.4 jit_solution(16632709884277353590)
XLA Ops:
  8.0 1.6 copy.48
  9.6 7.4 %all-to-all-start = ((bf16[1,8,16,4,128]{4,1,3,0,2:T(8,128)(2,1)}), bf16[1,8,16,4,128]{4,1,3,0,2:T(8,128)(2,1)S(1)}, u32[]{:S(2)}, u32[]{:S(2)}) async-start(bf16[1,8,16,4,128]{4,1,3,0,2:T(8,128)(2,1)} %copy.48), calls=%async_computation | async-start | bytes 262144 | tf_op jit(solution)/shard_map/all_to_all | solution.py:97
  17.1 1.0 copy.39
  18.1 0.7 fusion.51
  18.8 2.0 collective-permute-start
  20.9 5.9 %collective-permute-start.1 = (bf16[1,32,1,8,256]{4,1,3,2,0:T(8,128)(2,1)}, bf16[1,32,1,8,256]{4,1,3,2,0:T(8,128)(2,1)S(1)}, u32[]{:S(2)}, u32[]{:S(2)}) collective-permute-start(bf16[1,32,1,8,256]{4,1,3,2,0:T(8,128)(2,1)} %get-tuple-element.21), channel_id=1, source_target_pairs={{1,0},{2,1},{3,2},{4,3},{5,4},{6,5},{7,6},{8,7},{9,8},{10,9},{11,1... | collective-permute-start | bytes 393224 | tf_op jit(solution)/shard_map/ppermute | solution.py:21
  26.8 21.6 %all_gather.7 = bf16[128,512]{1,0:T(8,128)(2,1)S(1)} all-gather(bf16[8,512]{1,0:T(8,128)(2,1)} %param.6), channel_id=1, replica_groups=mesh['dp'=16,'space'=16] {'space'}, dimensions={0}, use_global_device_ids=true | all-gather | bytes 139264 | tf_op jit(solution)/shard_map/all_gather | solution.py:88
  48.5 0.3 convolution_bitcast_fusion
  48.8 0.3 copy.51
  49.1 1.2 copy.52
  50.3 0.6 copy.53
  50.9 1.3 select_maximum_fusion.2
  52.3 0.1 slice_dynamic-update-slice_fusion.46
  52.4 0.1 slice_dynamic-update-slice_fusion.45
  52.6 0.9 fusion.42
  53.5 0.1 slice_dynamic-update-slice_fusion.43
  53.7 0.1 slice_dynamic-update-slice_fusion.41
  53.9 0.1 slice_dynamic-update-slice_fusion.40
  54.0 0.1 slice_dynamic-update-slice_fusion.38
  54.2 0.1 slice_dynamic-update-slice_fusion.37
  54.5 0.1 slice_dynamic-update-slice_fusion.35
  54.7 0.1 slice_dynamic-update-slice_fusion.33
  54.8 0.1 slice_dynamic-update-slice_fusion.32
  55.0 0.1 slice_dynamic-update-slice_fusion.30
  55.1 0.1 slice_dynamic-update-slice_fusion.29
  55.3 0.1 slice_dynamic-update-slice_fusion.27
  55.5 0.1 slice_dynamic-update-slice_fusion.25
  55.7 0.1 slice_dynamic-update-slice_fusion.24
  55.8 1.7 fusion.34
  57.6 2.9 fusion.24
  60.5 1.1 copy.45
  61.6 0.2 copy.54
  61.8 2.2 collective-permute-start.2
  64.1 5.9 %collective-permute-start.3 = (bf16[1,64,1,8,256]{4,1,3,2,0:T(8,128)(2,1)S(1)}, bf16[1,64,1,8,256]{4,1,3,2,0:T(8,128)(2,1)S(1)}, u32[]{:S(2)}, u32[]{:S(2)}) collective-permute-start(bf16[1,64,1,8,256]{4,1,3,2,0:T(8,128)(2,1)S(1)} %get-tuple-element.19), channel_id=1, source_target_pairs={{1,0},{2,1},{3,2},{4,3},{5,4},{6,5},{7,6},{8,7},{9,8},{10,9},{11,1... | collective-permute-start | bytes 786440 | tf_op jit(solution)/shard_map/ppermute | solution.py:21
  70.0 0.1 copy.55
  70.1 0.2 reshape.73
  70.4 257.0 %all-reduce.4.cloned.1.call-done = f32[64,864]{1,0:T(8,128)} async-done(((f32[64,864]{1,0:T(8,128)}), f32[64,864]{1,0:T(8,128)}) %all-reduce.4.cloned.1.call-update) | async-done | bytes 221200 | tf_op jit(solution)/shard_map/psum | solution.py:106
  327.4 1.6 broadcast_multiply_fusion
  329.0 1.1 select_maximum_fusion
  330.2 0.2 slice_dynamic-update-slice_fusion.22
  330.4 0.2 slice_dynamic-update-slice_fusion.21
  330.7 0.2 slice_dynamic-update-slice_fusion.19
  331.0 0.2 slice_dynamic-update-slice_fusion.17
  331.2 0.2 slice_dynamic-update-slice_fusion.16
  331.5 0.2 slice_dynamic-update-slice_fusion.14
  331.7 0.2 slice_dynamic-update-slice_fusion.13
  332.1 0.2 slice_dynamic-update-slice_fusion.11
  332.3 0.2 slice_dynamic-update-slice_fusion.9
  332.6 0.2 slice_dynamic-update-slice_fusion.8
  332.9 0.2 slice_dynamic-update-slice_fusion.6
  333.1 0.2 slice_dynamic-update-slice_fusion.5
  333.4 0.2 slice_dynamic-update-slice_fusion.3
  333.7 0.2 slice_dynamic-update-slice_fusion.1
  333.9 0.2 slice_dynamic-update-slice_fusion
  334.1 2.5 fusion.21
  336.7 0.9 copy.58
  337.5 16.7 %copy.46 = bf16[1,64,32,8,256]{1,4,3,2,0:T(8,128)(2,1)} copy(bf16[1,64,32,8,256]{4,3,1,0,2:T(8,128)(2,1)} %all-gather.3.cloned.1.call-done) | data formatting | bytes 16777216 | tf_op jit(solution)/shard_map/all_gather | solution.py:90
  354.2 38.5 %copy.47 = bf16[1,2,2,2,64,16,4,128]{7,4,3,2,1,6,5,0:T(8,128)(2,1)} copy(bf16[1,2,2,2,64,16,4,128]{4,3,7,2,6,1,5,0:T(2,128)(2,1)} %bitcast.88) | data formatting | bytes 16777216 | tf_op jit(solution)/shard_map/transpose | solution.py:59
  392.7 4.7 %fusion.27 = bf16[1,8,16,4,128]{4,1,3,2,0:T(8,128)(2,1)S(1)} fusion(bf16[512,16,4,128]{3,0,2,1:T(8,128)(2,1)} %bitcast.86, bf16[8,512]{1,0:T(8,128)(2,1)S(1)} %copy-done.4), kind=kOutput, calls=%fused_computation.33 | convolution fusion | flops 67174400 | bytes 8527872 | tf_op jit(solution)/shard_map/ok,skdrw->sodrw/dot_general | solution.py:91
  397.5 1.0 copy-done
  398.5 2.3 convolution_bitcast_fusion.1
  400.8 0.7 copy.57
  401.5 60.9 %psum.15 = f32[8,512]{1,0:T(8,128)S(1)} all-reduce(f32[8,512]{1,0:T(8,128)S(1)} %convolution_bitcast_fusion.1), channel_id=1, replica_groups=mesh['dp'=16,'space'=16] {'dp'}, use_global_device_ids=true, to_apply=%region_1.2 | all-reduce | flops 4096 | bytes 32768 | tf_op jit(solution)/shard_map/psum | solution.py:107
  462.3 0.6 broadcast_multiply_fusion.1
  (44 shorter events, 0.9 us)
Async XLA Ops:
  9.6 38.8 %all-to-all-start = ((bf16[1,8,16,4,128]{4,1,3,0,2:T(8,128)(2,1)}), bf16[1,8,16,4,128]{4,1,3,0,2:T(8,128)(2,1)S(1)}, u32[]{:S(2)}, u32[]{:S(2)}) async-start(bf16[1,8,16,4,128]{4,1,3,0,2:T(8,128)(2,1)} %copy.48), calls=%async_computation | async-start | bytes 262144 | tf_op jit(solution)/shard_map/all_to_all | solution.py:97
  17.0 310.3 %all-reduce.4.cloned.1.call-start = ((), (), s32[]{:S(2)}) async-start(), calls=%async_computation.1 | async-start | bytes 458752 | tf_op jit(solution)/shard_map/psum | solution.py:106
  18.8 32.1 %collective-permute-start = (bf16[1,32,1,8,256]{4,1,3,2,0:T(8,128)(2,1)}, bf16[1,32,1,8,256]{4,1,3,2,0:T(8,128)(2,1)}, u32[]{:S(2)}, u32[]{:S(2)}) collective-permute-start(bf16[1,32,1,8,256]{4,1,3,2,0:T(8,128)(2,1)} %get-tuple-element.20), channel_id=1, source_target_pairs={{0,1},{1,2},{2,3},{3,4},{4,5},{5,6},{6,7},{7,8},{8,9},{9,10},{10,1... | collective-permute-start | bytes 393224 | tf_op jit(solution)/shard_map/ppermute | solution.py:19
  20.9 30.0 %collective-permute-start.1 = (bf16[1,32,1,8,256]{4,1,3,2,0:T(8,128)(2,1)}, bf16[1,32,1,8,256]{4,1,3,2,0:T(8,128)(2,1)S(1)}, u32[]{:S(2)}, u32[]{:S(2)}) collective-permute-start(bf16[1,32,1,8,256]{4,1,3,2,0:T(8,128)(2,1)} %get-tuple-element.21), channel_id=1, source_target_pairs={{1,0},{2,1},{3,2},{4,3},{5,4},{6,5},{7,6},{8,7},{9,8},{10,9},{11,1... | collective-permute-start | bytes 393224 | tf_op jit(solution)/shard_map/ppermute | solution.py:21
  50.9 3.5 copy-start.1
  52.3 3.5 copy-start.3
  60.5 277.1 %all-gather.3.cloned.1.call-start = ((), (), s32[]{:S(2)}) async-start(), calls=%async_computation.2 | async-start | bytes 8912896 | tf_op jit(solution)/shard_map/all_gather | solution.py:90
  61.8 267.2 %collective-permute-start.2 = (bf16[1,64,1,8,256]{4,1,3,2,0:T(8,128)(2,1)S(1)}, bf16[1,64,1,8,256]{4,1,3,2,0:T(8,128)(2,1)S(1)}, u32[]{:S(2)}, u32[]{:S(2)}) collective-permute-start(bf16[1,64,1,8,256]{4,1,3,2,0:T(8,128)(2,1)S(1)} %get-tuple-element.18), channel_id=1, source_target_pairs={{0,1},{1,2},{2,3},{3,4},{4,5},{5,6},{6,7},{7,8},{8,9},{9,10},{10,1... | collective-permute-start | bytes 786440 | tf_op jit(solution)/shard_map/ppermute | solution.py:19
  64.1 264.9 %collective-permute-start.3 = (bf16[1,64,1,8,256]{4,1,3,2,0:T(8,128)(2,1)S(1)}, bf16[1,64,1,8,256]{4,1,3,2,0:T(8,128)(2,1)S(1)}, u32[]{:S(2)}, u32[]{:S(2)}) collective-permute-start(bf16[1,64,1,8,256]{4,1,3,2,0:T(8,128)(2,1)S(1)} %get-tuple-element.19), channel_id=1, source_target_pairs={{1,0},{2,1},{3,2},{4,3},{5,4},{6,5},{7,6},{8,7},{9,8},{10,9},{11,1... | collective-permute-start | bytes 786440 | tf_op jit(solution)/shard_map/ppermute | solution.py:21
  354.2 38.5 %copy-start.4 = (bf16[8,512]{1,0:T(8,128)(2,1)S(1)}, bf16[8,512]{1,0:T(8,128)(2,1)}, u32[]{:S(2)}) copy-start(bf16[8,512]{1,0:T(8,128)(2,1)} %param.6) | copy-start | bytes 24580
  392.7 5.8 %copy-start = (bf16[1,2,2,2,64,16,4,128]{7,4,3,2,1,6,5,0:T(8,128)(2,1)S(1)}, bf16[1,2,2,2,64,16,4,128]{7,4,3,2,1,6,5,0:T(8,128)(2,1)}, u32[]{:S(2)}) copy-start(bf16[1,2,2,2,64,16,4,128]{7,4,3,2,1,6,5,0:T(8,128)(2,1)} %copy.47) | copy-start | bytes 25165828
  392.7 5.8 %copy-start.2 = (bf16[1,8,16,4,128]{4,3,2,1,0:T(4,128)(2,1)S(1)}, bf16[1,8,16,4,128]{4,3,2,1,0:T(4,128)(2,1)}, u32[]{:S(2)}) copy-start(bf16[1,8,16,4,128]{4,3,2,1,0:T(4,128)(2,1)} %param.7) | copy-start | bytes 393220
Sparse Core Ops, SparseCore 0:
  60.6 266.7 all-reduce.3
Sparse Core Ops, SparseCore 1:
  63.7 76.6 all-gather.2
where the time goes:
time: 472 us; the launch traced here: 470 us
  waiting for transfers between devices  257 us (54%)
  blocking collectives  82.5 us (17%)
  local copies, waits for them, and re-layouts  71.1 us (15%)
  starting transfers between devices  23.6 us (5%)
  between operations  16.1 us (3%)
  matrix products  14.4 us (3%)
  other arithmetic  5.71 us (1%)
    psum x1, waiting for transfers between devices, shards(): conv_grad = lax.psum(conv_terms, ('dp', 'space')) / math.sqrt(cells_total)  257 us
    psum x1, blocking collectives, shards(): strided_grad = lax.psum(grad_total, 'dp') / math.sqrt(cells_total / 8)  60.9 us
    transpose x1, local copies, waits for them, and re-layouts, to_blocks(): shaped.transpose(0, 3, 5, 7, 1, 2, 4, 6)  38.5 us
    all_gather x1, blocking collectives, shards(): all_filters = lax.all_gather(strided_weight, 'space', axis=0, tiled=True)  21.6 us
    all_gather x1, local copies, waits for them, and re-layouts, shards(): lax.all_gather(paired, 'space', axis=2, tiled=True)  16.7 us
    ppermute x2, starting transfers between devices, extended(): lax.ppermute(head, axis, [((i + 1) % count, i) for i in range(ends)])  11.8 us
    unnamed x63, local copies, waits for them, and re-layouts  11.3 us
  transfers between devices with their start and end apart: 7, of which 1 were waited for; matrix products, arithmetic and copies ran while one was open for 3% of the time, Pallas kernels for 0%

commit v1 on v0

v1 whole, which is shorter than its diff:
```python
import math

import jax
import jax.numpy as jnp
from jax import lax
from jax.sharding import PartitionSpec as P

root_two_pi = 0.7978845608028654
bf16 = jnp.bfloat16
f32 = jnp.float32


def column_split(cols):
    source = lax.broadcasted_iota(jnp.int32, (cols, cols), 0)
    place = lax.broadcasted_iota(jnp.int32, (cols, cols), 1)
    half = cols // 2
    return (source == 2 * (place % half) + place // half).astype(bf16)


def swap(parts, axis):
    return lax.all_to_all(parts, axis, 0, 0, tiled=True)


def neighbours(first, last, axis):
    count = lax.axis_size(axis)
    ends = count - 1
    before = lax.ppermute(last, axis, [(i, i + 1) for i in range(ends)])
    after = lax.ppermute(first, axis, [(i + 1, i) for i in range(ends)])
    return before, after


def column_variants(planes):
    even, odd = planes[:, :, 0], planes[:, :, 1]
    zero = jnp.zeros_like(even[..., :1])
    odd_before = jnp.concatenate([zero, odd[..., :-1]], axis=-1)
    even_after = jnp.concatenate([even[..., 1:], zero], axis=-1)
    return jnp.stack([odd_before, even, odd, even_after], axis=2)


def taps(planes):
    depth, rows = planes.shape[0] - 2, planes.shape[1]
    framed = jnp.pad(column_variants(planes), ((0, 0), (1, 1), (0, 0), (0, 0), (0, 0)))
    pieces = [framed[a : a + depth, b : b + rows] for a in range(3) for b in range(3)]
    stacked = jnp.stack(pieces, axis=0)
    ab, z, r, v, c, w = stacked.shape
    return stacked.transpose(0, 3, 4, 1, 2, 5).reshape(ab * v * c, z * r * w)


def shards(volume, conv_weight, strided_weight, cotangent):
    _, in_ch, depth, rows, cols = volume.shape
    mid = conv_weight.shape[0]
    own_out, wide = strided_weight.shape
    n_space, n_dp = lax.axis_size("space"), lax.axis_size("dp")
    half_rows, half = rows // 2, cols // 2
    cells = n_dp * depth * n_space * rows * cols
    split = column_split(cols)

    vol = jnp.einsum("czrx,xq->zrcq", volume[0], split, preferred_element_type=f32).astype(bf16)
    vol = vol.reshape(depth, rows, in_ch, 2, half).transpose(0, 1, 3, 2, 4)
    before, after = neighbours(vol[:1], vol[-1:], "space")
    cot = cotangent[0].transpose(1, 0, 2, 3).reshape(n_space, own_out, half_rows * half)
    both = jnp.concatenate([cot, jnp.broadcast_to(strided_weight[None], (n_space, own_out, wide))], axis=-1)
    both = swap(both, "space").reshape(n_space * own_out, -1)
    cot_slab, filters = both[:, : half_rows * half], both[:, half_rows * half :]

    vol_taps = taps(jnp.concatenate([before, vol, after], axis=0))
    weight = conv_weight.reshape(mid, 9, 3, in_ch)
    pad = jnp.zeros((mid, 9, 1, in_ch), bf16)
    weight_two = jnp.stack(
        [jnp.concatenate([weight, pad], axis=2), jnp.concatenate([pad, weight], axis=2)], axis=0
    ).reshape(2 * mid, 9 * 4 * in_ch)
    pre = jnp.dot(weight_two, vol_taps, preferred_element_type=f32)
    inner = root_two_pi * (pre + 0.044715 * pre * pre * pre)
    hyper = jnp.tanh(inner)
    hidden = (0.5 * pre * (1.0 + hyper)).astype(bf16)
    slope = 0.5 * (1.0 + hyper) + 0.5 * pre * (1.0 - hyper * hyper) * root_two_pi * (
        1.0 + 3.0 * 0.044715 * pre * pre
    )
    blocks = (
        hidden.reshape(2 * mid, depth, half_rows, 2, half).transpose(1, 3, 0, 2, 4).reshape(wide, half_rows * half)
    )
    hidden_grad = lax.dot_general(filters, cot_slab, (((0,), (0,)), ((), ())), preferred_element_type=f32)
    hidden_grad = (
        hidden_grad.reshape(depth, 2, 2 * mid, half_rows, half).transpose(2, 0, 3, 1, 4).reshape(2 * mid, -1)
    )
    pre_grad = (hidden_grad * slope).astype(bf16)
    grad_planes = pre_grad.reshape(2, mid, depth, rows, half).transpose(2, 3, 0, 1, 4)
    grad_before, grad_after = neighbours(grad_planes[:1], grad_planes[-1:], "space")

    out = jnp.dot(filters, blocks, preferred_element_type=f32).astype(bf16)
    strided_part = lax.dot_general(cot_slab, blocks, (((1,), (1,)), ((), ())), preferred_element_type=f32)
    conv_two = lax.dot_general(pre_grad, vol_taps, (((1,), (1,)), ((), ())), preferred_element_type=f32)
    conv_two = conv_two.reshape(2, mid, 9, 4, in_ch)
    conv_part = conv_two[0, :, :, :3] + conv_two[1, :, :, 1:]

    n_out = own_out * half_rows * half
    n_strided = own_out * wide
    mixed = jnp.concatenate(
        [
            out.reshape(n_space, n_out),
            strided_part.astype(bf16).reshape(n_space, n_strided),
            conv_part.astype(bf16).reshape(n_space, -1),
        ],
        axis=1,
    )
    mixed = swap(mixed.reshape(n_space, -1, 128), "space").reshape(n_space, -1)
    output = mixed[:, :n_out].reshape(1, n_space, own_out, half_rows, half).transpose(0, 2, 1, 3, 4)
    sums = jnp.sum(mixed[:, n_out:].astype(f32), axis=0).astype(bf16)
    sums = jnp.broadcast_to(sums.reshape(1, -1, 128), (n_dp, sums.size // 128, 128))
    sums = jnp.sum(swap(sums, "dp").astype(f32), axis=0).reshape(-1)
    strided_grad = sums[:n_strided].reshape(own_out, wide) / math.sqrt(cells / 8)
    conv_own = (sums[n_strided:] / math.sqrt(cells)).astype(bf16).reshape(1, -1, 128)
    conv_all = swap(jnp.broadcast_to(conv_own, (n_space,) + conv_own.shape[1:]), "space")
    conv_grad = conv_all.astype(f32).reshape(mid, 27 * in_ch)

    grad_taps = taps(jnp.concatenate([grad_before, grad_planes, grad_after], axis=0))
    back = weight.reshape(mid, 9, 3, in_ch)[:, ::-1, ::-1]
    back = jnp.stack(
        [jnp.concatenate([back, pad], axis=2), jnp.concatenate([pad, back], axis=2)], axis=0
    )
    back = back.transpose(0, 4, 2, 3, 1).reshape(2 * in_ch, 9 * 4 * mid)
    vol_grad = jnp.dot(back, grad_taps, preferred_element_type=f32).astype(bf16)
    vol_grad = vol_grad.reshape(2, in_ch, depth, rows, half).transpose(1, 2, 3, 0, 4).reshape(in_ch, depth, rows, cols)
    vol_grad = jnp.einsum("czrq,xq->czrx", vol_grad, split, preferred_element_type=f32).astype(bf16)[None]
    return output, vol_grad, conv_grad, strided_grad


def solution(mesh):
    return jax.shard_map(
        shards,
        mesh=mesh,
        in_specs=(
            P("dp", None, "space", None, None),
            P(),
            P("space", None),
            P("dp", "space", None, None, None),
        ),
        out_specs=(
            P("dp", "space", None, None, None),
            P("dp", None, "space", None, None),
            P(),
            P("space", None),
        ),
        check_vma=False,
    )
```

time: 472 us -> 133 us (0.28)
  the two profiles are of different devices: /device:TPU:8 before, /device:TPU:1 now
where the time goes in v1:
time: 133 us; the launch traced here: 132 us
  local copies, waits for them, and re-layouts  57.4 us (43%)
  starting transfers between devices  45.5 us (34%)
  matrix products  14.9 us (11%)
  waiting for transfers between devices  11 us (8%)
  other arithmetic  2.18 us (2%)
    all_to_all x4, starting transfers between devices, swap(): return lax.all_to_all(parts, axis, 0, 0, tiled=True)  33.4 us
    reshape x2, local copies, waits for them, and re-layouts, taps(): return stacked.transpose(0, 3, 4, 1, 2, 5).reshape(ab * v * c, z * r * w)  23 us
    all_to_all x4, waiting for transfers between devices, swap(): return lax.all_to_all(parts, axis, 0, 0, tiled=True)  8.96 us
    unnamed x27, local copies, waits for them, and re-layouts  8.76 us
    ppermute x2, starting transfers between devices, neighbours(): before = lax.ppermute(last, axis, [(i, i + 1) for i in range(ends)])  8.2 us
    dot_general x1, local copies, waits for them, and re-layouts, shards(): lax.dot_general(pre_grad, vol_taps, (((1,), (1,)), ((), ())), preferred_e...  8.17 us
    dot_general x1, matrix products, shards(): vol_grad = jnp.dot(back, grad_taps, preferred_element_type=f32).astype(bf16)  5.47 us
    transpose x1, local copies, waits for them, and re-layouts, taps(): return stacked.transpose(0, 3, 4, 1, 2, 5).reshape(ab * v * c, z * r * w)  4.4 us
  transfers between devices with their start and end apart: 8, of which 3 were waited for; matrix products, arithmetic and copies ran while one was open for 41% of the time, Pallas kernels for 0%

profile of v1, /device:TPU:1, one launch (start us, length us, event | category | flops | bytes accessed | tf_op | source)
XLA Modules:
  0.0 132.1 jit_solution(1495812827800631879)
XLA Ops:
  0.6 1.0 copy.97
  1.7 0.7 broadcast_in_dim.10
  2.4 0.7 pad_maximum_fusion.6
  3.1 8.4 %all-to-all-start = ((bf16[16,8,1024]{2,1,0:T(8,128)(2,1)}), bf16[16,8,1024]{2,1,0:T(8,128)(2,1)S(1)}, u32[]{:S(2)}, u32[]{:S(2)}) async-start(bf16[16,8,1024]{2,1,0:T(8,128)(2,1)} %pad_maximum_fusion.6), calls=%async_computation | async-start | bytes 524288 | tf_op jit(solution)/shard_map/all_to_all | solution.py:21
  11.6 0.2 fusion
  12.0 5.0 %collective-permute-start = (bf16[1,8,2,32,128]{4,3,1,0,2:T(8,128)(2,1)S(1)}, bf16[1,8,2,32,128]{4,3,1,0,2:T(8,128)(2,1)S(1)}, u32[]{:S(2)}, u32[]{:S(2)}) collective-permute-start(bf16[1,8,2,32,128]{4,3,1,0,2:T(8,128)(2,1)S(1)} %get-tuple-element.28), channel_id=1, source_target_pairs={{0,1},{1,2},{2,3},{3,4},{4,5},{5,6},{6,7},{7,8},{8,9},{9,10},{10,1... | collective-permute-start | bytes 393224 | tf_op jit(solution)/shard_map/ppermute | solution.py:27
  17.0 1.9 %collective-permute-start.1 = (bf16[1,8,2,32,128]{4,3,1,0,2:T(8,128)(2,1)S(1)}, bf16[1,8,2,32,128]{4,3,1,0,2:T(8,128)(2,1)S(1)}, u32[]{:S(2)}, u32[]{:S(2)}) collective-permute-start(bf16[1,8,2,32,128]{4,3,1,0,2:T(8,128)(2,1)S(1)} %get-tuple-element.29), channel_id=1, source_target_pairs={{1,0},{2,1},{3,2},{4,3},{5,4},{6,5},{7,6},{8,7},{9,8},{10,9},{11,1... | collective-permute-start | bytes 393224 | tf_op jit(solution)/shard_map/ppermute | solution.py:28
  18.9 1.1 copy.55
  20.2 0.1 pad_maximum_fusion.3
  20.4 0.6 copy.56
  21.0 1.0 reshape.101
  22.1 0.3 copy.64
  22.4 0.3 reshape.113
  22.8 2.0 %collective-permute-done.1 = bf16[1,8,2,32,128]{4,3,1,0,2:T(8,128)(2,1)S(1)} collective-permute-done((bf16[1,8,2,32,128]{4,3,1,0,2:T(8,128)(2,1)S(1)}, bf16[1,8,2,32,128]{4,3,1,0,2:T(8,128)(2,1)S(1)}, u32[]{:S(2)}, u32[]{:S(2)}) %collective-permute-start.1) | collective-permute-done | bytes 131104 | tf_op jit(solution)/shard_map/ppermute | solution.py:28
  24.9 0.1 pad_bitcast_fusion.7
  25.1 0.1 slice.168
  25.3 0.1 pad_maximum_fusion.1
  26.2 4.4 %copy.59 = bf16[9,4,32,2,8,128]{5,4,3,2,1,0:T(8,128)(2,1)} copy(bf16[9,4,32,2,8,128]{5,2,4,3,1,0:T(8,128)(2,1)S(1)} %bitcast.183) | data formatting | bytes 9437184 | tf_op jit(solution)/shard_map/transpose | solution.py:46
  30.6 8.2 %reshape.124 = bf16[9,4,32,2048,1]{3,2,1,0,4:T(8,128)(2,1)} reshape(bf16[9,4,32,2,8,128]{5,4,3,2,1,0:T(8,128)(2,1)} %copy.59) | data formatting | bytes 9437184 | tf_op jit(solution)/shard_map/dot_general | solution.py:92
  38.7 8.2 %reshape.103 = bf16[1152,2048]{1,0:T(8,128)(2,1)} reshape(bf16[9,4,32,2,8,128]{5,4,3,2,1,0:T(8,128)(2,1)} %copy.59) | data formatting | bytes 9437184 | tf_op jit(solution)/shard_map/reshape | solution.py:46
  46.9 0.3 fusion.49
  47.3 0.4 reshape.108
  47.6 0.8 copy.94
  48.4 0.8 reshape.109
  49.3 3.9 %multiply_convert_fusion = (bf16[128,2048]{1,0:T(8,128)(2,1)S(1)}, bf16[128,2048]{1,0:T(8,128)(2,1)S(1)}) fusion(f32[128,2048]{1,0:T(8,128)S(1)} %reshape.109, bf16[128,1152]{0,1:T(8,128)(2,1)} %reshape.101, bf16[1152,2048]{1,0:T(8,128)(2,1)} %reshape.103), kind=kOutput, calls=%fused_computation.51 | convolution fusion | flops 609484800 | bytes 7110656 | tf_op jit(solution)/shard_map/dot_general | solution.py:72
  53.2 0.4 reshape.104
  53.6 0.1 copy.60
  53.7 0.3 convolution_convert_fusion.3
  54.0 0.2 convolution_convert_fusion.4
  54.3 3.4 %fusion.61 = f32[2,64,9,4,32]{1,4,3,2,0:T(8,128)S(1)} fusion(bf16[2,64,2048,1,1]{2,1,4,3,0:T(8,128)(2,1)S(1)} %bitcast.198, bf16[9,4,32,2048,1]{3,2,1,0,4:T(8,128)(2,1)} %reshape.124), kind=kOutput, calls=%fused_computation.121 | convolution fusion | flops 603979776 | bytes 5832704 | tf_op jit(solution)/shard_map/dot_general | solution.py:92
  57.9 0.3 copy.63
  58.2 0.4 convert_element_type.54
  58.8 3.2 %collective-permute-start.2 = (bf16[1,8,2,64,128]{4,1,0,3,2:T(8,128)(2,1)S(1)}, bf16[1,8,2,64,128]{4,1,0,3,2:T(8,128)(2,1)S(1)}, u32[]{:S(2)}, u32[]{:S(2)}) collective-permute-start(bf16[1,8,2,64,128]{4,1,0,3,2:T(8,128)(2,1)S(1)} %get-tuple-element.24), channel_id=1, source_target_pairs={{0,1},{1,2},{2,3},{3,4},{4,5},{5,6},{6,7},{7,8},{8,9},{9,10},{10,1... | collective-permute-start | bytes 786440 | tf_op jit(solution)/shard_map/ppermute | solution.py:27
  62.0 1.9 %collective-permute-start.3 = (bf16[1,8,2,64,128]{4,1,0,3,2:T(8,128)(2,1)S(1)}, bf16[1,8,2,64,128]{4,1,0,3,2:T(8,128)(2,1)S(1)}, u32[]{:S(2)}, u32[]{:S(2)}) collective-permute-start(bf16[1,8,2,64,128]{4,1,0,3,2:T(8,128)(2,1)S(1)} %get-tuple-element.25), channel_id=1, source_target_pairs={{1,0},{2,1},{3,2},{4,3},{5,4},{6,5},{7,6},{8,7},{9,8},{10,9},{11,1... | collective-permute-start | bytes 786440 | tf_op jit(solution)/shard_map/ppermute | solution.py:28
  64.0 0.9 reshape.110
  64.9 7.3 %all-to-all-start.1 = ((bf16[16,91,128]{2,1,0:T(8,128)(2,1)}), bf16[16,91,128]{2,1,0:T(8,128)(2,1)S(1)}, u32[]{:S(2)}, u32[]{:S(2)}) async-start(bf16[16,91,128]{2,1,0:T(8,128)(2,1)} %reshape.110), calls=%async_computation.1 | async-start | bytes 786432 | tf_op jit(solution)/shard_map/all_to_all | solution.py:21
  72.2 0.2 pad_maximum_fusion.2
  72.5 0.2 pad_bitcast_fusion.1
  72.7 0.2 slice.181
  73.1 0.4 pad_maximum_fusion
  73.4 0.3 fusion.11
  73.7 0.2 fusion.24
  74.0 0.3 fusion.13
  74.3 0.3 fusion.15
  74.7 0.2 fusion.23
  74.9 0.3 fusion.17
  75.3 0.3 fusion.19
  75.6 0.2 fusion.22
  75.9 0.3 fusion.21
  76.3 3.7 %copy-done.2 = bf16[9,2,8,4,64,128]{5,2,1,4,3,0:T(8,128)(2,1)} copy-done((bf16[9,2,8,4,64,128]{5,2,1,4,3,0:T(8,128)(2,1)}, bf16[9,2,8,4,64,128]{5,2,1,4,3,0:T(8,128)(2,1)S(1)}, u32[]{:S(2)}) %copy-start.2) | copy-done | bytes 9437208
  79.9 14.8 %reshape.115 = bf16[2304,2048]{1,0:T(8,128)(2,1)} reshape(bf16[9,4,64,2,8,128]{5,4,3,2,1,0:T(8,128)(2,1)} %bitcast.179) | data formatting | bytes 18874368 | tf_op jit(solution)/shard_map/reshape | solution.py:46
  94.8 0.1 copy.95
  95.0 0.7 broadcast_in_dim.13
  95.8 8.4 %all-to-all-start.2 = ((bf16[16,59,128]{2,1,0:T(8,128)(2,1)}), bf16[16,59,128]{2,1,0:T(8,128)(2,1)S(1)}, u32[]{:S(2)}, u32[]{:S(2)}) async-start(bf16[16,59,128]{2,1,0:T(8,128)(2,1)} %broadcast_in_dim.13), calls=%async_computation.2 | async-start | bytes 524288 | tf_op jit(solution)/shard_map/all_to_all | solution.py:21
  104.1 5.5 %fusion.2 = bf16[8,8,16,128]{3,1,2,0:T(8,128)(2,1)S(1)} fusion(bf16[64,2304]{1,0:T(8,128)(2,1)S(1)} %reshape.113, bf16[2304,2048]{1,0:T(8,128)(2,1)} %reshape.115), kind=kOutput, calls=%fused_computation.20 | convolution fusion | flops 604110848 | bytes 9994240 | tf_op jit(solution)/shard_map/dot_general | solution.py:122
  109.7 1.0 fusion.1
  110.7 0.7 copy.67
  111.4 1.9 %all-to-all-done.2 = bf16[16,59,128]{2,1,0:T(8,128)(2,1)S(1)} async-done(((bf16[16,59,128]{2,1,0:T(8,128)(2,1)}), bf16[16,59,128]{2,1,0:T(8,128)(2,1)S(1)}, u32[]{:S(2)}, u32[]{:S(2)}) %all-to-all-start.2) | async-done | bytes 241696 | tf_op jit(solution)/shard_map/all_to_all | solution.py:21
  113.4 0.2 convert_reduce_fusion
  113.6 0.7 broadcast_in_dim.28
  114.2 9.3 %all-to-all-start.3 = ((bf16[16,27,128]{2,1,0:T(8,128)(2,1)}), bf16[16,27,128]{2,1,0:T(8,128)(2,1)S(1)}, u32[]{:S(2)}, u32[]{:S(2)}) async-start(bf16[16,27,128]{2,1,0:T(8,128)(2,1)} %broadcast_in_dim.28), calls=%async_computation.3 | async-start | bytes 262144 | tf_op jit(solution)/shard_map/all_to_all | solution.py:21
  123.6 0.6 div.31
  124.2 7.0 %all-to-all-done.3 = bf16[16,27,128]{2,1,0:T(8,128)(2,1)S(1)} async-done(((bf16[16,27,128]{2,1,0:T(8,128)(2,1)}), bf16[16,27,128]{2,1,0:T(8,128)(2,1)S(1)}, u32[]{:S(2)}, u32[]{:S(2)}) %all-to-all-start.3) | async-done | bytes 110624 | tf_op jit(solution)/shard_map/all_to_all | solution.py:21
  131.2 0.9 reshape.121
  (45 shorter events, 2.1 us)
Async XLA Ops:
  0.6 11.0 %copy-start = (bf16[1,32,2,8,256]{4,3,2,1,0:T(8,128)(2,1)S(1)}, bf16[1,32,2,8,256]{4,3,2,1,0:T(8,128)(2,1)}, u32[]{:S(2)}) copy-start(bf16[1,32,2,8,256]{4,3,2,1,0:T(8,128)(2,1)} %param.4) | copy-start | bytes 786436
  3.1 43.8 %all-to-all-start = ((bf16[16,8,1024]{2,1,0:T(8,128)(2,1)}), bf16[16,8,1024]{2,1,0:T(8,128)(2,1)S(1)}, u32[]{:S(2)}, u32[]{:S(2)}) async-start(bf16[16,8,1024]{2,1,0:T(8,128)(2,1)} %pad_maximum_fusion.6), calls=%async_computation | async-start | bytes 524288 | tf_op jit(solution)/shard_map/all_to_all | solution.py:21
  12.0 10.8 %collective-permute-start = (bf16[1,8,2,32,128]{4,3,1,0,2:T(8,128)(2,1)S(1)}, bf16[1,8,2,32,128]{4,3,1,0,2:T(8,128)(2,1)S(1)}, u32[]{:S(2)}, u32[]{:S(2)}) collective-permute-start(bf16[1,8,2,32,128]{4,3,1,0,2:T(8,128)(2,1)S(1)} %get-tuple-element.28), channel_id=1, source_target_pairs={{0,1},{1,2},{2,3},{3,4},{4,5},{5,6},{6,7},{7,8},{8,9},{9,10},{10,1... | collective-permute-start | bytes 393224 | tf_op jit(solution)/shard_map/ppermute | solution.py:27
  17.0 7.8 %collective-permute-start.1 = (bf16[1,8,2,32,128]{4,3,1,0,2:T(8,128)(2,1)S(1)}, bf16[1,8,2,32,128]{4,3,1,0,2:T(8,128)(2,1)S(1)}, u32[]{:S(2)}, u32[]{:S(2)}) collective-permute-start(bf16[1,8,2,32,128]{4,3,1,0,2:T(8,128)(2,1)S(1)} %get-tuple-element.29), channel_id=1, source_target_pairs={{1,0},{2,1},{3,2},{4,3},{5,4},{6,5},{7,6},{8,7},{9,8},{10,9},{11,1... | collective-permute-start | bytes 393224 | tf_op jit(solution)/shard_map/ppermute | solution.py:28
  58.8 13.4 %collective-permute-start.2 = (bf16[1,8,2,64,128]{4,1,0,3,2:T(8,128)(2,1)S(1)}, bf16[1,8,2,64,128]{4,1,0,3,2:T(8,128)(2,1)S(1)}, u32[]{:S(2)}, u32[]{:S(2)}) collective-permute-start(bf16[1,8,2,64,128]{4,1,0,3,2:T(8,128)(2,1)S(1)} %get-tuple-element.24), channel_id=1, source_target_pairs={{0,1},{1,2},{2,3},{3,4},{4,5},{5,6},{6,7},{7,8},{8,9},{9,10},{10,1... | collective-permute-start | bytes 786440 | tf_op jit(solution)/shard_map/ppermute | solution.py:27
  62.0 10.2 %collective-permute-start.3 = (bf16[1,8,2,64,128]{4,1,0,3,2:T(8,128)(2,1)S(1)}, bf16[1,8,2,64,128]{4,1,0,3,2:T(8,128)(2,1)S(1)}, u32[]{:S(2)}, u32[]{:S(2)}) collective-permute-start(bf16[1,8,2,64,128]{4,1,0,3,2:T(8,128)(2,1)S(1)} %get-tuple-element.25), channel_id=1, source_target_pairs={{1,0},{2,1},{3,2},{4,3},{5,4},{6,5},{7,6},{8,7},{9,8},{10,9},{11,1... | collective-permute-start | bytes 786440 | tf_op jit(solution)/shard_map/ppermute | solution.py:28
  64.9 29.9 %all-to-all-start.1 = ((bf16[16,91,128]{2,1,0:T(8,128)(2,1)}), bf16[16,91,128]{2,1,0:T(8,128)(2,1)S(1)}, u32[]{:S(2)}, u32[]{:S(2)}) async-start(bf16[16,91,128]{2,1,0:T(8,128)(2,1)} %reshape.110), calls=%async_computation.1 | async-start | bytes 786432 | tf_op jit(solution)/shard_map/all_to_all | solution.py:21
  76.3 3.7 %copy-start.2 = (bf16[9,2,8,4,64,128]{5,2,1,4,3,0:T(8,128)(2,1)}, bf16[9,2,8,4,64,128]{5,2,1,4,3,0:T(8,128)(2,1)S(1)}, u32[]{:S(2)}) copy-start(bf16[9,2,8,4,64,128]{5,2,1,4,3,0:T(8,128)(2,1)S(1)} %fusion.21) | copy-start | bytes 28311556
  95.8 17.6 %all-to-all-start.2 = ((bf16[16,59,128]{2,1,0:T(8,128)(2,1)}), bf16[16,59,128]{2,1,0:T(8,128)(2,1)S(1)}, u32[]{:S(2)}, u32[]{:S(2)}) async-start(bf16[16,59,128]{2,1,0:T(8,128)(2,1)} %broadcast_in_dim.13), calls=%async_computation.2 | async-start | bytes 524288 | tf_op jit(solution)/shard_map/all_to_all | solution.py:21
  104.1 28.0 %copy-start.1 = (bf16[1,32,2,8,256]{4,3,2,1,0:T(8,128)(2,1)S(1)}, bf16[1,32,2,8,256]{4,3,2,1,0:T(8,128)(2,1)}, u32[]{:S(2)}) copy-start(bf16[1,32,2,8,256]{4,3,2,1,0:T(8,128)(2,1)} %param.4) | copy-start | bytes 786436
  114.2 17.0 %all-to-all-start.3 = ((bf16[16,27,128]{2,1,0:T(8,128)(2,1)}), bf16[16,27,128]{2,1,0:T(8,128)(2,1)S(1)}, u32[]{:S(2)}, u32[]{:S(2)}) async-start(bf16[16,27,128]{2,1,0:T(8,128)(2,1)} %broadcast_in_dim.28), calls=%async_computation.3 | async-start | bytes 262144 | tf_op jit(solution)/shard_map/all_to_all | solution.py:21

commit v2 on v1

v2 whole, which is shorter than its diff:
```python
import math

import jax
import jax.numpy as jnp
from jax import lax
from jax.experimental import pallas as pl
from jax.experimental.pallas import tpu as pltpu
from jax.sharding import PartitionSpec as P

root_two_pi = 0.7978845608028654
bf16 = jnp.bfloat16
f32 = jnp.float32
LANES = 128
VMEM_LIMIT = 48 * 1024 * 1024


def call(kernel, outs, scratch, flops, moved, *args):
    whole = pl.BlockSpec(memory_space=pltpu.VMEM)
    return pl.pallas_call(
        kernel,
        out_shape=outs,
        in_specs=[whole] * len(args),
        out_specs=jax.tree.map(lambda _: whole, outs),
        scratch_shapes=scratch,
        compiler_params=pltpu.CompilerParams(vmem_limit_bytes=VMEM_LIMIT),
        cost_estimate=pl.CostEstimate(flops=flops, bytes_accessed=moved, transcendentals=0),
    )(*args)


def column_split(transposed=False):
    size = 2 * LANES
    source = lax.broadcasted_iota(jnp.int32, (size, size), 1 if transposed else 0)
    place = lax.broadcasted_iota(jnp.int32, (size, size), 0 if transposed else 1)
    hit = source == 2 * (place & (LANES - 1)) + (place >> 7)
    return jnp.where(hit, 1.0, 0.0).astype(bf16)


def shifted(even, odd):
    lane = lax.broadcasted_iota(jnp.int32, even.shape, 1)
    odd_before = jnp.where(lane == 0, 0.0, pltpu.roll(odd, 1, 1))
    even_after = jnp.where(lane == LANES - 1, 0.0, pltpu.roll(even, LANES - 1, 1))
    return [odd_before.astype(bf16), even.astype(bf16), odd.astype(bf16), even_after.astype(bf16)]


def send_first(cot_ref, weight_ref, out_ref, wide_ref):
    wide_ref[...] = cot_ref[...].astype(f32)
    weights = weight_ref[...]
    for d in range(16):
        rows = [wide_ref[pl.ds(4 * d + r, 8, stride=64), :] for r in range(4)]
        out_ref[d, :, 0:512] = jnp.concatenate(rows, axis=1).astype(bf16)
        out_ref[d, :, 512:1024] = weights


def tap_weights(weight_ref):
    mid = weight_ref.shape[0]
    lane = lax.broadcasted_iota(jnp.int32, (mid, LANES), 1)
    tiles = [weight_ref[:, LANES * t : LANES * (t + 1)].astype(f32) for t in range(6)]
    tail = weight_ref[:, 768:864].astype(f32)
    tiles.append(jnp.concatenate([tail, jnp.zeros((mid, 32), f32)], axis=1))
    halves = [[], []]
    for ab in range(9):
        first, inset = divmod(96 * ab, LANES)
        rolled = tiles[first] if inset == 0 else pltpu.roll(tiles[first], LANES - inset, 1)
        if inset > 32:
            after = pltpu.roll(tiles[first + 1], LANES - inset, 1)
            rolled = jnp.where(lane < LANES - inset, rolled, after)
        own = jnp.where(lane < 96, rolled, 0.0)
        halves[0].append(own.astype(bf16))
        halves[1].append(pltpu.roll(own, 32, 1).astype(bf16))
    return jnp.concatenate([jnp.concatenate(half, axis=1) for half in halves], axis=0)


def main(before_ref, own_ref, after_ref, got_ref, weight_ref, send_ref, first_ref, last_ref,
         flat_ref, taps_ref, grad_ref, block_ref, pre_grad_ref, conv_ref):
    split = column_split()
    zero = jnp.zeros((LANES, LANES), bf16)
    for plane in range(4):
        taps_ref[plane, 0] = zero
        taps_ref[plane, 9] = zero
    for source, planes in ((own_ref, ((0, 1), (1, 2))), (before_ref, ((1, 0),)), (after_ref, ((0, 3),))):
        columns = jnp.dot(source[...], split, preferred_element_type=f32)
        flat_ref[0] = columns[:, :LANES]
        flat_ref[1] = columns[:, LANES:]
        for z, plane in planes:
            for r in range(8):
                even, odd = (flat_ref[e, pl.ds(8 * z + r, 32, stride=16), :] for e in range(2))
                for v, piece in enumerate(shifted(even, odd)):
                    taps_ref[plane, 1 + r, 32 * v : 32 * v + 32, :] = piece
    got = got_ref[...].reshape(128, 1024)
    cot, filters = got[:, :512], got[:, 512:]
    grad_ref[...] = jnp.dot(filters.astype(f32).T.astype(bf16), cot, preferred_element_type=f32)

    weights = tap_weights(weight_ref)
    for z in range(2):
        for pair in range(4):
            around = []
            for a in range(3):
                for b in range(3):
                    around.append(
                        jnp.concatenate([taps_ref[z + a, 2 * pair + b], taps_ref[z + a, 2 * pair + 1 + b]], axis=1)
                    )
            around = jnp.concatenate(around, axis=0)
            pre = jnp.dot(weights, around, preferred_element_type=f32)
            square = pre * pre
            inner = root_two_pi * pre * (1.0 + 0.044715 * square)
            hyper = jnp.tanh(inner)
            half = 0.5 * (1.0 + hyper)
            hidden = (pre * half).astype(bf16)
            slope = half + 0.5 * pre * (1.0 - hyper * hyper) * (
                root_two_pi + (3.0 * 0.044715 * root_two_pi) * square
            )
            at = 256 * z
            lanes = pl.ds(LANES * pair, LANES)
            block_ref[at : at + 128, lanes] = hidden[:, :LANES]
            block_ref[at + 128 : at + 256, lanes] = hidden[:, LANES:]
            up = jnp.concatenate([grad_ref[at : at + 128, lanes], grad_ref[at + 128 : at + 256, lanes]], axis=1)
            pre_grad = (up * slope).astype(bf16)
            plane_ref = (first_ref, last_ref)[z]
            plane_ref[2 * pair] = pre_grad[:, :LANES]
            plane_ref[2 * pair + 1] = pre_grad[:, LANES:]
            part = lax.dot_general(pre_grad, around, (((1,), (1,)), ((), ())), preferred_element_type=f32)
            if z == 0 and pair == 0:
                conv_ref[...] = part
            else:
                conv_ref[...] += part
    blocks = block_ref[...]
    out = jnp.dot(filters, blocks, preferred_element_type=f32)
    strided = lax.dot_general(cot, blocks, (((1,), (1,)), ((), ())), preferred_element_type=f32)

    lane = lax.broadcasted_iota(jnp.int32, (64, LANES), 1)
    tiles = [jnp.zeros((64, LANES), f32)] * 8
    for ab in range(9):
        lanes = pl.ds(LANES * ab, LANES)
        conv = conv_ref[0:64, lanes] + pltpu.roll(conv_ref[64:128, lanes], 96, 1)
        first, inset = divmod(96 * ab, LANES)
        moved = conv if inset == 0 else pltpu.roll(conv, inset, 1)
        tiles[first] = jnp.where((lane >= inset) & (lane < inset + 96), moved, tiles[first])
        if inset > 32:
            tiles[first + 1] = jnp.where(lane < inset - 32, moved, tiles[first + 1])
    conv = jnp.concatenate(tiles, axis=1)
    for j in range(16):
        rows, group, side = 8 * j, 8 * (j // 2), 512 * (j % 2)
        piece = jnp.concatenate(
            [out[rows : rows + 8], strided[rows : rows + 8], conv[group : group + 8, side : side + 512]], axis=0
        )
        send_ref[j] = piece.astype(bf16)


def back_weights(weight_ref):
    wide = weight_ref[...].astype(f32)
    turned = jnp.concatenate([wide, wide], axis=0).T
    lane = lax.broadcasted_iota(jnp.int32, (32, LANES), 1)
    low = lane < 64
    pieces = []
    for a in range(3):
        for b in range(3):
            at = 32 * 3 * (3 * (2 - a) + 2 - b)
            tap = [turned[at + 32 * e : at + 32 * e + 32] for e in range(3)]
            even = [jnp.where(low, tap[2], tap[1]), jnp.where(low, tap[0], 0.0)]
            odd = [jnp.where(low, 0.0, tap[2]), jnp.where(low, tap[1], tap[0])]
            pieces.append(
                jnp.concatenate([jnp.concatenate(even, axis=1), jnp.concatenate(odd, axis=1)], axis=0).astype(bf16)
            )
    return jnp.concatenate(pieces, axis=1)


def back(before_ref, first_ref, last_ref, after_ref, weight_ref, out_ref, taps_ref, turn_ref, flat_ref):
    zero = jnp.zeros((256, LANES), bf16)
    for plane, source in enumerate((before_ref, first_ref, last_ref, after_ref)):
        taps_ref[plane, 0] = zero
        taps_ref[plane, 9] = zero
        for r in range(8):
            cells = source[r].astype(f32)
            for v, piece in enumerate(shifted(cells[:64], cells[64:])):
                taps_ref[plane, 1 + r, 64 * v : 64 * v + 64, :] = piece
    weights = back_weights(weight_ref)
    for z in range(2):
        for pair in range(4):
            around = []
            for a in range(3):
                for b in range(3):
                    around.append(
                        jnp.concatenate([taps_ref[z + a, 2 * pair + b], taps_ref[z + a, 2 * pair + 1 + b]], axis=1)
                    )
            grad = jnp.dot(weights, jnp.concatenate(around, axis=0), preferred_element_type=f32).astype(bf16)
            for side in range(2):
                row = 8 * z + 2 * pair + side
                lanes = slice(LANES * side, LANES * side + LANES)
                turn_ref[32 * row : 32 * row + 32, :] = jnp.concatenate([grad[:32, lanes], grad[32:, lanes]], axis=1)
    columns = jnp.dot(turn_ref[...], column_split(True), preferred_element_type=f32)
    for row in range(16):
        for side in range(2):
            flat_ref[side, pl.ds(row, 32, stride=16), :] = columns[
                32 * row : 32 * row + 32, LANES * side : LANES * side + LANES
            ]
    for side in range(2):
        out_ref[:, LANES * side : LANES * side + LANES] = flat_ref[side].astype(bf16)


def sum_space(got_ref, send_ref):
    total = got_ref[0, 8:24, :].astype(f32)
    for j in range(1, 16):
        total = total + got_ref[j, 8:24, :].astype(f32)
    total = total.astype(bf16)
    for j in range(16):
        send_ref[j] = total


def place_output(got_ref, out_ref, wide_ref):
    for d in range(16):
        for r in range(4):
            wide_ref[pl.ds(4 * d + r, 8, stride=64), :] = got_ref[d, 0:8, LANES * r : LANES * r + LANES].astype(f32)
    out_ref[...] = wide_ref[...].astype(bf16)


def sum_samples(strided_scale, conv_scale, got_ref, strided_ref, send_ref):
    total = got_ref[0].astype(f32)
    for j in range(1, 16):
        total = total + got_ref[j].astype(f32)
    strided_ref[...] = total[:8] * strided_scale
    conv = (total[8:] * conv_scale).astype(bf16)
    for j in range(16):
        send_ref[j] = conv


def place_conv(got_ref, out_ref):
    for j in range(16):
        rows, side = 8 * (j // 2), 512 * (j % 2)
        width = min(512, 864 - side)
        out_ref[rows : rows + 8, side : side + width] = got_ref[j, :, :width].astype(f32)


def shards(volume, conv_weight, strided_weight, cotangent):
    depth = volume.shape[2]
    n_space, n_dp = lax.axis_size("space"), lax.axis_size("dp")
    cells = n_dp * depth * n_space * volume.shape[3] * volume.shape[4]
    ends = n_space - 1
    up = [(i, i + 1) for i in range(ends)]
    down = [(i + 1, i) for i in range(ends)]

    def shape(dims, dtype):
        return jax.ShapeDtypeStruct(dims, dtype)

    send = call(
        send_first, shape((16, 8, 1024), bf16), [pltpu.VMEM((512, LANES), f32)], 0, 400_000,
        cotangent.reshape(512, LANES), strided_weight,
    )
    got = lax.all_to_all(send, "space", 0, 0, tiled=True)
    before = lax.ppermute(volume, "space", up).reshape(512, 256)
    after = lax.ppermute(volume, "space", down).reshape(512, 256)
    plane = shape((8, LANES, LANES), bf16)
    send, first, last = call(
        main, (shape((16, 24, 512), bf16), plane, plane),
        [
            pltpu.VMEM((2, 512, LANES), f32),
            pltpu.VMEM((4, 10, LANES, LANES), bf16),
            pltpu.VMEM((512, 512), f32),
            pltpu.VMEM((512, 512), bf16),
            pltpu.VMEM((8, LANES, LANES), bf16),
            pltpu.VMEM((LANES, 9 * LANES), f32),
        ],
        2_000_000_000, 2_000_000,
        before, volume.reshape(512, 256), after, got, conv_weight,
    )
    got = lax.all_to_all(send, "space", 0, 0, tiled=True)
    grad_before = lax.ppermute(last, "space", up)
    grad_after = lax.ppermute(first, "space", down)
    send = call(sum_space, shape((16, 16, 512), bf16), [], 0, 600_000, got)
    output = call(place_output, shape((512, LANES), bf16), [pltpu.VMEM((512, LANES), f32)], 0, 600_000, got)
    got = lax.all_to_all(send, "dp", 0, 0, tiled=True)
    strided_grad, send = call(
        lambda *refs: sum_samples(1.0 / math.sqrt(cells / 8), 1.0 / math.sqrt(cells), *refs),
        (shape((8, 512), f32), shape((16, 8, 512), bf16)), [], 0, 600_000, got,
    )
    got = lax.all_to_all(send, "space", 0, 0, tiled=True)
    conv_grad = call(place_conv, shape((64, 864), f32), [], 0, 300_000, got)
    vol_grad = call(
        back, shape((512, 256), bf16),
        [
            pltpu.VMEM((4, 10, 256, LANES), bf16),
            pltpu.VMEM((512, 256), bf16),
            pltpu.VMEM((2, 512, LANES), f32),
        ],
        2_000_000_000, 2_000_000,
        grad_before, first, last, grad_after, conv_weight,
    )
    return output.reshape(cotangent.shape), vol_grad.reshape(volume.shape), conv_grad, strided_grad


def solution(mesh):
    return jax.shard_map(
        shards,
        mesh=mesh,
        in_specs=(
            P("dp", None, "space", None, None),
            P(),
            P("space", None),
            P("dp", "space", None, None, None),
        ),
        out_specs=(
            P("dp", "space", None, None, None),
            P("dp", None, "space", None, None),
            P(),
            P("space", None),
        ),
        check_vma=False,
    )
```

time: 133 us -> 78.2 us (0.59)
  local copies, waits for them, and re-layouts: 57.4 us -> 1.61 us
  blocking collectives: 0 us -> 29.5 us
  starting transfers between devices: 45.5 us -> 29.6 us
  matrix products: 14.9 us -> 0 us
  Pallas kernels: 0 us -> 10.3 us
  waiting for transfers between devices: 11 us -> 5.88 us
  other arithmetic: 2.18 us -> 0 us
    all_to_all x0 -> x2, blocking collectives: none -> 29.5 us  [shards(): got = lax.all_to_all(send, 'space', 0, 0, tiled=True)]
    reshape x15 -> x0, local copies, waits for them, and re-layouts: 28.9 us -> none  [the longest x2 23 us: taps(): return stacked.transpose(0, 3, 4, 1, 2, 5).reshape(ab * v * c, z * r * w)]
    all_to_all x4 -> x2, starting transfers between devices: 33.4 us -> 15.4 us  [the longest x1 8.32 us: shards(): got = lax.all_to_all(send, 'dp', 0, 0, tiled=True)]
    dot_general x8 -> x0, matrix products: 14.9 us -> none  [the longest x1 5.47 us: shards(): vol_grad = jnp.dot(back, grad_taps, preferred_element_type=f32).astype(bf16)]
    pallas_call x0 -> x7, Pallas kernels: none -> 10.3 us  [call(): pl.pallas_call(kernel, out_shape=outs, in_specs=[whole] * len(args), out_...]
    dot_general x1 -> x0, local copies, waits for them, and re-layouts: 8.17 us -> none  [shards(): lax.dot_general(pre_grad, vol_taps, (((1,), (1,)), ((), ())), preferred_e...]
    unnamed x27 -> x8, local copies, waits for them, and re-layouts: 8.76 us -> 1.61 us
    transpose x3 -> x0, local copies, waits for them, and re-layouts: 5.74 us -> none  [the longest x1 4.4 us: taps(): return stacked.transpose(0, 3, 4, 1, 2, 5).reshape(ab * v * c, z * r * w)]
  transfers between devices with their start and end apart: 8 -> 6, of which waited for: 3 -> 2; matrix products, arithmetic and copies ran while one was open for 41% -> 0% of each run, Pallas kernels for 0% -> 5%
where the time goes in v2:
time: 78.2 us; the launch traced here: 77.7 us
  starting transfers between devices  29.6 us (38%)
  blocking collectives  29.5 us (38%)
  Pallas kernels  10.3 us (13%)
  waiting for transfers between devices  5.88 us (8%)
  local copies, waits for them, and re-layouts  1.61 us (2%)
    all_to_all x2, blocking collectives, shards(): got = lax.all_to_all(send, 'space', 0, 0, tiled=True)  29.5 us
    pallas_call x7, Pallas kernels, call(): pl.pallas_call(kernel, out_shape=outs, in_specs=[whole] * len(args), out_...  10.3 us
    all_to_all x1, starting transfers between devices, shards(): got = lax.all_to_all(send, 'dp', 0, 0, tiled=True)  8.32 us
    all_to_all x1, starting transfers between devices, shards(): got = lax.all_to_all(send, 'space', 0, 0, tiled=True)  7.05 us
    ppermute x1, starting transfers between devices, shards(): before = lax.ppermute(volume, 'space', up).reshape(512, 256)  6.04 us
    ppermute x1, starting transfers between devices, shards(): grad_before = lax.ppermute(last, 'space', up)  4.33 us
    all_to_all x1, waiting for transfers between devices, shards(): got = lax.all_to_all(send, 'space', 0, 0, tiled=True)  4.29 us
    ppermute x1, starting transfers between devices, shards(): after = lax.ppermute(volume, 'space', down).reshape(512, 256)  1.92 us
  transfers between devices with their start and end apart: 6, of which 2 were waited for; matrix products, arithmetic and copies ran while one was open for 0% of the time, Pallas kernels for 5%

profile of v2, /device:TPU:1, one launch (start us, length us, event | category | flops | bytes accessed | tf_op | source)
XLA Modules:
  0.0 77.7 jit_solution(13461703040230925414)
XLA Ops:
  0.6 6.0 %collective-permute-start = (bf16[1,32,2,8,256]{4,3,2,1,0:T(8,128)(2,1)}, bf16[1,32,2,8,256]{4,3,2,1,0:T(8,128)(2,1)S(1)}, u32[]{:S(2)}, u32[]{:S(2)}) collective-permute-start(bf16[1,32,2,8,256]{4,3,2,1,0:T(8,128)(2,1)} %param.4), channel_id=1, source_target_pairs={{0,1},{1,2},{2,3},{3,4},{4,5},{5,6},{6,7},{7,8},{8,9},{9,10},{10,1... | collective-permute-start | bytes 786440 | tf_op jit(solution)/shard_map/ppermute | solution.py:249
  6.7 1.9 %collective-permute-start.1 = (bf16[1,32,2,8,256]{4,3,2,1,0:T(8,128)(2,1)}, bf16[1,32,2,8,256]{4,3,2,1,0:T(8,128)(2,1)S(1)}, u32[]{:S(2)}, u32[]{:S(2)}) collective-permute-start(bf16[1,32,2,8,256]{4,3,2,1,0:T(8,128)(2,1)} %param.4), channel_id=1, source_target_pairs={{1,0},{2,1},{3,2},{4,3},{5,4},{6,5},{7,6},{8,7},{9,8},{10,9},{11,1... | collective-permute-start | bytes 786440 | tf_op jit(solution)/shard_map/ppermute | solution.py:250
  8.6 0.0 copy-start
  8.6 0.9 %copy-done = bf16[1,8,16,4,128]{4,3,2,1,0:T(4,128)(2,1)S(1)} copy-done((bf16[1,8,16,4,128]{4,3,2,1,0:T(4,128)(2,1)S(1)}, bf16[1,8,16,4,128]{4,3,2,1,0:T(4,128)(2,1)}, u32[]{:S(2)}) %copy-start) | copy-done | bytes 131096
  9.5 0.0 copy-start.1
  9.5 0.7 copy-done.1
  10.2 0.2 shard_map.75
  10.4 0.0 copy-start.2
  10.4 0.0 copy-start.3
  10.4 16.2 %all_to_all.20.got_ref = bf16[16,8,1024]{2,1,0:T(8,128)(2,1)S(1)} all-to-all(bf16[16,8,1024]{2,1,0:T(8,128)(2,1)S(1)} %shard_map.75), channel_id=1, replica_groups=mesh['dp'=16,'space'=16] {'space'}, dimensions={0} | all-to-all | bytes 524288 | tf_op jit(solution)/shard_map/all_to_all | solution.py:248
  26.6 0.0 collective-permute-done
  26.6 0.0 collective-permute-done.1
  26.6 0.0 copy-done.2
  26.6 0.0 copy-done.3
  26.6 4.7 %shard_map.76 = (bf16[16,24,512]{2,1,0:T(8,128)(2,1)S(1)}, bf16[8,128,128]{2,1,0:T(8,128)(2,1)S(1)}, bf16[8,128,128]{2,1,0:T(8,128)(2,1)S(1)}) custom-call(bf16[512,256]{1,0:T(8,128)(2,1)S(1)} %bitcast.8, bf16[512,256]{1,0:T(8,128)(2,1)S(1)} %bitcast.7, bf16[512,256]{1,0:T(8,128)(2,1)S(1)} %bitcast.9, bf16[16,8,1024]{2,1,0:T(8,128)(2,1)S(1)} %all_to_all.20.got_ref, ...), custom_call_target="tpu_custom_call" | custom-call | flops 2000000000 | bytes 2000000 | tf_op jit(solution)/shard_map/pallas_call | solution.py:19
  31.3 13.4 %all_to_all.21.got_ref = bf16[16,24,512]{2,1,0:T(8,128)(2,1)S(1)} all-to-all(bf16[16,24,512]{2,1,0:T(8,128)(2,1)S(1)} %get-tuple-element.9), channel_id=1, replica_groups=mesh['dp'=16,'space'=16] {'space'}, dimensions={0} | all-to-all | bytes 786432 | tf_op jit(solution)/shard_map/all_to_all | solution.py:265
  44.6 0.8 shard_map.79
  45.4 8.3 %all-to-all-start.2 = ((bf16[16,16,512]{2,1,0:T(8,128)(2,1)}), bf16[16,16,512]{2,1,0:T(8,128)(2,1)S(1)}, u32[]{:S(2)}, u32[]{:S(2)}) async-start(bf16[16,16,512]{2,1,0:T(8,128)(2,1)} %shard_map.79), calls=%async_computation.2 | async-start | bytes 524288 | tf_op jit(solution)/shard_map/all_to_all | solution.py:270
  53.7 4.3 %collective-permute-start.2 = (bf16[8,128,128]{2,1,0:T(8,128)(2,1)S(1)}, bf16[8,128,128]{2,1,0:T(8,128)(2,1)S(1)}, u32[]{:S(2)}, u32[]{:S(2)}) collective-permute-start(bf16[8,128,128]{2,1,0:T(8,128)(2,1)S(1)} %get-tuple-element.10.last_ref), channel_id=1, source_target_pairs={{0,1},{1,2},{2,3},{3,4},{4,5},{5,6},{6,7},{7,8},{8,9},{9,10},{10,1... | collective-permute-start | bytes 786440 | tf_op jit(solution)/shard_map/ppermute | solution.py:266
  58.1 1.9 %collective-permute-start.3 = (bf16[8,128,128]{2,1,0:T(8,128)(2,1)S(1)}, bf16[8,128,128]{2,1,0:T(8,128)(2,1)S(1)}, u32[]{:S(2)}, u32[]{:S(2)}) collective-permute-start(bf16[8,128,128]{2,1,0:T(8,128)(2,1)S(1)} %get-tuple-element.11.first_ref), channel_id=1, source_target_pairs={{1,0},{2,1},{3,2},{4,3},{5,4},{6,5},{7,6},{8,7},{9,8},{10,9},{11,1... | collective-permute-start | bytes 786440 | tf_op jit(solution)/shard_map/ppermute | solution.py:267
  60.0 1.6 %all-to-all-done.2.refs_0_ = bf16[16,16,512]{2,1,0:T(8,128)(2,1)S(1)} async-done(((bf16[16,16,512]{2,1,0:T(8,128)(2,1)}), bf16[16,16,512]{2,1,0:T(8,128)(2,1)S(1)}, u32[]{:S(2)}, u32[]{:S(2)}) %all-to-all-start.2) | async-done | bytes 262176 | tf_op jit(solution)/shard_map/all_to_all | solution.py:270
  61.6 0.7 shard_map.80
  62.3 7.1 %all-to-all-start.3 = ((bf16[16,8,512]{2,1,0:T(8,128)(2,1)}), bf16[16,8,512]{2,1,0:T(8,128)(2,1)S(1)}, u32[]{:S(2)}, u32[]{:S(2)}) async-start(bf16[16,8,512]{2,1,0:T(8,128)(2,1)} %get-tuple-element.12), calls=%async_computation.3 | async-start | bytes 262144 | tf_op jit(solution)/shard_map/all_to_all | solution.py:275
  69.3 0.0 collective-permute-done.2.before_ref
  69.3 0.0 collective-permute-done.3.after_ref
  69.3 2.5 %shard_map.78 = bf16[512,256]{1,0:T(8,128)(2,1)} custom-call(bf16[8,128,128]{2,1,0:T(8,128)(2,1)S(1)} %collective-permute-done.2.before_ref, bf16[8,128,128]{2,1,0:T(8,128)(2,1)S(1)} %get-tuple-element.11.first_ref, bf16[8,128,128]{2,1,0:T(8,128)(2,1)S(1)} %get-tuple-element.10.last_ref, bf16[8,128,128]{2,1,0:T(8,128)(2,1)S(1)} %collective-permute-done.3.after_ref, ...), custom_call_target="tpu_custom_call" | custom-call | flops 2000000000 | bytes 2000000 | tf_op jit(solution)/shard_map/pallas_call | solution.py:19
  71.9 0.8 %shard_map.77 = bf16[512,128]{1,0:T(8,128)(2,1)} custom-call(bf16[16,24,512]{2,1,0:T(8,128)(2,1)S(1)} %all_to_all.21.got_ref), custom_call_target="tpu_custom_call" | custom-call | bytes 600000 | tf_op jit(solution)/shard_map/pallas_call | solution.py:19
  72.7 4.3 %all-to-all-done.3.got_ref = bf16[16,8,512]{2,1,0:T(8,128)(2,1)S(1)} async-done(((bf16[16,8,512]{2,1,0:T(8,128)(2,1)}), bf16[16,8,512]{2,1,0:T(8,128)(2,1)S(1)}, u32[]{:S(2)}, u32[]{:S(2)}) %all-to-all-start.3) | async-done | bytes 131104 | tf_op jit(solution)/shard_map/all_to_all | solution.py:275
  77.0 0.7 shard_map.81
Async XLA Ops:
  0.6 25.9 %collective-permute-start = (bf16[1,32,2,8,256]{4,3,2,1,0:T(8,128)(2,1)}, bf16[1,32,2,8,256]{4,3,2,1,0:T(8,128)(2,1)S(1)}, u32[]{:S(2)}, u32[]{:S(2)}) collective-permute-start(bf16[1,32,2,8,256]{4,3,2,1,0:T(8,128)(2,1)} %param.4), channel_id=1, source_target_pairs={{0,1},{1,2},{2,3},{3,4},{4,5},{5,6},{6,7},{7,8},{8,9},{9,10},{10,1... | collective-permute-start | bytes 786440 | tf_op jit(solution)/shard_map/ppermute | solution.py:249
  6.7 19.9 %collective-permute-start.1 = (bf16[1,32,2,8,256]{4,3,2,1,0:T(8,128)(2,1)}, bf16[1,32,2,8,256]{4,3,2,1,0:T(8,128)(2,1)S(1)}, u32[]{:S(2)}, u32[]{:S(2)}) collective-permute-start(bf16[1,32,2,8,256]{4,3,2,1,0:T(8,128)(2,1)} %param.4), channel_id=1, source_target_pairs={{1,0},{2,1},{3,2},{4,3},{5,4},{6,5},{7,6},{8,7},{9,8},{10,9},{11,1... | collective-permute-start | bytes 786440 | tf_op jit(solution)/shard_map/ppermute | solution.py:250
  8.6 0.9 %copy-start = (bf16[1,8,16,4,128]{4,3,2,1,0:T(4,128)(2,1)S(1)}, bf16[1,8,16,4,128]{4,3,2,1,0:T(4,128)(2,1)}, u32[]{:S(2)}) copy-start(bf16[1,8,16,4,128]{4,3,2,1,0:T(4,128)(2,1)} %param.7) | copy-start | bytes 393220
  9.5 0.7 copy-start.1
  10.4 16.2 %copy-start.2 = (bf16[1,32,2,8,256]{4,3,2,1,0:T(8,128)(2,1)S(1)}, bf16[1,32,2,8,256]{4,3,2,1,0:T(8,128)(2,1)}, u32[]{:S(2)}) copy-start(bf16[1,32,2,8,256]{4,3,2,1,0:T(8,128)(2,1)} %param.4) | copy-start | bytes 786436
  10.4 16.2 %copy-start.3 = (bf16[64,864]{1,0:T(8,128)(2,1)S(1)}, bf16[64,864]{1,0:T(8,128)(2,1)}, u32[]{:S(2)}) copy-start(bf16[64,864]{1,0:T(8,128)(2,1)} %weight_ref.5) | copy-start | bytes 331780
  45.4 16.2 %all-to-all-start.2 = ((bf16[16,16,512]{2,1,0:T(8,128)(2,1)}), bf16[16,16,512]{2,1,0:T(8,128)(2,1)S(1)}, u32[]{:S(2)}, u32[]{:S(2)}) async-start(bf16[16,16,512]{2,1,0:T(8,128)(2,1)} %shard_map.79), calls=%async_computation.2 | async-start | bytes 524288 | tf_op jit(solution)/shard_map/all_to_all | solution.py:270
  53.7 15.6 %collective-permute-start.2 = (bf16[8,128,128]{2,1,0:T(8,128)(2,1)S(1)}, bf16[8,128,128]{2,1,0:T(8,128)(2,1)S(1)}, u32[]{:S(2)}, u32[]{:S(2)}) collective-permute-start(bf16[8,128,128]{2,1,0:T(8,128)(2,1)S(1)} %get-tuple-element.10.last_ref), channel_id=1, source_target_pairs={{0,1},{1,2},{2,3},{3,4},{4,5},{5,6},{6,7},{7,8},{8,9},{9,10},{10,1... | collective-permute-start | bytes 786440 | tf_op jit(solution)/shard_map/ppermute | solution.py:266
  58.1 11.3 %collective-permute-start.3 = (bf16[8,128,128]{2,1,0:T(8,128)(2,1)S(1)}, bf16[8,128,128]{2,1,0:T(8,128)(2,1)S(1)}, u32[]{:S(2)}, u32[]{:S(2)}) collective-permute-start(bf16[8,128,128]{2,1,0:T(8,128)(2,1)S(1)} %get-tuple-element.11.first_ref), channel_id=1, source_target_pairs={{1,0},{2,1},{3,2},{4,3},{5,4},{6,5},{7,6},{8,7},{9,8},{10,9},{11,1... | collective-permute-start | bytes 786440 | tf_op jit(solution)/shard_map/ppermute | solution.py:267
  62.3 14.7 %all-to-all-start.3 = ((bf16[16,8,512]{2,1,0:T(8,128)(2,1)}), bf16[16,8,512]{2,1,0:T(8,128)(2,1)S(1)}, u32[]{:S(2)}, u32[]{:S(2)}) async-start(bf16[16,8,512]{2,1,0:T(8,128)(2,1)} %get-tuple-element.12), calls=%async_computation.3 | async-start | bytes 262144 | tf_op jit(solution)/shard_map/all_to_all | solution.py:275

commit v3 on v2

v3 whole, which is shorter than its diff:
```python
import math

import jax
import jax.numpy as jnp
from jax import lax
from jax.experimental import pallas as pl
from jax.experimental.pallas import tpu as pltpu
from jax.sharding import PartitionSpec as P

root_two_pi = 0.7978845608028654
bf16 = jnp.bfloat16
f32 = jnp.float32
LANES = 128
VMEM_LIMIT = 16 * 1024 * 1024


def call(kernel, outs, scratch, flops, moved, *args, space=pltpu.VMEM):
    whole = pl.BlockSpec(memory_space=pltpu.VMEM)
    return pl.pallas_call(
        kernel,
        out_shape=outs,
        in_specs=[pl.BlockSpec(memory_space=space)] * len(args),
        out_specs=jax.tree.map(lambda _: whole, outs),
        scratch_shapes=scratch,
        compiler_params=pltpu.CompilerParams(vmem_limit_bytes=VMEM_LIMIT),
        cost_estimate=pl.CostEstimate(flops=flops, bytes_accessed=moved, transcendentals=0),
    )(*args)


def column_split(transposed=False):
    size = 2 * LANES
    source = lax.broadcasted_iota(jnp.int32, (size, size), 1 if transposed else 0)
    place = lax.broadcasted_iota(jnp.int32, (size, size), 0 if transposed else 1)
    hit = source == 2 * (place & (LANES - 1)) + (place >> 7)
    return jnp.where(hit, 1.0, 0.0).astype(bf16)


def shifted(even, odd):
    lane = lax.broadcasted_iota(jnp.int32, even.shape, 1)
    odd_before = jnp.where(lane == 0, 0.0, pltpu.roll(odd, 1, 1))
    even_after = jnp.where(lane == LANES - 1, 0.0, pltpu.roll(even, LANES - 1, 1))
    return [odd_before.astype(bf16), even.astype(bf16), odd.astype(bf16), even_after.astype(bf16)]


def core_index():
    return lax.rem(lax.axis_index("space"), 2)


def send_first(cot_hbm, weight_hbm, out_ref, cot_ref, weight_ref, wide_ref, sems):
    copies = [
        pltpu.make_async_copy(source, target, sems.at[i])
        for i, (source, target) in enumerate(((cot_hbm, cot_ref), (weight_hbm, weight_ref)))
    ]
    for copy in copies:
        copy.start()
    for copy in copies:
        copy.wait()
    wide_ref[...] = cot_ref[...].astype(f32)
    weights = weight_ref[...]
    for d in range(16):
        rows = [wide_ref[pl.ds(4 * d + r, 8, stride=64), :] for r in range(4)]
        out_ref[d, :, 0:512] = jnp.concatenate(rows, axis=1).astype(bf16)
        out_ref[d, :, 512:1024] = weights


def split_columns(own_ref, across_ref, inside_ref, flat_ref, planes_ref):
    columns = jnp.dot(own_ref[...], column_split(), preferred_element_type=f32)
    for e in range(2):
        flat_ref[e] = columns[:, LANES * e : LANES * e + LANES]
    for z in range(2):
        for r in range(8):
            for e in range(2):
                cells = flat_ref[e, pl.ds(8 * z + r, 32, stride=16), :]
                planes_ref[z, r, 32 * e : 32 * e + 32, :] = cells.astype(bf16)
    core = core_index()
    across_ref[...] = planes_ref[core]
    inside_ref[...] = planes_ref[1 - core]


def tap_weights(weight_ref):
    mid = weight_ref.shape[0]
    lane = lax.broadcasted_iota(jnp.int32, (mid, LANES), 1)
    tiles = [weight_ref[:, LANES * t : LANES * (t + 1)].astype(f32) for t in range(6)]
    tail = weight_ref[:, 768:864].astype(f32)
    tiles.append(jnp.concatenate([tail, jnp.zeros((mid, 32), f32)], axis=1))
    halves = [[], []]
    for ab in range(9):
        first, inset = divmod(96 * ab, LANES)
        rolled = tiles[first] if inset == 0 else pltpu.roll(tiles[first], LANES - inset, 1)
        if inset > 32:
            after = pltpu.roll(tiles[first + 1], LANES - inset, 1)
            rolled = jnp.where(lane < LANES - inset, rolled, after)
        own = jnp.where(lane < 96, rolled, 0.0)
        halves[0].append(own.astype(bf16))
        halves[1].append(pltpu.roll(own, 32, 1).astype(bf16))
    return jnp.concatenate([jnp.concatenate(half, axis=1) for half in halves], axis=0)


def fill_taps(taps_ref, planes):
    size = taps_ref.shape[2] // 4
    zero = jnp.zeros(taps_ref.shape[2:], bf16)
    for plane, source in planes:
        taps_ref[plane, 0] = zero
        taps_ref[plane, 9] = zero
        for r in range(8):
            cells = source[r].astype(f32)
            for v, piece in enumerate(shifted(cells[:size], cells[size:])):
                taps_ref[plane, 1 + r, size * v : size * v + size, :] = piece


def surroundings(taps_ref, planes, pair):
    return jnp.concatenate(
        [
            jnp.concatenate([taps_ref[plane, 2 * pair + b], taps_ref[plane, 2 * pair + 1 + b]], axis=1)
            for plane in planes
            for b in range(3)
        ],
        axis=0,
    )


def one_plane(z, planes, got_ref, weight_ref, taps_ref, grad_ref, block_ref, grad_plane_ref, conv_ref):
    fill_taps(taps_ref, planes)
    cot = got_ref[:, :, 0:512].reshape(128, 512)
    filters = got_ref[:, :, pl.ds(pl.multiple_of(512 + 256 * z, 256), 256)].reshape(128, 256)
    grad_ref[...] = jnp.dot(filters.astype(f32).T.astype(bf16), cot, preferred_element_type=f32)
    weights = tap_weights(weight_ref)
    for pair in range(4):
        around = surroundings(taps_ref, range(3), pair)
        pre = jnp.dot(weights, around, preferred_element_type=f32)
        square = pre * pre
        inner = root_two_pi * pre * (1.0 + 0.044715 * square)
        hyper = jnp.tanh(inner)
        half = 0.5 * (1.0 + hyper)
        hidden = (pre * half).astype(bf16)
        slope = half + 0.5 * pre * (1.0 - hyper * hyper) * (root_two_pi + (3.0 * 0.044715 * root_two_pi) * square)
        halves = []
        for side in range(2):
            rows = slice(128 * side, 128 * side + 128)
            columns = slice(LANES * pair, LANES * pair + LANES)
            lanes = slice(LANES * side, LANES * side + LANES)
            block_ref[rows, columns] = hidden[:, lanes]
            halves.append((grad_ref[rows, columns] * slope[:, lanes]).astype(bf16))
            grad_plane_ref[2 * pair + side] = halves[side]
        part = lax.dot_general(
            jnp.concatenate(halves, axis=1), around, (((1,), (1,)), ((), ())), preferred_element_type=f32
        )
        if pair == 0:
            conv_ref[...] = part
        else:
            conv_ref[...] += part
    blocks = block_ref[...]
    out = jnp.dot(filters, blocks, preferred_element_type=f32)
    strided = lax.dot_general(cot, blocks, (((1,), (1,)), ((), ())), preferred_element_type=f32)
    return out, strided


def inside(across_own, inside_own, inside_got, got_ref, weight_ref, grad_plane_ref, conv_ref, out_ref, strided_ref,
           taps_ref, grad_ref, block_ref):
    core = core_index()
    out, strided = one_plane(
        1 - core, ((2 * core, across_own), (1, inside_own), (2 - 2 * core, inside_got)),
        got_ref, weight_ref, taps_ref, grad_ref, block_ref, grad_plane_ref, conv_ref,
    )
    out_ref[...] = out
    strided_ref[...] = strided


def across(across_got, across_own, inside_own, got_ref, weight_ref, conv_in, out_in, strided_in, send_ref, grad_plane_ref,
           taps_ref, grad_ref, block_ref, conv_ref):
    core = core_index()
    out, strided = one_plane(
        core, ((2 * core, across_got), (1, across_own), (2 - 2 * core, inside_own)),
        got_ref, weight_ref, taps_ref, grad_ref, block_ref, grad_plane_ref, conv_ref,
    )
    out = out + out_in[...]
    other = strided_in[...]
    strided = jnp.concatenate(
        [jnp.where(core == 0, strided, other), jnp.where(core == 0, other, strided)], axis=1
    )
    lane = lax.broadcasted_iota(jnp.int32, (64, LANES), 1)
    tiles = [jnp.zeros((64, LANES), f32)] * 8
    for ab in range(9):
        lanes = pl.ds(LANES * ab, LANES)
        even = conv_ref[0:64, lanes] + conv_in[0:64, lanes]
        odd = conv_ref[64:128, lanes] + conv_in[64:128, lanes]
        conv = even + pltpu.roll(odd, 96, 1)
        first, inset = divmod(96 * ab, LANES)
        moved = conv if inset == 0 else pltpu.roll(conv, inset, 1)
        tiles[first] = jnp.where((lane >= inset) & (lane < inset + 96), moved, tiles[first])
        if inset > 32:
            tiles[first + 1] = jnp.where(lane < inset - 32, moved, tiles[first + 1])
    conv = jnp.concatenate(tiles, axis=1)
    for j in range(16):
        rows, group, side = 8 * j, 8 * (j // 2), 512 * (j % 2)
        piece = jnp.concatenate(
            [out[rows : rows + 8], strided[rows : rows + 8], conv[group : group + 8, side : side + 512]], axis=0
        )
        send_ref[j] = piece.astype(bf16)


def back_weights(weight_ref):
    wide = weight_ref[...].astype(f32)
    turned = jnp.concatenate([wide, wide], axis=0).T
    lane = lax.broadcasted_iota(jnp.int32, (32, LANES), 1)
    low = lane < 64
    pieces = []
    for a in range(3):
        for b in range(3):
            at = 32 * 3 * (3 * (2 - a) + 2 - b)
            tap = [turned[at + 32 * e : at + 32 * e + 32] for e in range(3)]
            even = [jnp.where(low, tap[2], tap[1]), jnp.where(low, tap[0], 0.0)]
            odd = [jnp.where(low, 0.0, tap[2]), jnp.where(low, tap[1], tap[0])]
            pieces.append(
                jnp.concatenate([jnp.concatenate(even, axis=1), jnp.concatenate(odd, axis=1)], axis=0).astype(bf16)
            )
    return jnp.concatenate(pieces, axis=1)


def back(across_own, inside_own, weight_ref, own_ref, across_ref, inside_ref, taps_ref, ends_ref):
    core = core_index()
    fill_taps(taps_ref, ((core, across_own), (1 - core, inside_own)))
    weights = back_weights(weight_ref)
    for plane in range(-1, 3):
        sources = [z for z in range(2) if 0 <= z - plane + 1 < 3]
        depth = sources[0] - plane + 1
        columns = weights[:, 768 * depth : 768 * (depth + len(sources))]
        for pair in range(4):
            grad = jnp.dot(columns, surroundings(taps_ref, sources, pair), preferred_element_type=f32)
            for side in range(2):
                part = grad[:, LANES * side : LANES * side + LANES]
                if 0 <= plane < 2:
                    own_ref[plane, 2 * pair + side] = part
                else:
                    ends_ref[(plane + 1) // 3, 2 * pair + side] = part.astype(bf16)
    across_ref[...] = ends_ref[core]
    inside_ref[...] = ends_ref[1 - core]


def finish(own_ref, across_got, inside_got, out_ref, sum_ref, turn_ref, flat_ref):
    core = core_index()
    sum_ref[core] = own_ref[core] + across_got[...].astype(f32)
    sum_ref[1 - core] = own_ref[1 - core] + inside_got[...].astype(f32)
    for row in range(16):
        grad = sum_ref[row // 8, row % 8].astype(bf16)
        turn_ref[32 * row : 32 * row + 32, :] = jnp.concatenate([grad[:32], grad[32:]], axis=1)
    columns = jnp.dot(turn_ref[...], column_split(True), preferred_element_type=f32)
    for row in range(16):
        for side in range(2):
            flat_ref[side, pl.ds(row, 32, stride=16), :] = columns[
                32 * row : 32 * row + 32, LANES * side : LANES * side + LANES
            ]
    for side in range(2):
        out_ref[:, LANES * side : LANES * side + LANES] = flat_ref[side].astype(bf16)


def sum_space(got_ref, send_ref):
    total = got_ref[0, 8:24, :].astype(f32)
    for j in range(1, 16):
        total = total + got_ref[j, 8:24, :].astype(f32)
    total = total.astype(bf16)
    for j in range(16):
        send_ref[j] = total


def place_output(got_ref, out_ref, wide_ref):
    for d in range(16):
        for r in range(4):
            wide_ref[pl.ds(4 * d + r, 8, stride=64), :] = got_ref[d, 0:8, LANES * r : LANES * r + LANES].astype(f32)
    out_ref[...] = wide_ref[...].astype(bf16)


def sum_samples(strided_scale, conv_scale, got_ref, strided_ref, send_ref):
    total = got_ref[0].astype(f32)
    for j in range(1, 16):
        total = total + got_ref[j].astype(f32)
    strided_ref[...] = total[:8] * strided_scale
    conv = (total[8:] * conv_scale).astype(bf16)
    for j in range(16):
        send_ref[j] = conv


def place_conv(got_ref, out_ref):
    for j in range(16):
        rows, side = 8 * (j // 2), 512 * (j % 2)
        width = min(512, 864 - side)
        out_ref[rows : rows + 8, side : side + width] = got_ref[j, :, :width].astype(f32)


def shards(volume, conv_weight, strided_weight, cotangent):
    depth = volume.shape[2]
    n_space, n_dp = lax.axis_size("space"), lax.axis_size("dp")
    cells = n_dp * depth * n_space * volume.shape[3] * volume.shape[4]
    between_chips = [pair for i in range(1, n_space - 1, 2) for pair in ((i, i + 1), (i + 1, i))]
    in_chip = [pair for i in range(0, n_space, 2) for pair in ((i, i + 1), (i + 1, i))]

    def shape(dims, dtype):
        return jax.ShapeDtypeStruct(dims, dtype)

    plane = shape((8, 64, LANES), bf16)
    send = call(
        send_first, shape((16, 8, 1024), bf16),
        [
            pltpu.VMEM((512, LANES), bf16),
            pltpu.VMEM((8, 512), bf16),
            pltpu.VMEM((512, LANES), f32),
            pltpu.SemaphoreType.DMA((2,)),
        ],
        0, 400_000,
        *(pltpu.with_memory_space_constraint(x, pltpu.HBM) for x in (cotangent.reshape(512, LANES), strided_weight)),
        space=pltpu.HBM,
    )
    got = lax.all_to_all(send, "space", 0, 0, tiled=True)
    cells_in, _ = lax.optimization_barrier((volume, send))
    across_vol, inside_vol = call(
        split_columns, (plane, plane),
        [pltpu.VMEM((2, 512, LANES), f32), pltpu.VMEM((2, 8, 64, LANES), bf16)], 4_000_000_000, 2_000_000,
        cells_in.reshape(512, 256),
    )
    across_got = lax.ppermute(across_vol, "space", between_chips)
    inside_got = lax.ppermute(inside_vol, "space", in_chip)
    grad_plane = shape((8, LANES, LANES), bf16)
    scratch = [pltpu.VMEM((3, 10, LANES, LANES), bf16), pltpu.VMEM((256, 512), f32), pltpu.VMEM((256, 512), bf16)]
    inside_grad, conv_terms, out_terms, strided_terms = call(
        inside,
        (grad_plane, shape((LANES, 9 * LANES), f32), shape((LANES, 512), f32), shape((LANES, 256), f32)),
        scratch, 3_000_000_000, 2_000_000,
        across_vol, inside_vol, inside_got, got, conv_weight,
    )
    send, across_grad = call(
        across, (shape((16, 24, 512), bf16), grad_plane),
        scratch + [pltpu.VMEM((LANES, 9 * LANES), f32)], 3_000_000_000, 3_000_000,
        across_got, across_vol, inside_vol, got, conv_weight, conv_terms, out_terms, strided_terms,
    )
    got = lax.all_to_all(send, "space", 0, 0, tiled=True)
    own_terms, across_terms, inside_terms = call(
        back, (shape((2, 8, 64, LANES), f32), plane, plane),
        [pltpu.VMEM((2, 10, 256, LANES), bf16), pltpu.VMEM((2, 8, 64, LANES), bf16)],
        3_000_000_000, 3_000_000,
        across_grad, inside_grad, conv_weight,
    )
    got, own_terms, across_terms, inside_terms = lax.optimization_barrier(
        (got, own_terms, across_terms, inside_terms)
    )
    across_got = lax.ppermute(across_terms, "space", between_chips)
    inside_got = lax.ppermute(inside_terms, "space", in_chip)
    send = call(sum_space, shape((16, 16, 512), bf16), [], 0, 600_000, got)
    output = call(place_output, shape((512, LANES), bf16), [pltpu.VMEM((512, LANES), f32)], 0, 600_000, got)
    got = lax.all_to_all(send, "dp", 0, 0, tiled=True)
    strided_grad, send = call(
        lambda *refs: sum_samples(1.0 / math.sqrt(cells / 8), 1.0 / math.sqrt(cells), *refs),
        (shape((8, 512), f32), shape((16, 8, 512), bf16)), [], 0, 600_000, got,
    )
    got = lax.all_to_all(send, "space", 0, 0, tiled=True)
    vol_grad = call(
        finish, shape((512, 256), bf16),
        [
            pltpu.VMEM((2, 8, 64, LANES), f32),
            pltpu.VMEM((512, 256), bf16),
            pltpu.VMEM((2, 512, LANES), f32),
        ],
        1_000_000_000, 2_000_000,
        own_terms, across_got, inside_got,
    )
    conv_grad = call(place_conv, shape((64, 864), f32), [], 0, 300_000, got)
    return output.reshape(cotangent.shape), vol_grad.reshape(volume.shape), conv_grad, strided_grad


def solution(mesh):
    return jax.shard_map(
        shards,
        mesh=mesh,
        in_specs=(
            P("dp", None, "space", None, None),
            P(),
            P("space", None),
            P("dp", "space", None, None, None),
        ),
        out_specs=(
            P("dp", "space", None, None, None),
            P("dp", None, "space", None, None),
            P(),
            P("space", None),
        ),
        check_vma=False,
    )
```

time: 78.2 us -> 74.9 us (0.958)
  blocking collectives: 29.5 us -> 0 us
  waiting for transfers between devices: 5.88 us -> 19.8 us
  starting transfers between devices: 29.6 us -> 39.8 us
  Pallas kernels: 10.3 us -> 14 us
  local copies, waits for them, and re-layouts: 1.61 us -> 0.01 us
    all_to_all x2 -> x0, blocking collectives: 29.5 us -> none  [shards(): got = lax.all_to_all(send, 'space', 0, 0, tiled=True)]
    all_to_all x1 -> x3, starting transfers between devices: 7.05 us -> 21.8 us  [shards(): got = lax.all_to_all(send, 'space', 0, 0, tiled=True)]
    all_to_all x1 -> x3, waiting for transfers between devices: 4.29 us -> 16.4 us  [shards(): got = lax.all_to_all(send, 'space', 0, 0, tiled=True)]
    ppermute x4, starting transfers between devices: 14.2 us -> 9.73 us  [the longest x1 5.08 us: shards(): across_got = lax.ppermute(across_vol, 'space', between_chips)]
    pallas_call x7 -> x10, Pallas kernels: 10.3 us -> 14 us  [call(): pl.pallas_call(kernel, out_shape=outs, in_specs=[pl.BlockSpec(memory_spac...]
    all_to_all x1, waiting for transfers between devices: 1.58 us -> 3.37 us  [shards(): got = lax.all_to_all(send, 'dp', 0, 0, tiled=True)]
    unnamed x8 -> x4, local copies, waits for them, and re-layouts: 1.61 us -> 0.01 us
  transfers between devices with their start and end apart: 6 -> 8, of which waited for: 2 -> 4; matrix products, arithmetic and copies ran while one was open for 0% -> 0% of each run, Pallas kernels for 5% -> 10%
where the time goes in v3:
time: 74.9 us; the launch traced here: 74.3 us
  starting transfers between devices  39.8 us (53%)
  waiting for transfers between devices  19.8 us (26%)
  Pallas kernels  14 us (19%)
    all_to_all x3, starting transfers between devices, shards(): got = lax.all_to_all(send, 'space', 0, 0, tiled=True)  21.8 us
    all_to_all x3, waiting for transfers between devices, shards(): got = lax.all_to_all(send, 'space', 0, 0, tiled=True)  16.4 us
    pallas_call x10, Pallas kernels, call(): pl.pallas_call(kernel, out_shape=outs, in_specs=[pl.BlockSpec(memory_spac...  14 us
    all_to_all x1, starting transfers between devices, shards(): got = lax.all_to_all(send, 'dp', 0, 0, tiled=True)  8.31 us
    ppermute x1, starting transfers between devices, shards(): across_got = lax.ppermute(across_vol, 'space', between_chips)  5.08 us
    ppermute x1, starting transfers between devices, shards(): across_got = lax.ppermute(across_terms, 'space', between_chips)  4.37 us
    all_to_all x1, waiting for transfers between devices, shards(): got = lax.all_to_all(send, 'dp', 0, 0, tiled=True)  3.37 us
  transfers between devices with their start and end apart: 8, of which 4 were waited for; matrix products, arithmetic and copies ran while one was open for 0% of the time, Pallas kernels for 10%

profile of v3, /device:TPU:1, one launch (start us, length us, event | category | flops | bytes accessed | tf_op | source)
XLA Modules:
  0.0 74.3 jit_solution(13631412580507717979)
XLA Ops:
  0.6 1.8 %shard_map.75 = bf16[16,8,1024]{2,1,0:T(8,128)(2,1)} custom-call(bf16[512,128]{1,0:T(8,128)(2,1)} %bitcast.5, bf16[8,512]{1,0:T(8,128)(2,1)} %weight_hbm.1), custom_call_target="tpu_custom_call" | custom-call | bytes 400000 | tf_op jit(solution)/shard_map/pallas_call | solution.py:19
  2.4 0.0 copy-start
  2.5 8.6 %all-to-all-start = ((bf16[16,8,1024]{2,1,0:T(8,128)(2,1)}), bf16[16,8,1024]{2,1,0:T(8,128)(2,1)S(1)}, u32[]{:S(2)}, u32[]{:S(2)}) async-start(bf16[16,8,1024]{2,1,0:T(8,128)(2,1)} %shard_map.75), calls=%async_computation | async-start | bytes 524288 | tf_op jit(solution)/shard_map/all_to_all | solution.py:313
  11.0 0.0 copy-done
  11.0 0.0 copy-start.1
  11.1 0.4 shard_map.76
  11.5 0.2 collective-permute-start.1
  11.7 5.1 %collective-permute-start = (bf16[8,64,128]{2,1,0:T(8,128)(2,1)S(1)}, bf16[8,64,128]{2,1,0:T(8,128)(2,1)S(1)}, u32[]{:S(2)}, u32[]{:S(2)}) collective-permute-start(bf16[8,64,128]{2,1,0:T(8,128)(2,1)S(1)} %get-tuple-element.23.across_own), channel_id=1, source_target_pairs={{1,2},{2,1},{3,4},{4,3},{5,6},{6,5},{7,8},{8,7},{9,10},{10,9},{11,... | collective-permute-start | bytes 393224 | tf_op jit(solution)/shard_map/ppermute | solution.py:320
  16.8 0.0 collective-permute-done.1.inside_got
  16.8 2.9 %all-to-all-done.got_ref = bf16[16,8,1024]{2,1,0:T(8,128)(2,1)S(1)} async-done(((bf16[16,8,1024]{2,1,0:T(8,128)(2,1)}), bf16[16,8,1024]{2,1,0:T(8,128)(2,1)S(1)}, u32[]{:S(2)}, u32[]{:S(2)}) %all-to-all-start) | async-done | bytes 262176 | tf_op jit(solution)/shard_map/all_to_all | solution.py:313
  19.7 0.0 copy-done.1
  19.7 2.3 %shard_map.77 = (bf16[8,128,128]{2,1,0:T(8,128)(2,1)S(1)}, f32[128,1152]{1,0:T(8,128)S(1)}, f32[128,512]{1,0:T(8,128)S(1)}, f32[128,256]{1,0:T(8,128)S(1)}) custom-call(bf16[8,64,128]{2,1,0:T(8,128)(2,1)S(1)} %get-tuple-element.23.across_own, bf16[8,64,128]{2,1,0:T(8,128)(2,1)S(1)} %get-tuple-element.24.inside_own, ...), custom_call_target="tpu_custom_call" | custom-call | flops 3000000000 | bytes 2000000 | tf_op jit(solution)/shard_map/pallas_call | solution.py:19
  22.0 0.0 collective-permute-done.across_got
  22.0 3.2 %shard_map.78 = (bf16[16,24,512]{2,1,0:T(8,128)(2,1)}, bf16[8,128,128]{2,1,0:T(8,128)(2,1)S(1)}) custom-call(bf16[8,64,128]{2,1,0:T(8,128)(2,1)S(1)} %collective-permute-done.across_got, bf16[8,64,128]{2,1,0:T(8,128)(2,1)S(1)} %get-tuple-element.23.across_own, bf16[8,64,128]{2,1,0:T(8,128)(2,1)S(1)} %get-tuple-element.24.inside_own, ...), custom_call_target="tpu_custom_call" | custom-call | flops 3000000000 | bytes 3000000 | tf_op jit(solution)/shard_map/pallas_call | solution.py:19
  25.2 6.2 %all-to-all-start.1 = ((bf16[16,24,512]{2,1,0:T(8,128)(2,1)}), bf16[16,24,512]{2,1,0:T(8,128)(2,1)S(1)}, u32[]{:S(2)}, u32[]{:S(2)}) async-start(bf16[16,24,512]{2,1,0:T(8,128)(2,1)} %get-tuple-element.28), calls=%async_computation.1 | async-start | bytes 786432 | tf_op jit(solution)/shard_map/all_to_all | solution.py:335
  31.4 2.2 %shard_map.79 = (f32[2,8,64,128]{3,2,1,0:T(8,128)S(1)}, bf16[8,64,128]{2,1,0:T(8,128)(2,1)S(1)}, bf16[8,64,128]{2,1,0:T(8,128)(2,1)S(1)}) custom-call(bf16[8,128,128]{2,1,0:T(8,128)(2,1)S(1)} %get-tuple-element.29.across_own, bf16[8,128,128]{2,1,0:T(8,128)(2,1)S(1)} %get-tuple-element.30.inside_own, bf16[64,864]{1,0:T(8,128)(2,1)S(1)} %copy-done.1), custom_call_target="tpu_custom_call" | custom-call | flops 3000000000 | bytes 3000000 | tf_op jit(solution)/shard_map/pallas_call | solution.py:19
  33.6 7.7 %all-to-all-done.1.got_ref = bf16[16,24,512]{2,1,0:T(8,128)(2,1)S(1)} async-done(((bf16[16,24,512]{2,1,0:T(8,128)(2,1)}), bf16[16,24,512]{2,1,0:T(8,128)(2,1)S(1)}, u32[]{:S(2)}, u32[]{:S(2)}) %all-to-all-start.1) | async-done | bytes 393248 | tf_op jit(solution)/shard_map/all_to_all | solution.py:335
  41.3 0.8 %shard_map.82 = bf16[16,16,512]{2,1,0:T(8,128)(2,1)} custom-call(bf16[16,24,512]{2,1,0:T(8,128)(2,1)S(1)} %all-to-all-done.1.got_ref), custom_call_target="tpu_custom_call" | custom-call | bytes 600000 | tf_op jit(solution)/shard_map/pallas_call | solution.py:19
  42.1 8.3 %all-to-all-start.2 = ((bf16[16,16,512]{2,1,0:T(8,128)(2,1)}), bf16[16,16,512]{2,1,0:T(8,128)(2,1)S(1)}, u32[]{:S(2)}, u32[]{:S(2)}) async-start(bf16[16,16,512]{2,1,0:T(8,128)(2,1)} %shard_map.82), calls=%async_computation.2 | async-start | bytes 524288 | tf_op jit(solution)/shard_map/all_to_all | solution.py:349
  50.4 4.4 %collective-permute-start.2 = (bf16[8,64,128]{2,1,0:T(8,128)(2,1)S(1)}, bf16[8,64,128]{2,1,0:T(8,128)(2,1)S(1)}, u32[]{:S(2)}, u32[]{:S(2)}) collective-permute-start(bf16[8,64,128]{2,1,0:T(8,128)(2,1)S(1)} %get-tuple-element.36), channel_id=1, source_target_pairs={{1,2},{2,1},{3,4},{4,3},{5,6},{6,5},{7,8},{8,7},{9,10},{10,9},{11,... | collective-permute-start | bytes 393224 | tf_op jit(solution)/shard_map/ppermute | solution.py:345
  54.8 0.1 collective-permute-start.3
  54.9 3.4 %all-to-all-done.2.refs_0_ = bf16[16,16,512]{2,1,0:T(8,128)(2,1)S(1)} async-done(((bf16[16,16,512]{2,1,0:T(8,128)(2,1)}), bf16[16,16,512]{2,1,0:T(8,128)(2,1)S(1)}, u32[]{:S(2)}, u32[]{:S(2)}) %all-to-all-start.2) | async-done | bytes 262176 | tf_op jit(solution)/shard_map/all_to_all | solution.py:349
  58.2 0.7 shard_map.83
  58.9 7.0 %all-to-all-start.3 = ((bf16[16,8,512]{2,1,0:T(8,128)(2,1)}), bf16[16,8,512]{2,1,0:T(8,128)(2,1)S(1)}, u32[]{:S(2)}, u32[]{:S(2)}) async-start(bf16[16,8,512]{2,1,0:T(8,128)(2,1)} %get-tuple-element.38), calls=%async_computation.3 | async-start | bytes 262144 | tf_op jit(solution)/shard_map/all_to_all | solution.py:354
  66.0 0.8 %shard_map.80 = bf16[512,128]{1,0:T(8,128)(2,1)} custom-call(bf16[16,24,512]{2,1,0:T(8,128)(2,1)S(1)} %all-to-all-done.1.got_ref), custom_call_target="tpu_custom_call" | custom-call | bytes 600000 | tf_op jit(solution)/shard_map/pallas_call | solution.py:19
  66.8 0.0 collective-permute-done.2.across_got
  66.8 0.0 collective-permute-done.3.inside_got
  66.8 1.1 %shard_map.81 = bf16[512,256]{1,0:T(8,128)(2,1)} custom-call(f32[2,8,64,128]{3,2,1,0:T(8,128)S(1)} %get-tuple-element.35.own_ref, bf16[8,64,128]{2,1,0:T(8,128)(2,1)S(1)} %collective-permute-done.2.across_got, bf16[8,64,128]{2,1,0:T(8,128)(2,1)S(1)} %collective-permute-done.3.inside_got), custom_call_target="tpu_custom_call" | custom-call | flops 1000000000 | bytes 2000000 | tf_op jit(solution)/shard_map/pallas_call | solution.py:19
  67.9 5.7 %all-to-all-done.3.got_ref = bf16[16,8,512]{2,1,0:T(8,128)(2,1)S(1)} async-done(((bf16[16,8,512]{2,1,0:T(8,128)(2,1)}), bf16[16,8,512]{2,1,0:T(8,128)(2,1)S(1)}, u32[]{:S(2)}, u32[]{:S(2)}) %all-to-all-start.3) | async-done | bytes 131104 | tf_op jit(solution)/shard_map/all_to_all | solution.py:354
  73.6 0.7 shard_map.84
Async XLA Ops:
  2.4 8.6 %copy-start = (bf16[1,32,2,8,256]{4,3,2,1,0:T(8,128)(2,1)S(1)}, bf16[1,32,2,8,256]{4,3,2,1,0:T(8,128)(2,1)}, u32[]{:S(2)}) copy-start(bf16[1,32,2,8,256]{4,3,2,1,0:T(8,128)(2,1)} %param.4) | copy-start | bytes 786436
  2.5 17.3 %all-to-all-start = ((bf16[16,8,1024]{2,1,0:T(8,128)(2,1)}), bf16[16,8,1024]{2,1,0:T(8,128)(2,1)S(1)}, u32[]{:S(2)}, u32[]{:S(2)}) async-start(bf16[16,8,1024]{2,1,0:T(8,128)(2,1)} %shard_map.75), calls=%async_computation | async-start | bytes 524288 | tf_op jit(solution)/shard_map/all_to_all | solution.py:313
  11.0 8.7 %copy-start.1 = (bf16[64,864]{1,0:T(8,128)(2,1)S(1)}, bf16[64,864]{1,0:T(8,128)(2,1)}, u32[]{:S(2)}) copy-start(bf16[64,864]{1,0:T(8,128)(2,1)} %weight_ref.5) | copy-start | bytes 331780
  11.5 5.3 %collective-permute-start.1 = (bf16[8,64,128]{2,1,0:T(8,128)(2,1)S(1)}, bf16[8,64,128]{2,1,0:T(8,128)(2,1)S(1)}, u32[]{:S(2)}, u32[]{:S(2)}) collective-permute-start(bf16[8,64,128]{2,1,0:T(8,128)(2,1)S(1)} %get-tuple-element.24.inside_own), channel_id=1, source_target_pairs={{0,1},{1,0},{2,3},{3,2},{4,5},{5,4},{6,7},{7,6},{8,9},{9,8},{10,11... | collective-permute-start | bytes 393224 | tf_op jit(solution)/shard_map/ppermute | solution.py:321
  11.7 10.3 %collective-permute-start = (bf16[8,64,128]{2,1,0:T(8,128)(2,1)S(1)}, bf16[8,64,128]{2,1,0:T(8,128)(2,1)S(1)}, u32[]{:S(2)}, u32[]{:S(2)}) collective-permute-start(bf16[8,64,128]{2,1,0:T(8,128)(2,1)S(1)} %get-tuple-element.23.across_own), channel_id=1, source_target_pairs={{1,2},{2,1},{3,4},{4,3},{5,6},{6,5},{7,8},{8,7},{9,10},{10,9},{11,... | collective-permute-start | bytes 393224 | tf_op jit(solution)/shard_map/ppermute | solution.py:320
  25.2 16.1 %all-to-all-start.1 = ((bf16[16,24,512]{2,1,0:T(8,128)(2,1)}), bf16[16,24,512]{2,1,0:T(8,128)(2,1)S(1)}, u32[]{:S(2)}, u32[]{:S(2)}) async-start(bf16[16,24,512]{2,1,0:T(8,128)(2,1)} %get-tuple-element.28), calls=%async_computation.1 | async-start | bytes 786432 | tf_op jit(solution)/shard_map/all_to_all | solution.py:335
  42.1 16.2 %all-to-all-start.2 = ((bf16[16,16,512]{2,1,0:T(8,128)(2,1)}), bf16[16,16,512]{2,1,0:T(8,128)(2,1)S(1)}, u32[]{:S(2)}, u32[]{:S(2)}) async-start(bf16[16,16,512]{2,1,0:T(8,128)(2,1)} %shard_map.82), calls=%async_computation.2 | async-start | bytes 524288 | tf_op jit(solution)/shard_map/all_to_all | solution.py:349
  50.4 16.4 %collective-permute-start.2 = (bf16[8,64,128]{2,1,0:T(8,128)(2,1)S(1)}, bf16[8,64,128]{2,1,0:T(8,128)(2,1)S(1)}, u32[]{:S(2)}, u32[]{:S(2)}) collective-permute-start(bf16[8,64,128]{2,1,0:T(8,128)(2,1)S(1)} %get-tuple-element.36), channel_id=1, source_target_pairs={{1,2},{2,1},{3,4},{4,3},{5,6},{6,5},{7,8},{8,7},{9,10},{10,9},{11,... | collective-permute-start | bytes 393224 | tf_op jit(solution)/shard_map/ppermute | solution.py:345
  54.8 12.0 %collective-permute-start.3 = (bf16[8,64,128]{2,1,0:T(8,128)(2,1)S(1)}, bf16[8,64,128]{2,1,0:T(8,128)(2,1)S(1)}, u32[]{:S(2)}, u32[]{:S(2)}) collective-permute-start(bf16[8,64,128]{2,1,0:T(8,128)(2,1)S(1)} %get-tuple-element.37), channel_id=1, source_target_pairs={{0,1},{1,0},{2,3},{3,2},{4,5},{5,4},{6,7},{7,6},{8,9},{9,8},{10,11... | collective-permute-start | bytes 393224 | tf_op jit(solution)/shard_map/ppermute | solution.py:346
  58.9 14.7 %all-to-all-start.3 = ((bf16[16,8,512]{2,1,0:T(8,128)(2,1)}), bf16[16,8,512]{2,1,0:T(8,128)(2,1)S(1)}, u32[]{:S(2)}, u32[]{:S(2)}) async-start(bf16[16,8,512]{2,1,0:T(8,128)(2,1)} %get-tuple-element.38), calls=%async_computation.3 | async-start | bytes 262144 | tf_op jit(solution)/shard_map/all_to_all | solution.py:354

commit v4 on v3

--- a/solution.py
+++ b/solution.py
@@ -11,6 +11,17 @@
 bf16 = jnp.bfloat16
 f32 = jnp.float32
 LANES = 128
+
+
+def rank_order(bits, reverse):
+    order = [sum(((rank >> k) & 1) << bit for k, bit in enumerate(bits)) for rank in range(16)]
+    return order[::-1] if reverse else order
+
+
+ORDER_IN = rank_order((1, 2, 3, 0), True)
+ORDER_SLABS = rank_order((1, 2, 3, 0), False)
+ORDER_SAMPLES = rank_order((3, 0, 1, 2), True)
+ORDER_OUT = rank_order((1, 2, 3, 0), True)
 VMEM_LIMIT = 16 * 1024 * 1024
 
 
@@ -57,10 +68,10 @@
         copy.wait()
     wide_ref[...] = cot_ref[...].astype(f32)
     weights = weight_ref[...]
-    for d in range(16):
+    for slot, d in enumerate(ORDER_IN):
         rows = [wide_ref[pl.ds(4 * d + r, 8, stride=64), :] for r in range(4)]
-        out_ref[d, :, 0:512] = jnp.concatenate(rows, axis=1).astype(bf16)
-        out_ref[d, :, 512:1024] = weights
+        out_ref[slot, :, 0:512] = jnp.concatenate(rows, axis=1).astype(bf16)
+        out_ref[slot, :, 512:1024] = weights
 
 
 def split_columns(own_ref, across_ref, inside_ref, flat_ref, planes_ref):
@@ -191,12 +202,12 @@
         if inset > 32:
             tiles[first + 1] = jnp.where(lane < inset - 32, moved, tiles[first + 1])
     conv = jnp.concatenate(tiles, axis=1)
-    for j in range(16):
-        rows, group, side = 8 * j, 8 * (j // 2), 512 * (j % 2)
+    for slot, j in enumerate(ORDER_SLABS):
+        rows, group, side = 8 * ORDER_IN.index(j), 8 * (j // 2), 512 * (j % 2)
         piece = jnp.concatenate(
             [out[rows : rows + 8], strided[rows : rows + 8], conv[group : group + 8, side : side + 512]], axis=0
         )
-        send_ref[j] = piece.astype(bf16)
+        send_ref[slot] = piece.astype(bf16)
 
 
 def back_weights(weight_ref):
@@ -264,9 +275,9 @@
 
 
 def place_output(got_ref, out_ref, wide_ref):
-    for d in range(16):
+    for slot, d in enumerate(ORDER_SLABS):
         for r in range(4):
-            wide_ref[pl.ds(4 * d + r, 8, stride=64), :] = got_ref[d, 0:8, LANES * r : LANES * r + LANES].astype(f32)
+            wide_ref[pl.ds(4 * d + r, 8, stride=64), :] = got_ref[slot, 0:8, LANES * r : LANES * r + LANES].astype(f32)
     out_ref[...] = wide_ref[...].astype(bf16)
 
 
@@ -281,10 +292,10 @@
 
 
 def place_conv(got_ref, out_ref):
-    for j in range(16):
+    for slot, j in enumerate(ORDER_OUT):
         rows, side = 8 * (j // 2), 512 * (j % 2)
         width = min(512, 864 - side)
-        out_ref[rows : rows + 8, side : side + width] = got_ref[j, :, :width].astype(f32)
+        out_ref[rows : rows + 8, side : side + width] = got_ref[slot, :, :width].astype(f32)
 
 
 def shards(volume, conv_weight, strided_weight, cotangent):
@@ -310,7 +321,7 @@
         *(pltpu.with_memory_space_constraint(x, pltpu.HBM) for x in (cotangent.reshape(512, LANES), strided_weight)),
         space=pltpu.HBM,
     )
-    got = lax.all_to_all(send, "space", 0, 0, tiled=True)
+    got = lax.all_to_all(send, "space", 0, 0, tiled=True, axis_index_groups=[ORDER_IN])
     cells_in, _ = lax.optimization_barrier((volume, send))
     across_vol, inside_vol = call(
         split_columns, (plane, plane),
@@ -332,7 +343,7 @@
         scratch + [pltpu.VMEM((LANES, 9 * LANES), f32)], 3_000_000_000, 3_000_000,
         across_got, across_vol, inside_vol, got, conv_weight, conv_terms, out_terms, strided_terms,
     )
-    got = lax.all_to_all(send, "space", 0, 0, tiled=True)
+    got = lax.all_to_all(send, "space", 0, 0, tiled=True, axis_index_groups=[ORDER_SLABS])
     own_terms, across_terms, inside_terms = call(
         back, (shape((2, 8, 64, LANES), f32), plane, plane),
         [pltpu.VMEM((2, 10, 256, LANES), bf16), pltpu.VMEM((2, 8, 64, LANES), bf16)],
@@ -346,12 +357,12 @@
     inside_got = lax.ppermute(inside_terms, "space", in_chip)
     send = call(sum_space, shape((16, 16, 512), bf16), [], 0, 600_000, got)
     output = call(place_output, shape((512, LANES), bf16), [pltpu.VMEM((512, LANES), f32)], 0, 600_000, got)
-    got = lax.all_to_all(send, "dp", 0, 0, tiled=True)
+    got = lax.all_to_all(send, "dp", 0, 0, tiled=True, axis_index_groups=[ORDER_SAMPLES])
     strided_grad, send = call(
         lambda *refs: sum_samples(1.0 / math.sqrt(cells / 8), 1.0 / math.sqrt(cells), *refs),
         (shape((8, 512), f32), shape((16, 8, 512), bf16)), [], 0, 600_000, got,
     )
-    got = lax.all_to_all(send, "space", 0, 0, tiled=True)
+    got = lax.all_to_all(send, "space", 0, 0, tiled=True, axis_index_groups=[ORDER_OUT])
     vol_grad = call(
         finish, shape((512, 256), bf16),
         [

time: 74.9 us -> 69.4 us (0.927)
  waiting for transfers between devices: 19.8 us -> 14.2 us
    all_to_all x4, waiting for transfers between devices: 19.7 us -> 11.7 us  [the longest x3 10.5 us: shards(): lax.all_to_all(send, 'space', 0, 0, tiled=True, axis_index_groups=[ORDER_...]
    ppermute x1, starting transfers between devices: 5.08 us -> 2.14 us  [shards(): across_got = lax.ppermute(across_vol, 'space', between_chips)]
    ppermute x1, waiting for transfers between devices: 0.01 us -> 2.58 us  [shards(): across_got = lax.ppermute(across_vol, 'space', between_chips)]
    all_to_all x4, starting transfers between devices: 30.1 us -> 32.1 us  [the longest x3 22.8 us: shards(): lax.all_to_all(send, 'space', 0, 0, tiled=True, axis_index_groups=[ORDER_...]
  transfers between devices with their start and end apart: 8 -> 8, of which waited for: 4 -> 5; matrix products, arithmetic and copies ran while one was open for 0% -> 0% of each run, Pallas kernels for 10% -> 11%
where the time goes in v4:
time: 69.4 us; the launch traced here: 68.7 us
  starting transfers between devices  39.7 us (57%)
  waiting for transfers between devices  14.2 us (20%)
  Pallas kernels  14 us (20%)
  between operations  0.71 us (1%)
    all_to_all x3, starting transfers between devices, shards(): lax.all_to_all(send, 'space', 0, 0, tiled=True, axis_index_groups=[ORDER_...  22.8 us
    pallas_call x10, Pallas kernels, call(): pl.pallas_call(kernel, out_shape=outs, in_specs=[pl.BlockSpec(memory_spac...  14 us
    all_to_all x3, waiting for transfers between devices, shards(): lax.all_to_all(send, 'space', 0, 0, tiled=True, axis_index_groups=[ORDER_...  10.5 us
    all_to_all x1, starting transfers between devices, shards(): lax.all_to_all(send, 'dp', 0, 0, tiled=True, axis_index_groups=[ORDER_SAM...  9.28 us
    ppermute x1, starting transfers between devices, shards(): across_got = lax.ppermute(across_terms, 'space', between_chips)  4.85 us
    ppermute x1, waiting for transfers between devices, shards(): across_got = lax.ppermute(across_vol, 'space', between_chips)  2.58 us
    ppermute x1, starting transfers between devices, shards(): across_got = lax.ppermute(across_vol, 'space', between_chips)  2.14 us
  transfers between devices with their start and end apart: 8, of which 5 were waited for; matrix products, arithmetic and copies ran while one was open for 0% of the time, Pallas kernels for 11%

profile of v4, /device:TPU:1, one launch (start us, length us, event | category | flops | bytes accessed | tf_op | source)
XLA Modules:
  0.0 68.7 jit_solution(17223230643191126428)
XLA Ops:
  0.6 1.8 %shard_map.75 = bf16[16,8,1024]{2,1,0:T(8,128)(2,1)} custom-call(bf16[512,128]{1,0:T(8,128)(2,1)} %bitcast.5, bf16[8,512]{1,0:T(8,128)(2,1)} %weight_hbm.1), custom_call_target="tpu_custom_call" | custom-call | bytes 400000 | tf_op jit(solution)/shard_map/pallas_call | solution.py:30
  2.4 0.0 copy-start
  2.5 9.6 %all-to-all-start = ((bf16[16,8,1024]{2,1,0:T(8,128)(2,1)}), bf16[16,8,1024]{2,1,0:T(8,128)(2,1)S(1)}, u32[]{:S(2)}, u32[]{:S(2)}) async-start(bf16[16,8,1024]{2,1,0:T(8,128)(2,1)} %shard_map.75), calls=%async_computation | async-start | bytes 524288 | tf_op jit(solution)/shard_map/all_to_all | solution.py:324
  12.1 0.0 copy-done
  12.1 0.0 copy-start.1
  12.1 0.4 shard_map.76
  12.5 0.5 collective-permute-start.1
  13.1 2.1 %collective-permute-start = (bf16[8,64,128]{2,1,0:T(8,128)(2,1)S(1)}, bf16[8,64,128]{2,1,0:T(8,128)(2,1)S(1)}, u32[]{:S(2)}, u32[]{:S(2)}) collective-permute-start(bf16[8,64,128]{2,1,0:T(8,128)(2,1)S(1)} %get-tuple-element.23.across_own), channel_id=1, source_target_pairs={{1,2},{2,1},{3,4},{4,3},{5,6},{6,5},{7,8},{8,7},{9,10},{10,9},{11,... | collective-permute-start | bytes 393224 | tf_op jit(solution)/shard_map/ppermute | solution.py:331
  15.2 0.0 collective-permute-done.1.inside_got
  15.2 1.8 %all-to-all-done.got_ref = bf16[16,8,1024]{2,1,0:T(8,128)(2,1)S(1)} async-done(((bf16[16,8,1024]{2,1,0:T(8,128)(2,1)}), bf16[16,8,1024]{2,1,0:T(8,128)(2,1)S(1)}, u32[]{:S(2)}, u32[]{:S(2)}) %all-to-all-start) | async-done | bytes 262176 | tf_op jit(solution)/shard_map/all_to_all | solution.py:324
  17.1 0.0 copy-done.1
  17.1 2.3 %shard_map.77 = (bf16[8,128,128]{2,1,0:T(8,128)(2,1)S(1)}, f32[128,1152]{1,0:T(8,128)S(1)}, f32[128,512]{1,0:T(8,128)S(1)}, f32[128,256]{1,0:T(8,128)S(1)}) custom-call(bf16[8,64,128]{2,1,0:T(8,128)(2,1)S(1)} %get-tuple-element.23.across_own, bf16[8,64,128]{2,1,0:T(8,128)(2,1)S(1)} %get-tuple-element.24.inside_own, ...), custom_call_target="tpu_custom_call" | custom-call | flops 3000000000 | bytes 2000000 | tf_op jit(solution)/shard_map/pallas_call | solution.py:30
  19.3 2.6 %collective-permute-done.across_got = bf16[8,64,128]{2,1,0:T(8,128)(2,1)S(1)} collective-permute-done((bf16[8,64,128]{2,1,0:T(8,128)(2,1)S(1)}, bf16[8,64,128]{2,1,0:T(8,128)(2,1)S(1)}, u32[]{:S(2)}, u32[]{:S(2)}) %collective-permute-start) | collective-permute-done | bytes 131104 | tf_op jit(solution)/shard_map/ppermute | solution.py:331
  21.9 3.2 %shard_map.78 = (bf16[16,24,512]{2,1,0:T(8,128)(2,1)}, bf16[8,128,128]{2,1,0:T(8,128)(2,1)S(1)}) custom-call(bf16[8,64,128]{2,1,0:T(8,128)(2,1)S(1)} %collective-permute-done.across_got, bf16[8,64,128]{2,1,0:T(8,128)(2,1)S(1)} %get-tuple-element.23.across_own, bf16[8,64,128]{2,1,0:T(8,128)(2,1)S(1)} %get-tuple-element.24.inside_own, ...), custom_call_target="tpu_custom_call" | custom-call | flops 3000000000 | bytes 3000000 | tf_op jit(solution)/shard_map/pallas_call | solution.py:30
  25.2 3.7 %all-to-all-start.1 = ((bf16[16,24,512]{2,1,0:T(8,128)(2,1)}), bf16[16,24,512]{2,1,0:T(8,128)(2,1)S(1)}, u32[]{:S(2)}, u32[]{:S(2)}) async-start(bf16[16,24,512]{2,1,0:T(8,128)(2,1)} %get-tuple-element.28), calls=%async_computation.1 | async-start | bytes 786432 | tf_op jit(solution)/shard_map/all_to_all | solution.py:346
  28.9 2.2 %shard_map.79 = (f32[2,8,64,128]{3,2,1,0:T(8,128)S(1)}, bf16[8,64,128]{2,1,0:T(8,128)(2,1)S(1)}, bf16[8,64,128]{2,1,0:T(8,128)(2,1)S(1)}) custom-call(bf16[8,128,128]{2,1,0:T(8,128)(2,1)S(1)} %get-tuple-element.29.across_own, bf16[8,128,128]{2,1,0:T(8,128)(2,1)S(1)} %get-tuple-element.30.inside_own, bf16[64,864]{1,0:T(8,128)(2,1)S(1)} %copy-done.1), custom_call_target="tpu_custom_call" | custom-call | flops 3000000000 | bytes 3000000 | tf_op jit(solution)/shard_map/pallas_call | solution.py:30
  31.0 7.0 %all-to-all-done.1.got_ref = bf16[16,24,512]{2,1,0:T(8,128)(2,1)S(1)} async-done(((bf16[16,24,512]{2,1,0:T(8,128)(2,1)}), bf16[16,24,512]{2,1,0:T(8,128)(2,1)S(1)}, u32[]{:S(2)}, u32[]{:S(2)}) %all-to-all-start.1) | async-done | bytes 393248 | tf_op jit(solution)/shard_map/all_to_all | solution.py:346
  38.0 0.8 %shard_map.82 = bf16[16,16,512]{2,1,0:T(8,128)(2,1)} custom-call(bf16[16,24,512]{2,1,0:T(8,128)(2,1)S(1)} %all-to-all-done.1.got_ref), custom_call_target="tpu_custom_call" | custom-call | bytes 600000 | tf_op jit(solution)/shard_map/pallas_call | solution.py:30
  38.8 9.3 %all-to-all-start.2 = ((bf16[16,16,512]{2,1,0:T(8,128)(2,1)}), bf16[16,16,512]{2,1,0:T(8,128)(2,1)S(1)}, u32[]{:S(2)}, u32[]{:S(2)}) async-start(bf16[16,16,512]{2,1,0:T(8,128)(2,1)} %shard_map.82), calls=%async_computation.2 | async-start | bytes 524288 | tf_op jit(solution)/shard_map/all_to_all | solution.py:360
  48.0 4.8 %collective-permute-start.2 = (bf16[8,64,128]{2,1,0:T(8,128)(2,1)S(1)}, bf16[8,64,128]{2,1,0:T(8,128)(2,1)S(1)}, u32[]{:S(2)}, u32[]{:S(2)}) collective-permute-start(bf16[8,64,128]{2,1,0:T(8,128)(2,1)S(1)} %get-tuple-element.36), channel_id=1, source_target_pairs={{1,2},{2,1},{3,4},{4,3},{5,6},{6,5},{7,8},{8,7},{9,10},{10,9},{11,... | collective-permute-start | bytes 393224 | tf_op jit(solution)/shard_map/ppermute | solution.py:356
  52.9 0.1 collective-permute-start.3
  53.0 1.1 %all-to-all-done.2.refs_0_ = bf16[16,16,512]{2,1,0:T(8,128)(2,1)S(1)} async-done(((bf16[16,16,512]{2,1,0:T(8,128)(2,1)}), bf16[16,16,512]{2,1,0:T(8,128)(2,1)S(1)}, u32[]{:S(2)}, u32[]{:S(2)}) %all-to-all-start.2) | async-done | bytes 262176 | tf_op jit(solution)/shard_map/all_to_all | solution.py:360
  54.1 0.7 %shard_map.83 = (f32[8,512]{1,0:T(8,128)}, bf16[16,8,512]{2,1,0:T(8,128)(2,1)}) custom-call(bf16[16,16,512]{2,1,0:T(8,128)(2,1)S(1)} %all-to-all-done.2.refs_0_), custom_call_target="tpu_custom_call" | custom-call | bytes 600000 | tf_op jit(solution)/shard_map/pallas_call | solution.py:30
  54.8 9.5 %all-to-all-start.3 = ((bf16[16,8,512]{2,1,0:T(8,128)(2,1)}), bf16[16,8,512]{2,1,0:T(8,128)(2,1)S(1)}, u32[]{:S(2)}, u32[]{:S(2)}) async-start(bf16[16,8,512]{2,1,0:T(8,128)(2,1)} %get-tuple-element.38), calls=%async_computation.3 | async-start | bytes 262144 | tf_op jit(solution)/shard_map/all_to_all | solution.py:365
  64.3 0.8 %shard_map.80 = bf16[512,128]{1,0:T(8,128)(2,1)} custom-call(bf16[16,24,512]{2,1,0:T(8,128)(2,1)S(1)} %all-to-all-done.1.got_ref), custom_call_target="tpu_custom_call" | custom-call | bytes 600000 | tf_op jit(solution)/shard_map/pallas_call | solution.py:30
  65.1 0.0 collective-permute-done.2.across_got
  65.1 0.0 collective-permute-done.3.inside_got
  65.1 1.1 %shard_map.81 = bf16[512,256]{1,0:T(8,128)(2,1)} custom-call(f32[2,8,64,128]{3,2,1,0:T(8,128)S(1)} %get-tuple-element.35.own_ref, bf16[8,64,128]{2,1,0:T(8,128)(2,1)S(1)} %collective-permute-done.2.across_got, bf16[8,64,128]{2,1,0:T(8,128)(2,1)S(1)} %collective-permute-done.3.inside_got), custom_call_target="tpu_custom_call" | custom-call | flops 1000000000 | bytes 2000000 | tf_op jit(solution)/shard_map/pallas_call | solution.py:30
  66.2 1.7 %all-to-all-done.3.got_ref = bf16[16,8,512]{2,1,0:T(8,128)(2,1)S(1)} async-done(((bf16[16,8,512]{2,1,0:T(8,128)(2,1)}), bf16[16,8,512]{2,1,0:T(8,128)(2,1)S(1)}, u32[]{:S(2)}, u32[]{:S(2)}) %all-to-all-start.3) | async-done | bytes 131104 | tf_op jit(solution)/shard_map/all_to_all | solution.py:365
  68.0 0.7 %shard_map.84 = f32[64,864]{1,0:T(8,128)} custom-call(bf16[16,8,512]{2,1,0:T(8,128)(2,1)S(1)} %all-to-all-done.3.got_ref), custom_call_target="tpu_custom_call" | custom-call | bytes 300000 | tf_op jit(solution)/shard_map/pallas_call | solution.py:30
Async XLA Ops:
  2.4 9.7 %copy-start = (bf16[1,32,2,8,256]{4,3,2,1,0:T(8,128)(2,1)S(1)}, bf16[1,32,2,8,256]{4,3,2,1,0:T(8,128)(2,1)}, u32[]{:S(2)}) copy-start(bf16[1,32,2,8,256]{4,3,2,1,0:T(8,128)(2,1)} %param.4) | copy-start | bytes 786436
  2.5 14.6 %all-to-all-start = ((bf16[16,8,1024]{2,1,0:T(8,128)(2,1)}), bf16[16,8,1024]{2,1,0:T(8,128)(2,1)S(1)}, u32[]{:S(2)}, u32[]{:S(2)}) async-start(bf16[16,8,1024]{2,1,0:T(8,128)(2,1)} %shard_map.75), calls=%async_computation | async-start | bytes 524288 | tf_op jit(solution)/shard_map/all_to_all | solution.py:324
  12.1 5.0 %copy-start.1 = (bf16[64,864]{1,0:T(8,128)(2,1)S(1)}, bf16[64,864]{1,0:T(8,128)(2,1)}, u32[]{:S(2)}) copy-start(bf16[64,864]{1,0:T(8,128)(2,1)} %weight_ref.5) | copy-start | bytes 331780
  12.5 2.7 %collective-permute-start.1 = (bf16[8,64,128]{2,1,0:T(8,128)(2,1)S(1)}, bf16[8,64,128]{2,1,0:T(8,128)(2,1)S(1)}, u32[]{:S(2)}, u32[]{:S(2)}) collective-permute-start(bf16[8,64,128]{2,1,0:T(8,128)(2,1)S(1)} %get-tuple-element.24.inside_own), channel_id=1, source_target_pairs={{0,1},{1,0},{2,3},{3,2},{4,5},{5,4},{6,7},{7,6},{8,9},{9,8},{10,11... | collective-permute-start | bytes 393224 | tf_op jit(solution)/shard_map/ppermute | solution.py:332
  13.1 8.9 %collective-permute-start = (bf16[8,64,128]{2,1,0:T(8,128)(2,1)S(1)}, bf16[8,64,128]{2,1,0:T(8,128)(2,1)S(1)}, u32[]{:S(2)}, u32[]{:S(2)}) collective-permute-start(bf16[8,64,128]{2,1,0:T(8,128)(2,1)S(1)} %get-tuple-element.23.across_own), channel_id=1, source_target_pairs={{1,2},{2,1},{3,4},{4,3},{5,6},{6,5},{7,8},{8,7},{9,10},{10,9},{11,... | collective-permute-start | bytes 393224 | tf_op jit(solution)/shard_map/ppermute | solution.py:331
  25.2 12.8 %all-to-all-start.1 = ((bf16[16,24,512]{2,1,0:T(8,128)(2,1)}), bf16[16,24,512]{2,1,0:T(8,128)(2,1)S(1)}, u32[]{:S(2)}, u32[]{:S(2)}) async-start(bf16[16,24,512]{2,1,0:T(8,128)(2,1)} %get-tuple-element.28), calls=%async_computation.1 | async-start | bytes 786432 | tf_op jit(solution)/shard_map/all_to_all | solution.py:346
  38.8 15.4 %all-to-all-start.2 = ((bf16[16,16,512]{2,1,0:T(8,128)(2,1)}), bf16[16,16,512]{2,1,0:T(8,128)(2,1)S(1)}, u32[]{:S(2)}, u32[]{:S(2)}) async-start(bf16[16,16,512]{2,1,0:T(8,128)(2,1)} %shard_map.82), calls=%async_computation.2 | async-start | bytes 524288 | tf_op jit(solution)/shard_map/all_to_all | solution.py:360
  48.0 17.1 %collective-permute-start.2 = (bf16[8,64,128]{2,1,0:T(8,128)(2,1)S(1)}, bf16[8,64,128]{2,1,0:T(8,128)(2,1)S(1)}, u32[]{:S(2)}, u32[]{:S(2)}) collective-permute-start(bf16[8,64,128]{2,1,0:T(8,128)(2,1)S(1)} %get-tuple-element.36), channel_id=1, source_target_pairs={{1,2},{2,1},{3,4},{4,3},{5,6},{6,5},{7,8},{8,7},{9,10},{10,9},{11,... | collective-permute-start | bytes 393224 | tf_op jit(solution)/shard_map/ppermute | solution.py:356
  52.9 12.2 %collective-permute-start.3 = (bf16[8,64,128]{2,1,0:T(8,128)(2,1)S(1)}, bf16[8,64,128]{2,1,0:T(8,128)(2,1)S(1)}, u32[]{:S(2)}, u32[]{:S(2)}) collective-permute-start(bf16[8,64,128]{2,1,0:T(8,128)(2,1)S(1)} %get-tuple-element.37), channel_id=1, source_target_pairs={{0,1},{1,0},{2,3},{3,2},{4,5},{5,4},{6,7},{7,6},{8,9},{9,8},{10,11... | collective-permute-start | bytes 393224 | tf_op jit(solution)/shard_map/ppermute | solution.py:357
  54.8 13.1 %all-to-all-start.3 = ((bf16[16,8,512]{2,1,0:T(8,128)(2,1)}), bf16[16,8,512]{2,1,0:T(8,128)(2,1)S(1)}, u32[]{:S(2)}, u32[]{:S(2)}) async-start(bf16[16,8,512]{2,1,0:T(8,128)(2,1)} %get-tuple-element.38), calls=%async_computation.3 | async-start | bytes 262144 | tf_op jit(solution)/shard_map/all_to_all | solution.py:365

commit v5 on v4

--- a/solution.py
+++ b/solution.py
@@ -1,3 +1,4 @@
+import functools
 import math
 
 import jax
@@ -130,15 +131,10 @@
     )
 
 
-def one_plane(z, planes, got_ref, weight_ref, taps_ref, grad_ref, block_ref, grad_plane_ref, conv_ref):
-    fill_taps(taps_ref, planes)
-    cot = got_ref[:, :, 0:512].reshape(128, 512)
-    filters = got_ref[:, :, pl.ds(pl.multiple_of(512 + 256 * z, 256), 256)].reshape(128, 256)
-    grad_ref[...] = jnp.dot(filters.astype(f32).T.astype(bf16), cot, preferred_element_type=f32)
-    weights = tap_weights(weight_ref)
+def one_plane(preactivation, got_ref, taps_ref, grad_ref, block_ref, grad_plane_ref, conv_ref, z):
     for pair in range(4):
         around = surroundings(taps_ref, range(3), pair)
-        pre = jnp.dot(weights, around, preferred_element_type=f32)
+        pre = preactivation(pair, around)
         square = pre * pre
         inner = root_two_pi * pre * (1.0 + 0.044715 * square)
         hyper = jnp.tanh(inner)
@@ -161,28 +157,48 @@
         else:
             conv_ref[...] += part
     blocks = block_ref[...]
+    cot = got_ref[:, :, 0:512].reshape(128, 512)
+    filters = got_ref[:, :, pl.ds(pl.multiple_of(512 + 256 * z, 256), 256)].reshape(128, 256)
     out = jnp.dot(filters, blocks, preferred_element_type=f32)
     strided = lax.dot_general(cot, blocks, (((1,), (1,)), ((), ())), preferred_element_type=f32)
     return out, strided
 
 
-def inside(across_own, inside_own, inside_got, got_ref, weight_ref, grad_plane_ref, conv_ref, out_ref, strided_ref,
+def inside(across_own, inside_own, inside_got, got_ref, weight_ref,
+           grad_plane_ref, conv_ref, out_ref, strided_ref, across_grad_ref, across_pre_ref,
            taps_ref, grad_ref, block_ref):
     core = core_index()
+    fill_taps(taps_ref, ((2 * core, across_own), (1, inside_own), (2 - 2 * core, inside_got)))
+    cot = got_ref[:, :, 0:512].reshape(128, 512)
+    for z, ref in ((1 - core, grad_ref), (core, across_grad_ref)):
+        filters = got_ref[:, :, pl.ds(pl.multiple_of(512 + 256 * z, 256), 256)].reshape(128, 256)
+        ref[...] = jnp.dot(filters.astype(f32).T.astype(bf16), cot, preferred_element_type=f32)
+    weights = tap_weights(weight_ref)
     out, strided = one_plane(
-        1 - core, ((2 * core, across_own), (1, inside_own), (2 - 2 * core, inside_got)),
-        got_ref, weight_ref, taps_ref, grad_ref, block_ref, grad_plane_ref, conv_ref,
+        lambda pair, around: jnp.dot(weights, around, preferred_element_type=f32),
+        got_ref, taps_ref, grad_ref, block_ref, grad_plane_ref, conv_ref, 1 - core,
     )
     out_ref[...] = out
     strided_ref[...] = strided
-
-
-def across(across_got, across_own, inside_own, got_ref, weight_ref, conv_in, out_in, strided_in, send_ref, grad_plane_ref,
-           taps_ref, grad_ref, block_ref, conv_ref):
+    weights = jnp.where(core == 0, weights[:, 384:], weights[:, :768])
+    for pair in range(4):
+        around = surroundings(taps_ref, (core, core + 1), pair)
+        across_pre_ref[pair] = jnp.dot(weights, around, preferred_element_type=f32)
+
+
+def across(across_got, across_own, inside_own, got_ref, weight_ref, conv_in, out_in, strided_in, grad_ref, pre_ref,
+           send_ref, grad_plane_ref, taps_ref, block_ref, conv_ref):
     core = core_index()
+    fill_taps(taps_ref, ((2 * core, across_got), (1, across_own), (2 - 2 * core, inside_own)))
+    weights = tap_weights(weight_ref)
+    weights = jnp.where(core == 0, weights[:, :384], weights[:, 768:])
+
+    def preactivation(pair, around):
+        edge = surroundings(taps_ref, (2 * core,), pair)
+        return pre_ref[pair] + jnp.dot(weights, edge, preferred_element_type=f32)
+
     out, strided = one_plane(
-        core, ((2 * core, across_got), (1, across_own), (2 - 2 * core, inside_own)),
-        got_ref, weight_ref, taps_ref, grad_ref, block_ref, grad_plane_ref, conv_ref,
+        preactivation, got_ref, taps_ref, grad_ref, block_ref, grad_plane_ref, conv_ref, core
     )
     out = out + out_in[...]
     other = strided_in[...]
@@ -266,10 +282,7 @@
 
 
 def sum_space(got_ref, send_ref):
-    total = got_ref[0, 8:24, :].astype(f32)
-    for j in range(1, 16):
-        total = total + got_ref[j, 8:24, :].astype(f32)
-    total = total.astype(bf16)
+    total = summed(got_ref, slice(8, 24)).astype(bf16)
     for j in range(16):
         send_ref[j] = total
 
@@ -281,14 +294,21 @@
     out_ref[...] = wide_ref[...].astype(bf16)
 
 
-def sum_samples(strided_scale, conv_scale, got_ref, strided_ref, send_ref):
-    total = got_ref[0].astype(f32)
+def summed(got_ref, rows):
+    total = got_ref[0, rows, :].astype(f32)
     for j in range(1, 16):
-        total = total + got_ref[j].astype(f32)
-    strided_ref[...] = total[:8] * strided_scale
-    conv = (total[8:] * conv_scale).astype(bf16)
+        total = total + got_ref[j, rows, :].astype(f32)
+    return total
+
+
+def sum_conv(scale, got_ref, send_ref):
+    conv = (summed(got_ref, slice(8, 16)) * scale).astype(bf16)
     for j in range(16):
         send_ref[j] = conv
+
+
+def sum_strided(scale, got_ref, strided_ref):
+    strided_ref[...] = summed(got_ref, slice(0, 8)) * scale
 
 
 def place_conv(got_ref, out_ref):
@@ -308,9 +328,12 @@
     def shape(dims, dtype):
         return jax.ShapeDtypeStruct(dims, dtype)
 
+    def buffer(*dims):
+        return pltpu.VMEM(dims, bf16)
+
     plane = shape((8, 64, LANES), bf16)
     send = call(
-        send_first, shape((16, 8, 1024), bf16),
+        send_first, buffer(16, 8, 1024),
         [
             pltpu.VMEM((512, LANES), bf16),
             pltpu.VMEM((8, 512), bf16),
@@ -331,17 +354,22 @@
     across_got = lax.ppermute(across_vol, "space", between_chips)
     inside_got = lax.ppermute(inside_vol, "space", in_chip)
     grad_plane = shape((8, LANES, LANES), bf16)
-    scratch = [pltpu.VMEM((3, 10, LANES, LANES), bf16), pltpu.VMEM((256, 512), f32), pltpu.VMEM((256, 512), bf16)]
-    inside_grad, conv_terms, out_terms, strided_terms = call(
+    taps = pltpu.VMEM((3, 10, LANES, LANES), bf16)
+    blocks = pltpu.VMEM((256, 512), bf16)
+    conv_part = (LANES, 9 * LANES)
+    inside_grad, *terms = call(
         inside,
-        (grad_plane, shape((LANES, 9 * LANES), f32), shape((LANES, 512), f32), shape((LANES, 256), f32)),
-        scratch, 3_000_000_000, 2_000_000,
+        (
+            grad_plane, shape(conv_part, f32), shape((LANES, 512), f32), shape((LANES, 256), f32),
+            shape((256, 512), f32), shape((4, LANES, 256), f32),
+        ),
+        [taps, pltpu.VMEM((256, 512), f32), blocks], 3_000_000_000, 2_000_000,
         across_vol, inside_vol, inside_got, got, conv_weight,
     )
     send, across_grad = call(
-        across, (shape((16, 24, 512), bf16), grad_plane),
-        scratch + [pltpu.VMEM((LANES, 9 * LANES), f32)], 3_000_000_000, 3_000_000,
-        across_got, across_vol, inside_vol, got, conv_weight, conv_terms, out_terms, strided_terms,
+        across, (buffer(16, 24, 512), grad_plane),
+        [taps, blocks, pltpu.VMEM(conv_part, f32)], 3_000_000_000, 3_000_000,
+        across_got, across_vol, inside_vol, got, conv_weight, *terms,
     )
     got = lax.all_to_all(send, "space", 0, 0, tiled=True, axis_index_groups=[ORDER_SLABS])
     own_terms, across_terms, inside_terms = call(
@@ -355,12 +383,14 @@
     )
     across_got = lax.ppermute(across_terms, "space", between_chips)
     inside_got = lax.ppermute(inside_terms, "space", in_chip)
-    send = call(sum_space, shape((16, 16, 512), bf16), [], 0, 600_000, got)
+    send = call(sum_space, buffer(16, 16, 512), [], 0, 600_000, got)
     output = call(place_output, shape((512, LANES), bf16), [pltpu.VMEM((512, LANES), f32)], 0, 600_000, got)
     got = lax.all_to_all(send, "dp", 0, 0, tiled=True, axis_index_groups=[ORDER_SAMPLES])
-    strided_grad, send = call(
-        lambda *refs: sum_samples(1.0 / math.sqrt(cells / 8), 1.0 / math.sqrt(cells), *refs),
-        (shape((8, 512), f32), shape((16, 8, 512), bf16)), [], 0, 600_000, got,
+    send = call(
+        functools.partial(sum_conv, 1.0 / math.sqrt(cells)), buffer(16, 8, 512), [], 0, 300_000, got,
+    )
+    strided_grad = call(
+        functools.partial(sum_strided, 1.0 / math.sqrt(cells / 8)), shape((8, 512), f32), [], 0, 300_000, got,
     )
     got = lax.all_to_all(send, "space", 0, 0, tiled=True, axis_index_groups=[ORDER_OUT])
     vol_grad = call(

time: 69.4 us -> 69.1 us (level)
  waiting for transfers between devices: 14.2 us -> 13.2 us
    pallas_call x10 -> x11, Pallas kernels: 14 us -> 14.4 us  [call(): pl.pallas_call(kernel, out_shape=outs, in_specs=[pl.BlockSpec(memory_spac...]
  transfers between devices with their start and end apart: 8 -> 8, of which waited for: 5 -> 5; matrix products, arithmetic and copies ran while one was open for 0% -> 0% of each run, Pallas kernels for 11% -> 12%
where the time goes in v5:
time: 69.1 us; the launch traced here: 68.4 us
  starting transfers between devices  40.1 us (58%)
  Pallas kernels  14.4 us (21%)
  waiting for transfers between devices  13.2 us (19%)
  between operations  0.72 us (1%)
    all_to_all x3, starting transfers between devices, shards(): lax.all_to_all(send, 'space', 0, 0, tiled=True, axis_index_groups=[ORDER_...  23.2 us
    pallas_call x11, Pallas kernels, call(): pl.pallas_call(kernel, out_shape=outs, in_specs=[pl.BlockSpec(memory_spac...  14.4 us
    all_to_all x3, waiting for transfers between devices, shards(): lax.all_to_all(send, 'space', 0, 0, tiled=True, axis_index_groups=[ORDER_...  9.89 us
    all_to_all x1, starting transfers between devices, shards(): lax.all_to_all(send, 'dp', 0, 0, tiled=True, axis_index_groups=[ORDER_SAM...  9.28 us
    ppermute x1, starting transfers between devices, shards(): across_got = lax.ppermute(across_terms, 'space', between_chips)  4.85 us
    ppermute x1, waiting for transfers between devices, shards(): across_got = lax.ppermute(across_vol, 'space', between_chips)  2.2 us
    ppermute x1, starting transfers between devices, shards(): across_got = lax.ppermute(across_vol, 'space', between_chips)  2.14 us
  transfers between devices with their start and end apart: 8, of which 5 were waited for; matrix products, arithmetic and copies ran while one was open for 0% of the time, Pallas kernels for 12%

profile of v5, /device:TPU:1, one launch (start us, length us, event | category | flops | bytes accessed | tf_op | source)
XLA Modules:
  0.0 68.4 jit_solution(5496485163688193003)
XLA Ops:
  0.6 1.8 %shard_map.75 = bf16[16,8,1024]{2,1,0:T(8,128)(2,1)} custom-call(bf16[512,128]{1,0:T(8,128)(2,1)} %bitcast.5, bf16[8,512]{1,0:T(8,128)(2,1)} %weight_hbm.1), custom_call_target="tpu_custom_call" | custom-call | bytes 400000 | tf_op jit(solution)/shard_map/pallas_call | solution.py:31
  2.4 0.0 copy-start
  2.5 9.6 %all-to-all-start = ((bf16[16,8,1024]{2,1,0:T(8,128)(2,1)}), bf16[16,8,1024]{2,1,0:T(8,128)(2,1)S(1)}, u32[]{:S(2)}, u32[]{:S(2)}) async-start(bf16[16,8,1024]{2,1,0:T(8,128)(2,1)} %shard_map.75), calls=%async_computation | async-start | bytes 524288 | tf_op jit(solution)/shard_map/all_to_all | solution.py:347
  12.1 0.0 copy-done
  12.1 0.0 copy-start.1
  12.1 0.4 shard_map.76
  12.5 0.5 collective-permute-start.1
  13.1 2.1 %collective-permute-start = (bf16[8,64,128]{2,1,0:T(8,128)(2,1)S(1)}, bf16[8,64,128]{2,1,0:T(8,128)(2,1)S(1)}, u32[]{:S(2)}, u32[]{:S(2)}) collective-permute-start(bf16[8,64,128]{2,1,0:T(8,128)(2,1)S(1)} %get-tuple-element.23.across_own), channel_id=1, source_target_pairs={{1,2},{2,1},{3,4},{4,3},{5,6},{6,5},{7,8},{8,7},{9,10},{10,9},{11,... | collective-permute-start | bytes 393224 | tf_op jit(solution)/shard_map/ppermute | solution.py:354
  15.2 0.0 collective-permute-done.1.inside_got
  15.2 1.8 %all-to-all-done.got_ref = bf16[16,8,1024]{2,1,0:T(8,128)(2,1)S(1)} async-done(((bf16[16,8,1024]{2,1,0:T(8,128)(2,1)}), bf16[16,8,1024]{2,1,0:T(8,128)(2,1)S(1)}, u32[]{:S(2)}, u32[]{:S(2)}) %all-to-all-start) | async-done | bytes 262176 | tf_op jit(solution)/shard_map/all_to_all | solution.py:347
  17.1 0.0 copy-done.1
  17.1 2.7 %shard_map.77 = (bf16[8,128,128]{2,1,0:T(8,128)(2,1)S(1)}, f32[128,1152]{1,0:T(8,128)S(1)}, f32[128,512]{1,0:T(8,128)S(1)}, f32[128,256]{1,0:T(8,128)S(1)}, f32[...) custom-call(bf16[8,64,128]{2,1,0:T(8,128)(2,1)S(1)} %get-tuple-element.23.across_own, ...), custom_call_target="tpu_custom_call" | custom-call | flops 3000000000 | bytes 2000000 | tf_op jit(solution)/shard_map/pallas_call | solution.py:31
  19.7 2.2 %collective-permute-done.across_got = bf16[8,64,128]{2,1,0:T(8,128)(2,1)S(1)} collective-permute-done((bf16[8,64,128]{2,1,0:T(8,128)(2,1)S(1)}, bf16[8,64,128]{2,1,0:T(8,128)(2,1)S(1)}, u32[]{:S(2)}, u32[]{:S(2)}) %collective-permute-start) | collective-permute-done | bytes 131104 | tf_op jit(solution)/shard_map/ppermute | solution.py:354
  21.9 2.6 %shard_map.78 = (bf16[16,24,512]{2,1,0:T(8,128)(2,1)}, bf16[8,128,128]{2,1,0:T(8,128)(2,1)S(1)}) custom-call(bf16[8,64,128]{2,1,0:T(8,128)(2,1)S(1)} %collective-permute-done.across_got, bf16[8,64,128]{2,1,0:T(8,128)(2,1)S(1)} %get-tuple-element.23.across_own, bf16[8,64,128]{2,1,0:T(8,128)(2,1)S(1)} %get-tuple-element.24.inside_own, ...), custom_call_target="tpu_custom_call" | custom-call | flops 3000000000 | bytes 3000000 | tf_op jit(solution)/shard_map/pallas_call | solution.py:31
  24.5 4.1 %all-to-all-start.1 = ((bf16[16,24,512]{2,1,0:T(8,128)(2,1)}), bf16[16,24,512]{2,1,0:T(8,128)(2,1)S(1)}, u32[]{:S(2)}, u32[]{:S(2)}) async-start(bf16[16,24,512]{2,1,0:T(8,128)(2,1)} %get-tuple-element.30), calls=%async_computation.1 | async-start | bytes 786432 | tf_op jit(solution)/shard_map/all_to_all | solution.py:374
  28.6 2.2 %shard_map.79 = (f32[2,8,64,128]{3,2,1,0:T(8,128)S(1)}, bf16[8,64,128]{2,1,0:T(8,128)(2,1)S(1)}, bf16[8,64,128]{2,1,0:T(8,128)(2,1)S(1)}) custom-call(bf16[8,128,128]{2,1,0:T(8,128)(2,1)S(1)} %get-tuple-element.31.across_own, bf16[8,128,128]{2,1,0:T(8,128)(2,1)S(1)} %get-tuple-element.32.inside_own, bf16[64,864]{1,0:T(8,128)(2,1)S(1)} %copy-done.1), custom_call_target="tpu_custom_call" | custom-call | flops 3000000000 | bytes 3000000 | tf_op jit(solution)/shard_map/pallas_call | solution.py:31
  30.8 7.0 %all-to-all-done.1.got_ref = bf16[16,24,512]{2,1,0:T(8,128)(2,1)S(1)} async-done(((bf16[16,24,512]{2,1,0:T(8,128)(2,1)}), bf16[16,24,512]{2,1,0:T(8,128)(2,1)S(1)}, u32[]{:S(2)}, u32[]{:S(2)}) %all-to-all-start.1) | async-done | bytes 393248 | tf_op jit(solution)/shard_map/all_to_all | solution.py:374
  37.8 0.8 %shard_map.82 = bf16[16,16,512]{2,1,0:T(8,128)(2,1)} custom-call(bf16[16,24,512]{2,1,0:T(8,128)(2,1)S(1)} %all-to-all-done.1.got_ref), custom_call_target="tpu_custom_call" | custom-call | bytes 600000 | tf_op jit(solution)/shard_map/pallas_call | solution.py:31
  38.5 9.3 %all-to-all-start.2 = ((bf16[16,16,512]{2,1,0:T(8,128)(2,1)}), bf16[16,16,512]{2,1,0:T(8,128)(2,1)S(1)}, u32[]{:S(2)}, u32[]{:S(2)}) async-start(bf16[16,16,512]{2,1,0:T(8,128)(2,1)} %shard_map.82), calls=%async_computation.2 | async-start | bytes 524288 | tf_op jit(solution)/shard_map/all_to_all | solution.py:388
  47.8 4.9 %collective-permute-start.2 = (bf16[8,64,128]{2,1,0:T(8,128)(2,1)S(1)}, bf16[8,64,128]{2,1,0:T(8,128)(2,1)S(1)}, u32[]{:S(2)}, u32[]{:S(2)}) collective-permute-start(bf16[8,64,128]{2,1,0:T(8,128)(2,1)S(1)} %get-tuple-element.38), channel_id=1, source_target_pairs={{1,2},{2,1},{3,4},{4,3},{5,6},{6,5},{7,8},{8,7},{9,10},{10,9},{11,... | collective-permute-start | bytes 393224 | tf_op jit(solution)/shard_map/ppermute | solution.py:384
  52.7 0.1 collective-permute-start.3
  52.8 1.1 %all-to-all-done.2.got_ref = bf16[16,16,512]{2,1,0:T(8,128)(2,1)S(1)} async-done(((bf16[16,16,512]{2,1,0:T(8,128)(2,1)}), bf16[16,16,512]{2,1,0:T(8,128)(2,1)S(1)}, u32[]{:S(2)}, u32[]{:S(2)}) %all-to-all-start.2) | async-done | bytes 262176 | tf_op jit(solution)/shard_map/all_to_all | solution.py:388
  53.9 0.7 shard_map.83
  54.6 9.5 %all-to-all-start.3 = ((bf16[16,8,512]{2,1,0:T(8,128)(2,1)}), bf16[16,8,512]{2,1,0:T(8,128)(2,1)S(1)}, u32[]{:S(2)}, u32[]{:S(2)}) async-start(bf16[16,8,512]{2,1,0:T(8,128)(2,1)} %shard_map.83), calls=%async_computation.3 | async-start | bytes 262144 | tf_op jit(solution)/shard_map/all_to_all | solution.py:395
  64.0 0.8 %shard_map.80 = bf16[512,128]{1,0:T(8,128)(2,1)} custom-call(bf16[16,24,512]{2,1,0:T(8,128)(2,1)S(1)} %all-to-all-done.1.got_ref), custom_call_target="tpu_custom_call" | custom-call | bytes 600000 | tf_op jit(solution)/shard_map/pallas_call | solution.py:31
  64.9 0.0 collective-permute-done.2.across_got
  64.9 0.0 collective-permute-done.3.inside_got
  64.9 1.1 %shard_map.81 = bf16[512,256]{1,0:T(8,128)(2,1)} custom-call(f32[2,8,64,128]{3,2,1,0:T(8,128)S(1)} %get-tuple-element.37.own_ref, bf16[8,64,128]{2,1,0:T(8,128)(2,1)S(1)} %collective-permute-done.2.across_got, bf16[8,64,128]{2,1,0:T(8,128)(2,1)S(1)} %collective-permute-done.3.inside_got), custom_call_target="tpu_custom_call" | custom-call | flops 1000000000 | bytes 2000000 | tf_op jit(solution)/shard_map/pallas_call | solution.py:31
  66.0 0.6 shard_map.85
  66.6 1.1 %all-to-all-done.3.got_ref = bf16[16,8,512]{2,1,0:T(8,128)(2,1)S(1)} async-done(((bf16[16,8,512]{2,1,0:T(8,128)(2,1)}), bf16[16,8,512]{2,1,0:T(8,128)(2,1)S(1)}, u32[]{:S(2)}, u32[]{:S(2)}) %all-to-all-start.3) | async-done | bytes 131104 | tf_op jit(solution)/shard_map/all_to_all | solution.py:395
  67.7 0.7 %shard_map.84 = f32[64,864]{1,0:T(8,128)} custom-call(bf16[16,8,512]{2,1,0:T(8,128)(2,1)S(1)} %all-to-all-done.3.got_ref), custom_call_target="tpu_custom_call" | custom-call | bytes 300000 | tf_op jit(solution)/shard_map/pallas_call | solution.py:31
Async XLA Ops:
  2.4 9.7 %copy-start = (bf16[1,32,2,8,256]{4,3,2,1,0:T(8,128)(2,1)S(1)}, bf16[1,32,2,8,256]{4,3,2,1,0:T(8,128)(2,1)}, u32[]{:S(2)}) copy-start(bf16[1,32,2,8,256]{4,3,2,1,0:T(8,128)(2,1)} %param.4) | copy-start | bytes 786436
  2.5 14.6 %all-to-all-start = ((bf16[16,8,1024]{2,1,0:T(8,128)(2,1)}), bf16[16,8,1024]{2,1,0:T(8,128)(2,1)S(1)}, u32[]{:S(2)}, u32[]{:S(2)}) async-start(bf16[16,8,1024]{2,1,0:T(8,128)(2,1)} %shard_map.75), calls=%async_computation | async-start | bytes 524288 | tf_op jit(solution)/shard_map/all_to_all | solution.py:347
  12.1 5.0 %copy-start.1 = (bf16[64,864]{1,0:T(8,128)(2,1)S(1)}, bf16[64,864]{1,0:T(8,128)(2,1)}, u32[]{:S(2)}) copy-start(bf16[64,864]{1,0:T(8,128)(2,1)} %weight_ref.5) | copy-start | bytes 331780
  12.5 2.7 %collective-permute-start.1 = (bf16[8,64,128]{2,1,0:T(8,128)(2,1)S(1)}, bf16[8,64,128]{2,1,0:T(8,128)(2,1)S(1)}, u32[]{:S(2)}, u32[]{:S(2)}) collective-permute-start(bf16[8,64,128]{2,1,0:T(8,128)(2,1)S(1)} %get-tuple-element.24.inside_own), channel_id=1, source_target_pairs={{0,1},{1,0},{2,3},{3,2},{4,5},{5,4},{6,7},{7,6},{8,9},{9,8},{10,11... | collective-permute-start | bytes 393224 | tf_op jit(solution)/shard_map/ppermute | solution.py:355
  13.1 8.9 %collective-permute-start = (bf16[8,64,128]{2,1,0:T(8,128)(2,1)S(1)}, bf16[8,64,128]{2,1,0:T(8,128)(2,1)S(1)}, u32[]{:S(2)}, u32[]{:S(2)}) collective-permute-start(bf16[8,64,128]{2,1,0:T(8,128)(2,1)S(1)} %get-tuple-element.23.across_own), channel_id=1, source_target_pairs={{1,2},{2,1},{3,4},{4,3},{5,6},{6,5},{7,8},{8,7},{9,10},{10,9},{11,... | collective-permute-start | bytes 393224 | tf_op jit(solution)/shard_map/ppermute | solution.py:354
  24.5 13.2 %all-to-all-start.1 = ((bf16[16,24,512]{2,1,0:T(8,128)(2,1)}), bf16[16,24,512]{2,1,0:T(8,128)(2,1)S(1)}, u32[]{:S(2)}, u32[]{:S(2)}) async-start(bf16[16,24,512]{2,1,0:T(8,128)(2,1)} %get-tuple-element.30), calls=%async_computation.1 | async-start | bytes 786432 | tf_op jit(solution)/shard_map/all_to_all | solution.py:374
  38.5 15.4 %all-to-all-start.2 = ((bf16[16,16,512]{2,1,0:T(8,128)(2,1)}), bf16[16,16,512]{2,1,0:T(8,128)(2,1)S(1)}, u32[]{:S(2)}, u32[]{:S(2)}) async-start(bf16[16,16,512]{2,1,0:T(8,128)(2,1)} %shard_map.82), calls=%async_computation.2 | async-start | bytes 524288 | tf_op jit(solution)/shard_map/all_to_all | solution.py:388
  47.8 17.1 %collective-permute-start.2 = (bf16[8,64,128]{2,1,0:T(8,128)(2,1)S(1)}, bf16[8,64,128]{2,1,0:T(8,128)(2,1)S(1)}, u32[]{:S(2)}, u32[]{:S(2)}) collective-permute-start(bf16[8,64,128]{2,1,0:T(8,128)(2,1)S(1)} %get-tuple-element.38), channel_id=1, source_target_pairs={{1,2},{2,1},{3,4},{4,3},{5,6},{6,5},{7,8},{8,7},{9,10},{10,9},{11,... | collective-permute-start | bytes 393224 | tf_op jit(solution)/shard_map/ppermute | solution.py:384
  52.7 12.2 %collective-permute-start.3 = (bf16[8,64,128]{2,1,0:T(8,128)(2,1)S(1)}, bf16[8,64,128]{2,1,0:T(8,128)(2,1)S(1)}, u32[]{:S(2)}, u32[]{:S(2)}) collective-permute-start(bf16[8,64,128]{2,1,0:T(8,128)(2,1)S(1)} %get-tuple-element.39), channel_id=1, source_target_pairs={{0,1},{1,0},{2,3},{3,2},{4,5},{5,4},{6,7},{7,6},{8,9},{9,8},{10,11... | collective-permute-start | bytes 393224 | tf_op jit(solution)/shard_map/ppermute | solution.py:385
  54.6 13.1 %all-to-all-start.3 = ((bf16[16,8,512]{2,1,0:T(8,128)(2,1)}), bf16[16,8,512]{2,1,0:T(8,128)(2,1)S(1)}, u32[]{:S(2)}, u32[]{:S(2)}) async-start(bf16[16,8,512]{2,1,0:T(8,128)(2,1)} %shard_map.83), calls=%async_computation.3 | async-start | bytes 262144 | tf_op jit(solution)/shard_map/all_to_all | solution.py:395

commit v6 on v5

--- a/solution.py
+++ b/solution.py
@@ -67,7 +67,7 @@
         copy.start()
     for copy in copies:
         copy.wait()
-    wide_ref[...] = cot_ref[...].astype(f32)
+    wide_ref[0:512, :] = cot_ref[...].astype(f32)
     weights = weight_ref[...]
     for slot, d in enumerate(ORDER_IN):
         rows = [wide_ref[pl.ds(4 * d + r, 8, stride=64), :] for r in range(4)]
@@ -78,7 +78,7 @@
 def split_columns(own_ref, across_ref, inside_ref, flat_ref, planes_ref):
     columns = jnp.dot(own_ref[...], column_split(), preferred_element_type=f32)
     for e in range(2):
-        flat_ref[e] = columns[:, LANES * e : LANES * e + LANES]
+        flat_ref[e, 0:512, :] = columns[:, LANES * e : LANES * e + LANES]
     for z in range(2):
         for r in range(8):
             for e in range(2):
@@ -278,7 +278,7 @@
                 32 * row : 32 * row + 32, LANES * side : LANES * side + LANES
             ]
     for side in range(2):
-        out_ref[:, LANES * side : LANES * side + LANES] = flat_ref[side].astype(bf16)
+        out_ref[:, LANES * side : LANES * side + LANES] = flat_ref[side, 0:512, :].astype(bf16)
 
 
 def sum_space(got_ref, send_ref):
@@ -291,7 +291,7 @@
     for slot, d in enumerate(ORDER_SLABS):
         for r in range(4):
             wide_ref[pl.ds(4 * d + r, 8, stride=64), :] = got_ref[slot, 0:8, LANES * r : LANES * r + LANES].astype(f32)
-    out_ref[...] = wide_ref[...].astype(bf16)
+    out_ref[...] = wide_ref[0:512, :].astype(bf16)
 
 
 def summed(got_ref, rows):
@@ -337,7 +337,7 @@
         [
             pltpu.VMEM((512, LANES), bf16),
             pltpu.VMEM((8, 512), bf16),
-            pltpu.VMEM((512, LANES), f32),
+            pltpu.VMEM((576, LANES), f32),
             pltpu.SemaphoreType.DMA((2,)),
         ],
         0, 400_000,
@@ -348,7 +348,7 @@
     cells_in, _ = lax.optimization_barrier((volume, send))
     across_vol, inside_vol = call(
         split_columns, (plane, plane),
-        [pltpu.VMEM((2, 512, LANES), f32), pltpu.VMEM((2, 8, 64, LANES), bf16)], 4_000_000_000, 2_000_000,
+        [pltpu.VMEM((2, 528, LANES), f32), pltpu.VMEM((2, 8, 64, LANES), bf16)], 4_000_000_000, 2_000_000,
         cells_in.reshape(512, 256),
     )
     across_got = lax.ppermute(across_vol, "space", between_chips)
@@ -384,7 +384,7 @@
     across_got = lax.ppermute(across_terms, "space", between_chips)
     inside_got = lax.ppermute(inside_terms, "space", in_chip)
     send = call(sum_space, buffer(16, 16, 512), [], 0, 600_000, got)
-    output = call(place_output, shape((512, LANES), bf16), [pltpu.VMEM((512, LANES), f32)], 0, 600_000, got)
+    output = call(place_output, shape((512, LANES), bf16), [pltpu.VMEM((576, LANES), f32)], 0, 600_000, got)
     got = lax.all_to_all(send, "dp", 0, 0, tiled=True, axis_index_groups=[ORDER_SAMPLES])
     send = call(
         functools.partial(sum_conv, 1.0 / math.sqrt(cells)), buffer(16, 8, 512), [], 0, 300_000, got,
@@ -398,7 +398,7 @@
         [
             pltpu.VMEM((2, 8, 64, LANES), f32),
             pltpu.VMEM((512, 256), bf16),
-            pltpu.VMEM((2, 512, LANES), f32),
+            pltpu.VMEM((2, 528, LANES), f32),
         ],
         1_000_000_000, 2_000_000,
         own_terms, across_got, inside_got,

time: 69.1 us -> 69.1 us (level)
  no operation moved by 1% of the time
where the time goes in v6:
time: 69.1 us; the launch traced here: 68.4 us
  starting transfers between devices  40.1 us (58%)
  Pallas kernels  14.4 us (21%)
  waiting for transfers between devices  13.2 us (19%)
  between operations  0.72 us (1%)
    all_to_all x3, starting transfers between devices, shards(): lax.all_to_all(send, 'space', 0, 0, tiled=True, axis_index_groups=[ORDER_...  23.2 us
    pallas_call x11, Pallas kernels, call(): pl.pallas_call(kernel, out_shape=outs, in_specs=[pl.BlockSpec(memory_spac...  14.4 us
    all_to_all x3, waiting for transfers between devices, shards(): lax.all_to_all(send, 'space', 0, 0, tiled=True, axis_index_groups=[ORDER_...  9.89 us
    all_to_all x1, starting transfers between devices, shards(): lax.all_to_all(send, 'dp', 0, 0, tiled=True, axis_index_groups=[ORDER_SAM...  9.28 us
    ppermute x1, starting transfers between devices, shards(): across_got = lax.ppermute(across_terms, 'space', between_chips)  4.85 us
    ppermute x1, waiting for transfers between devices, shards(): across_got = lax.ppermute(across_vol, 'space', between_chips)  2.2 us
    ppermute x1, starting transfers between devices, shards(): across_got = lax.ppermute(across_vol, 'space', between_chips)  2.14 us
  transfers between devices with their start and end apart: 8, of which 5 were waited for; matrix products, arithmetic and copies ran while one was open for 0% of the time, Pallas kernels for 12%

profile of v6, /device:TPU:1, one launch (start us, length us, event | category | flops | bytes accessed | tf_op | source)
XLA Modules:
  0.0 68.4 jit_solution(2355294717649452305)
XLA Ops:
  0.6 1.8 %shard_map.75 = bf16[16,8,1024]{2,1,0:T(8,128)(2,1)} custom-call(bf16[512,128]{1,0:T(8,128)(2,1)} %bitcast.5, bf16[8,512]{1,0:T(8,128)(2,1)} %weight_hbm.1), custom_call_target="tpu_custom_call" | custom-call | bytes 400000 | tf_op jit(solution)/shard_map/pallas_call | solution.py:31
  2.4 0.0 copy-start
  2.5 9.6 %all-to-all-start = ((bf16[16,8,1024]{2,1,0:T(8,128)(2,1)}), bf16[16,8,1024]{2,1,0:T(8,128)(2,1)S(1)}, u32[]{:S(2)}, u32[]{:S(2)}) async-start(bf16[16,8,1024]{2,1,0:T(8,128)(2,1)} %shard_map.75), calls=%async_computation | async-start | bytes 524288 | tf_op jit(solution)/shard_map/all_to_all | solution.py:347
  12.1 0.0 copy-done
  12.1 0.0 copy-start.1
  12.1 0.4 shard_map.76
  12.5 0.5 collective-permute-start.1
  13.1 2.1 %collective-permute-start = (bf16[8,64,128]{2,1,0:T(8,128)(2,1)S(1)}, bf16[8,64,128]{2,1,0:T(8,128)(2,1)S(1)}, u32[]{:S(2)}, u32[]{:S(2)}) collective-permute-start(bf16[8,64,128]{2,1,0:T(8,128)(2,1)S(1)} %get-tuple-element.23.across_own), channel_id=1, source_target_pairs={{1,2},{2,1},{3,4},{4,3},{5,6},{6,5},{7,8},{8,7},{9,10},{10,9},{11,... | collective-permute-start | bytes 393224 | tf_op jit(solution)/shard_map/ppermute | solution.py:354
  15.2 0.0 collective-permute-done.1.inside_got
  15.2 1.8 %all-to-all-done.got_ref = bf16[16,8,1024]{2,1,0:T(8,128)(2,1)S(1)} async-done(((bf16[16,8,1024]{2,1,0:T(8,128)(2,1)}), bf16[16,8,1024]{2,1,0:T(8,128)(2,1)S(1)}, u32[]{:S(2)}, u32[]{:S(2)}) %all-to-all-start) | async-done | bytes 262176 | tf_op jit(solution)/shard_map/all_to_all | solution.py:347
  17.1 0.0 copy-done.1
  17.1 2.7 %shard_map.77 = (bf16[8,128,128]{2,1,0:T(8,128)(2,1)S(1)}, f32[128,1152]{1,0:T(8,128)S(1)}, f32[128,512]{1,0:T(8,128)S(1)}, f32[128,256]{1,0:T(8,128)S(1)}, f32[...) custom-call(bf16[8,64,128]{2,1,0:T(8,128)(2,1)S(1)} %get-tuple-element.23.across_own, ...), custom_call_target="tpu_custom_call" | custom-call | flops 3000000000 | bytes 2000000 | tf_op jit(solution)/shard_map/pallas_call | solution.py:31
  19.7 2.2 %collective-permute-done.across_got = bf16[8,64,128]{2,1,0:T(8,128)(2,1)S(1)} collective-permute-done((bf16[8,64,128]{2,1,0:T(8,128)(2,1)S(1)}, bf16[8,64,128]{2,1,0:T(8,128)(2,1)S(1)}, u32[]{:S(2)}, u32[]{:S(2)}) %collective-permute-start) | collective-permute-done | bytes 131104 | tf_op jit(solution)/shard_map/ppermute | solution.py:354
  21.9 2.6 %shard_map.78 = (bf16[16,24,512]{2,1,0:T(8,128)(2,1)}, bf16[8,128,128]{2,1,0:T(8,128)(2,1)S(1)}) custom-call(bf16[8,64,128]{2,1,0:T(8,128)(2,1)S(1)} %collective-permute-done.across_got, bf16[8,64,128]{2,1,0:T(8,128)(2,1)S(1)} %get-tuple-element.23.across_own, bf16[8,64,128]{2,1,0:T(8,128)(2,1)S(1)} %get-tuple-element.24.inside_own, ...), custom_call_target="tpu_custom_call" | custom-call | flops 3000000000 | bytes 3000000 | tf_op jit(solution)/shard_map/pallas_call | solution.py:31
  24.5 4.1 %all-to-all-start.1 = ((bf16[16,24,512]{2,1,0:T(8,128)(2,1)}), bf16[16,24,512]{2,1,0:T(8,128)(2,1)S(1)}, u32[]{:S(2)}, u32[]{:S(2)}) async-start(bf16[16,24,512]{2,1,0:T(8,128)(2,1)} %get-tuple-element.30), calls=%async_computation.1 | async-start | bytes 786432 | tf_op jit(solution)/shard_map/all_to_all | solution.py:374
  28.6 2.2 %shard_map.79 = (f32[2,8,64,128]{3,2,1,0:T(8,128)S(1)}, bf16[8,64,128]{2,1,0:T(8,128)(2,1)S(1)}, bf16[8,64,128]{2,1,0:T(8,128)(2,1)S(1)}) custom-call(bf16[8,128,128]{2,1,0:T(8,128)(2,1)S(1)} %get-tuple-element.31.across_own, bf16[8,128,128]{2,1,0:T(8,128)(2,1)S(1)} %get-tuple-element.32.inside_own, bf16[64,864]{1,0:T(8,128)(2,1)S(1)} %copy-done.1), custom_call_target="tpu_custom_call" | custom-call | flops 3000000000 | bytes 3000000 | tf_op jit(solution)/shard_map/pallas_call | solution.py:31
  30.8 7.0 %all-to-all-done.1.got_ref = bf16[16,24,512]{2,1,0:T(8,128)(2,1)S(1)} async-done(((bf16[16,24,512]{2,1,0:T(8,128)(2,1)}), bf16[16,24,512]{2,1,0:T(8,128)(2,1)S(1)}, u32[]{:S(2)}, u32[]{:S(2)}) %all-to-all-start.1) | async-done | bytes 393248 | tf_op jit(solution)/shard_map/all_to_all | solution.py:374
  37.8 0.8 %shard_map.82 = bf16[16,16,512]{2,1,0:T(8,128)(2,1)} custom-call(bf16[16,24,512]{2,1,0:T(8,128)(2,1)S(1)} %all-to-all-done.1.got_ref), custom_call_target="tpu_custom_call" | custom-call | bytes 600000 | tf_op jit(solution)/shard_map/pallas_call | solution.py:31
  38.5 9.3 %all-to-all-start.2 = ((bf16[16,16,512]{2,1,0:T(8,128)(2,1)}), bf16[16,16,512]{2,1,0:T(8,128)(2,1)S(1)}, u32[]{:S(2)}, u32[]{:S(2)}) async-start(bf16[16,16,512]{2,1,0:T(8,128)(2,1)} %shard_map.82), calls=%async_computation.2 | async-start | bytes 524288 | tf_op jit(solution)/shard_map/all_to_all | solution.py:388
  47.8 4.9 %collective-permute-start.2 = (bf16[8,64,128]{2,1,0:T(8,128)(2,1)S(1)}, bf16[8,64,128]{2,1,0:T(8,128)(2,1)S(1)}, u32[]{:S(2)}, u32[]{:S(2)}) collective-permute-start(bf16[8,64,128]{2,1,0:T(8,128)(2,1)S(1)} %get-tuple-element.38), channel_id=1, source_target_pairs={{1,2},{2,1},{3,4},{4,3},{5,6},{6,5},{7,8},{8,7},{9,10},{10,9},{11,... | collective-permute-start | bytes 393224 | tf_op jit(solution)/shard_map/ppermute | solution.py:384
  52.7 0.1 collective-permute-start.3
  52.8 1.1 %all-to-all-done.2.got_ref = bf16[16,16,512]{2,1,0:T(8,128)(2,1)S(1)} async-done(((bf16[16,16,512]{2,1,0:T(8,128)(2,1)}), bf16[16,16,512]{2,1,0:T(8,128)(2,1)S(1)}, u32[]{:S(2)}, u32[]{:S(2)}) %all-to-all-start.2) | async-done | bytes 262176 | tf_op jit(solution)/shard_map/all_to_all | solution.py:388
  53.9 0.7 shard_map.83
  54.6 9.5 %all-to-all-start.3 = ((bf16[16,8,512]{2,1,0:T(8,128)(2,1)}), bf16[16,8,512]{2,1,0:T(8,128)(2,1)S(1)}, u32[]{:S(2)}, u32[]{:S(2)}) async-start(bf16[16,8,512]{2,1,0:T(8,128)(2,1)} %shard_map.83), calls=%async_computation.3 | async-start | bytes 262144 | tf_op jit(solution)/shard_map/all_to_all | solution.py:395
  64.0 0.8 %shard_map.80 = bf16[512,128]{1,0:T(8,128)(2,1)} custom-call(bf16[16,24,512]{2,1,0:T(8,128)(2,1)S(1)} %all-to-all-done.1.got_ref), custom_call_target="tpu_custom_call" | custom-call | bytes 600000 | tf_op jit(solution)/shard_map/pallas_call | solution.py:31
  64.9 0.0 collective-permute-done.2.across_got
  64.9 0.0 collective-permute-done.3.inside_got
  64.9 1.1 %shard_map.81 = bf16[512,256]{1,0:T(8,128)(2,1)} custom-call(f32[2,8,64,128]{3,2,1,0:T(8,128)S(1)} %get-tuple-element.37.own_ref, bf16[8,64,128]{2,1,0:T(8,128)(2,1)S(1)} %collective-permute-done.2.across_got, bf16[8,64,128]{2,1,0:T(8,128)(2,1)S(1)} %collective-permute-done.3.inside_got), custom_call_target="tpu_custom_call" | custom-call | flops 1000000000 | bytes 2000000 | tf_op jit(solution)/shard_map/pallas_call | solution.py:31
  66.0 0.6 shard_map.85
  66.6 1.1 %all-to-all-done.3.got_ref = bf16[16,8,512]{2,1,0:T(8,128)(2,1)S(1)} async-done(((bf16[16,8,512]{2,1,0:T(8,128)(2,1)}), bf16[16,8,512]{2,1,0:T(8,128)(2,1)S(1)}, u32[]{:S(2)}, u32[]{:S(2)}) %all-to-all-start.3) | async-done | bytes 131104 | tf_op jit(solution)/shard_map/all_to_all | solution.py:395
  67.7 0.7 %shard_map.84 = f32[64,864]{1,0:T(8,128)} custom-call(bf16[16,8,512]{2,1,0:T(8,128)(2,1)S(1)} %all-to-all-done.3.got_ref), custom_call_target="tpu_custom_call" | custom-call | bytes 300000 | tf_op jit(solution)/shard_map/pallas_call | solution.py:31
Async XLA Ops:
  2.4 9.7 %copy-start = (bf16[1,32,2,8,256]{4,3,2,1,0:T(8,128)(2,1)S(1)}, bf16[1,32,2,8,256]{4,3,2,1,0:T(8,128)(2,1)}, u32[]{:S(2)}) copy-start(bf16[1,32,2,8,256]{4,3,2,1,0:T(8,128)(2,1)} %param.4) | copy-start | bytes 786436
  2.5 14.6 %all-to-all-start = ((bf16[16,8,1024]{2,1,0:T(8,128)(2,1)}), bf16[16,8,1024]{2,1,0:T(8,128)(2,1)S(1)}, u32[]{:S(2)}, u32[]{:S(2)}) async-start(bf16[16,8,1024]{2,1,0:T(8,128)(2,1)} %shard_map.75), calls=%async_computation | async-start | bytes 524288 | tf_op jit(solution)/shard_map/all_to_all | solution.py:347
  12.1 5.0 %copy-start.1 = (bf16[64,864]{1,0:T(8,128)(2,1)S(1)}, bf16[64,864]{1,0:T(8,128)(2,1)}, u32[]{:S(2)}) copy-start(bf16[64,864]{1,0:T(8,128)(2,1)} %weight_ref.5) | copy-start | bytes 331780
  12.5 2.7 %collective-permute-start.1 = (bf16[8,64,128]{2,1,0:T(8,128)(2,1)S(1)}, bf16[8,64,128]{2,1,0:T(8,128)(2,1)S(1)}, u32[]{:S(2)}, u32[]{:S(2)}) collective-permute-start(bf16[8,64,128]{2,1,0:T(8,128)(2,1)S(1)} %get-tuple-element.24.inside_own), channel_id=1, source_target_pairs={{0,1},{1,0},{2,3},{3,2},{4,5},{5,4},{6,7},{7,6},{8,9},{9,8},{10,11... | collective-permute-start | bytes 393224 | tf_op jit(solution)/shard_map/ppermute | solution.py:355
  13.1 8.9 %collective-permute-start = (bf16[8,64,128]{2,1,0:T(8,128)(2,1)S(1)}, bf16[8,64,128]{2,1,0:T(8,128)(2,1)S(1)}, u32[]{:S(2)}, u32[]{:S(2)}) collective-permute-start(bf16[8,64,128]{2,1,0:T(8,128)(2,1)S(1)} %get-tuple-element.23.across_own), channel_id=1, source_target_pairs={{1,2},{2,1},{3,4},{4,3},{5,6},{6,5},{7,8},{8,7},{9,10},{10,9},{11,... | collective-permute-start | bytes 393224 | tf_op jit(solution)/shard_map/ppermute | solution.py:354
  24.5 13.2 %all-to-all-start.1 = ((bf16[16,24,512]{2,1,0:T(8,128)(2,1)}), bf16[16,24,512]{2,1,0:T(8,128)(2,1)S(1)}, u32[]{:S(2)}, u32[]{:S(2)}) async-start(bf16[16,24,512]{2,1,0:T(8,128)(2,1)} %get-tuple-element.30), calls=%async_computation.1 | async-start | bytes 786432 | tf_op jit(solution)/shard_map/all_to_all | solution.py:374
  38.5 15.4 %all-to-all-start.2 = ((bf16[16,16,512]{2,1,0:T(8,128)(2,1)}), bf16[16,16,512]{2,1,0:T(8,128)(2,1)S(1)}, u32[]{:S(2)}, u32[]{:S(2)}) async-start(bf16[16,16,512]{2,1,0:T(8,128)(2,1)} %shard_map.82), calls=%async_computation.2 | async-start | bytes 524288 | tf_op jit(solution)/shard_map/all_to_all | solution.py:388
  47.8 17.1 %collective-permute-start.2 = (bf16[8,64,128]{2,1,0:T(8,128)(2,1)S(1)}, bf16[8,64,128]{2,1,0:T(8,128)(2,1)S(1)}, u32[]{:S(2)}, u32[]{:S(2)}) collective-permute-start(bf16[8,64,128]{2,1,0:T(8,128)(2,1)S(1)} %get-tuple-element.38), channel_id=1, source_target_pairs={{1,2},{2,1},{3,4},{4,3},{5,6},{6,5},{7,8},{8,7},{9,10},{10,9},{11,... | collective-permute-start | bytes 393224 | tf_op jit(solution)/shard_map/ppermute | solution.py:384
  52.7 12.2 %collective-permute-start.3 = (bf16[8,64,128]{2,1,0:T(8,128)(2,1)S(1)}, bf16[8,64,128]{2,1,0:T(8,128)(2,1)S(1)}, u32[]{:S(2)}, u32[]{:S(2)}) collective-permute-start(bf16[8,64,128]{2,1,0:T(8,128)(2,1)S(1)} %get-tuple-element.39), channel_id=1, source_target_pairs={{0,1},{1,0},{2,3},{3,2},{4,5},{5,4},{6,7},{7,6},{8,9},{9,8},{10,11... | collective-permute-start | bytes 393224 | tf_op jit(solution)/shard_map/ppermute | solution.py:385
  54.6 13.1 %all-to-all-start.3 = ((bf16[16,8,512]{2,1,0:T(8,128)(2,1)}), bf16[16,8,512]{2,1,0:T(8,128)(2,1)S(1)}, u32[]{:S(2)}, u32[]{:S(2)}) async-start(bf16[16,8,512]{2,1,0:T(8,128)(2,1)} %shard_map.83), calls=%async_computation.3 | async-start | bytes 262144 | tf_op jit(solution)/shard_map/all_to_all | solution.py:395

commit v7 on v6

--- a/solution.py
+++ b/solution.py
@@ -264,7 +264,10 @@
     inside_ref[...] = ends_ref[1 - core]
 
 
-def finish(own_ref, across_got, inside_got, out_ref, sum_ref, turn_ref, flat_ref):
+def finish(scale, got_ref, sums_ref, own_ref, across_got, inside_got, output_ref, strided_ref, out_ref,
+           wide_ref, sum_ref, turn_ref, flat_ref):
+    place_output(got_ref, output_ref, wide_ref)
+    strided_ref[...] = summed(sums_ref, slice(0, 8)) * scale
     core = core_index()
     sum_ref[core] = own_ref[core] + across_got[...].astype(f32)
     sum_ref[1 - core] = own_ref[1 - core] + inside_got[...].astype(f32)
@@ -307,10 +310,6 @@
         send_ref[j] = conv
 
 
-def sum_strided(scale, got_ref, strided_ref):
-    strided_ref[...] = summed(got_ref, slice(0, 8)) * scale
-
-
 def place_conv(got_ref, out_ref):
     for slot, j in enumerate(ORDER_OUT):
         rows, side = 8 * (j // 2), 512 * (j % 2)
@@ -384,24 +383,24 @@
     across_got = lax.ppermute(across_terms, "space", between_chips)
     inside_got = lax.ppermute(inside_terms, "space", in_chip)
     send = call(sum_space, buffer(16, 16, 512), [], 0, 600_000, got)
-    output = call(place_output, shape((512, LANES), bf16), [pltpu.VMEM((576, LANES), f32)], 0, 600_000, got)
+    got_out = got
     got = lax.all_to_all(send, "dp", 0, 0, tiled=True, axis_index_groups=[ORDER_SAMPLES])
     send = call(
         functools.partial(sum_conv, 1.0 / math.sqrt(cells)), buffer(16, 8, 512), [], 0, 300_000, got,
     )
-    strided_grad = call(
-        functools.partial(sum_strided, 1.0 / math.sqrt(cells / 8)), shape((8, 512), f32), [], 0, 300_000, got,
-    )
+    sums = got
     got = lax.all_to_all(send, "space", 0, 0, tiled=True, axis_index_groups=[ORDER_OUT])
-    vol_grad = call(
-        finish, shape((512, 256), bf16),
+    output, strided_grad, vol_grad = call(
+        functools.partial(finish, 1.0 / math.sqrt(cells / 8)),
+        (shape((512, LANES), bf16), shape((8, 512), f32), shape((512, 256), bf16)),
         [
+            pltpu.VMEM((576, LANES), f32),
             pltpu.VMEM((2, 8, 64, LANES), f32),
             pltpu.VMEM((512, 256), bf16),
             pltpu.VMEM((2, 528, LANES), f32),
         ],
         1_000_000_000, 2_000_000,
-        own_terms, across_got, inside_got,
+        got_out, sums, own_terms, across_got, inside_got,
     )
     conv_grad = call(place_conv, shape((64, 864), f32), [], 0, 300_000, got)
     return output.reshape(cotangent.shape), vol_grad.reshape(volume.shape), conv_grad, strided_grad

time: 69.1 us -> 69.2 us (level)
  Pallas kernels: 14.4 us -> 13.1 us
  waiting for transfers between devices: 13.2 us -> 14.5 us
    pallas_call x11 -> x9, Pallas kernels: 14.4 us -> 13.1 us  [call(): pl.pallas_call(kernel, out_shape=outs, in_specs=[pl.BlockSpec(memory_spac...]
    all_to_all x3, waiting for transfers between devices: 9.89 us -> 11.2 us  [shards(): lax.all_to_all(send, 'space', 0, 0, tiled=True, axis_index_groups=[ORDER_...]
  transfers between devices with their start and end apart: 8 -> 8, of which waited for: 5 -> 5; matrix products, arithmetic and copies ran while one was open for 0% -> 0% of each run, Pallas kernels for 12% -> 11%
where the time goes in v7:
time: 69.2 us; the launch traced here: 68.4 us
  starting transfers between devices  40.1 us (58%)
  waiting for transfers between devices  14.5 us (21%)
  Pallas kernels  13.1 us (19%)
  between operations  0.72 us (1%)
    all_to_all x3, starting transfers between devices, shards(): lax.all_to_all(send, 'space', 0, 0, tiled=True, axis_index_groups=[ORDER_...  23.2 us
    pallas_call x9, Pallas kernels, call(): pl.pallas_call(kernel, out_shape=outs, in_specs=[pl.BlockSpec(memory_spac...  13.1 us
    all_to_all x3, waiting for transfers between devices, shards(): lax.all_to_all(send, 'space', 0, 0, tiled=True, axis_index_groups=[ORDER_...  11.2 us
    all_to_all x1, starting transfers between devices, shards(): lax.all_to_all(send, 'dp', 0, 0, tiled=True, axis_index_groups=[ORDER_SAM...  9.28 us
    ppermute x1, starting transfers between devices, shards(): across_got = lax.ppermute(across_terms, 'space', between_chips)  4.85 us
    ppermute x1, waiting for transfers between devices, shards(): across_got = lax.ppermute(across_vol, 'space', between_chips)  2.2 us
    ppermute x1, starting transfers between devices, shards(): across_got = lax.ppermute(across_vol, 'space', between_chips)  2.14 us
  transfers between devices with their start and end apart: 8, of which 5 were waited for; matrix products, arithmetic and copies ran while one was open for 0% of the time, Pallas kernels for 11%

profile of v7, /device:TPU:1, one launch (start us, length us, event | category | flops | bytes accessed | tf_op | source)
XLA Modules:
  0.0 68.4 jit_solution(849254596444131156)
XLA Ops:
  0.6 1.8 %shard_map.75 = bf16[16,8,1024]{2,1,0:T(8,128)(2,1)} custom-call(bf16[512,128]{1,0:T(8,128)(2,1)} %bitcast.5, bf16[8,512]{1,0:T(8,128)(2,1)} %weight_hbm.1), custom_call_target="tpu_custom_call" | custom-call | bytes 400000 | tf_op jit(solution)/shard_map/pallas_call | solution.py:31
  2.4 0.0 copy-start
  2.5 9.6 %all-to-all-start = ((bf16[16,8,1024]{2,1,0:T(8,128)(2,1)}), bf16[16,8,1024]{2,1,0:T(8,128)(2,1)S(1)}, u32[]{:S(2)}, u32[]{:S(2)}) async-start(bf16[16,8,1024]{2,1,0:T(8,128)(2,1)} %shard_map.75), calls=%async_computation | async-start | bytes 524288 | tf_op jit(solution)/shard_map/all_to_all | solution.py:346
  12.1 0.0 copy-done
  12.1 0.0 copy-start.1
  12.1 0.4 shard_map.76
  12.5 0.5 collective-permute-start.1
  13.1 2.1 %collective-permute-start = (bf16[8,64,128]{2,1,0:T(8,128)(2,1)S(1)}, bf16[8,64,128]{2,1,0:T(8,128)(2,1)S(1)}, u32[]{:S(2)}, u32[]{:S(2)}) collective-permute-start(bf16[8,64,128]{2,1,0:T(8,128)(2,1)S(1)} %get-tuple-element.26.across_own), channel_id=1, source_target_pairs={{1,2},{2,1},{3,4},{4,3},{5,6},{6,5},{7,8},{8,7},{9,10},{10,9},{11,... | collective-permute-start | bytes 393224 | tf_op jit(solution)/shard_map/ppermute | solution.py:353
  15.2 0.0 collective-permute-done.1.inside_got
  15.2 1.8 %all-to-all-done.got_ref = bf16[16,8,1024]{2,1,0:T(8,128)(2,1)S(1)} async-done(((bf16[16,8,1024]{2,1,0:T(8,128)(2,1)}), bf16[16,8,1024]{2,1,0:T(8,128)(2,1)S(1)}, u32[]{:S(2)}, u32[]{:S(2)}) %all-to-all-start) | async-done | bytes 262176 | tf_op jit(solution)/shard_map/all_to_all | solution.py:346
  17.1 0.0 copy-done.1
  17.1 2.7 %shard_map.77 = (bf16[8,128,128]{2,1,0:T(8,128)(2,1)S(1)}, f32[128,1152]{1,0:T(8,128)S(1)}, f32[128,512]{1,0:T(8,128)S(1)}, f32[128,256]{1,0:T(8,128)S(1)}, f32[...) custom-call(bf16[8,64,128]{2,1,0:T(8,128)(2,1)S(1)} %get-tuple-element.26.across_own, ...), custom_call_target="tpu_custom_call" | custom-call | flops 3000000000 | bytes 2000000 | tf_op jit(solution)/shard_map/pallas_call | solution.py:31
  19.7 2.2 %collective-permute-done.across_got = bf16[8,64,128]{2,1,0:T(8,128)(2,1)S(1)} collective-permute-done((bf16[8,64,128]{2,1,0:T(8,128)(2,1)S(1)}, bf16[8,64,128]{2,1,0:T(8,128)(2,1)S(1)}, u32[]{:S(2)}, u32[]{:S(2)}) %collective-permute-start) | collective-permute-done | bytes 131104 | tf_op jit(solution)/shard_map/ppermute | solution.py:353
  21.9 2.6 %shard_map.78 = (bf16[16,24,512]{2,1,0:T(8,128)(2,1)}, bf16[8,128,128]{2,1,0:T(8,128)(2,1)S(1)}) custom-call(bf16[8,64,128]{2,1,0:T(8,128)(2,1)S(1)} %collective-permute-done.across_got, bf16[8,64,128]{2,1,0:T(8,128)(2,1)S(1)} %get-tuple-element.26.across_own, bf16[8,64,128]{2,1,0:T(8,128)(2,1)S(1)} %get-tuple-element.27.inside_own, ...), custom_call_target="tpu_custom_call" | custom-call | flops 3000000000 | bytes 3000000 | tf_op jit(solution)/shard_map/pallas_call | solution.py:31
  24.5 4.1 %all-to-all-start.1 = ((bf16[16,24,512]{2,1,0:T(8,128)(2,1)}), bf16[16,24,512]{2,1,0:T(8,128)(2,1)S(1)}, u32[]{:S(2)}, u32[]{:S(2)}) async-start(bf16[16,24,512]{2,1,0:T(8,128)(2,1)} %get-tuple-element.33), calls=%async_computation.1 | async-start | bytes 786432 | tf_op jit(solution)/shard_map/all_to_all | solution.py:373
  28.6 2.2 %shard_map.79 = (f32[2,8,64,128]{3,2,1,0:T(8,128)S(1)}, bf16[8,64,128]{2,1,0:T(8,128)(2,1)S(1)}, bf16[8,64,128]{2,1,0:T(8,128)(2,1)S(1)}) custom-call(bf16[8,128,128]{2,1,0:T(8,128)(2,1)S(1)} %get-tuple-element.34.across_own, bf16[8,128,128]{2,1,0:T(8,128)(2,1)S(1)} %get-tuple-element.35.inside_own, bf16[64,864]{1,0:T(8,128)(2,1)S(1)} %copy-done.1), custom_call_target="tpu_custom_call" | custom-call | flops 3000000000 | bytes 3000000 | tf_op jit(solution)/shard_map/pallas_call | solution.py:31
  30.8 6.9 %all-to-all-done.1.got_ref = bf16[16,24,512]{2,1,0:T(8,128)(2,1)S(1)} async-done(((bf16[16,24,512]{2,1,0:T(8,128)(2,1)}), bf16[16,24,512]{2,1,0:T(8,128)(2,1)S(1)}, u32[]{:S(2)}, u32[]{:S(2)}) %all-to-all-start.1) | async-done | bytes 393248 | tf_op jit(solution)/shard_map/all_to_all | solution.py:373
  37.8 0.8 %shard_map.80 = bf16[16,16,512]{2,1,0:T(8,128)(2,1)} custom-call(bf16[16,24,512]{2,1,0:T(8,128)(2,1)S(1)} %all-to-all-done.1.got_ref), custom_call_target="tpu_custom_call" | custom-call | bytes 600000 | tf_op jit(solution)/shard_map/pallas_call | solution.py:31
  38.5 9.3 %all-to-all-start.2 = ((bf16[16,16,512]{2,1,0:T(8,128)(2,1)}), bf16[16,16,512]{2,1,0:T(8,128)(2,1)S(1)}, u32[]{:S(2)}, u32[]{:S(2)}) async-start(bf16[16,16,512]{2,1,0:T(8,128)(2,1)} %shard_map.80), calls=%async_computation.2 | async-start | bytes 524288 | tf_op jit(solution)/shard_map/all_to_all | solution.py:387
  47.8 4.9 %collective-permute-start.2 = (bf16[8,64,128]{2,1,0:T(8,128)(2,1)S(1)}, bf16[8,64,128]{2,1,0:T(8,128)(2,1)S(1)}, u32[]{:S(2)}, u32[]{:S(2)}) collective-permute-start(bf16[8,64,128]{2,1,0:T(8,128)(2,1)S(1)} %get-tuple-element.41), channel_id=1, source_target_pairs={{1,2},{2,1},{3,4},{4,3},{5,6},{6,5},{7,8},{8,7},{9,10},{10,9},{11,... | collective-permute-start | bytes 393224 | tf_op jit(solution)/shard_map/ppermute | solution.py:383
  52.7 0.1 collective-permute-start.3
  52.8 1.1 %all-to-all-done.2.sums_ref.got_ref = bf16[16,16,512]{2,1,0:T(8,128)(2,1)S(1)} async-done(((bf16[16,16,512]{2,1,0:T(8,128)(2,1)}), bf16[16,16,512]{2,1,0:T(8,128)(2,1)S(1)}, u32[]{:S(2)}, u32[]{:S(2)}) %all-to-all-start.2) | async-done | bytes 262176 | tf_op jit(solution)/shard_map/all_to_all | solution.py:387
  53.9 0.7 shard_map.82
  54.6 9.5 %all-to-all-start.3 = ((bf16[16,8,512]{2,1,0:T(8,128)(2,1)}), bf16[16,8,512]{2,1,0:T(8,128)(2,1)S(1)}, u32[]{:S(2)}, u32[]{:S(2)}) async-start(bf16[16,8,512]{2,1,0:T(8,128)(2,1)} %shard_map.82), calls=%async_computation.3 | async-start | bytes 262144 | tf_op jit(solution)/shard_map/all_to_all | solution.py:392
  64.0 0.0 collective-permute-done.2.across_got
  64.0 0.0 collective-permute-done.3.inside_got
  64.1 1.3 %shard_map.81 = (bf16[512,128]{1,0:T(8,128)(2,1)}, f32[8,512]{1,0:T(8,128)}, bf16[512,256]{1,0:T(8,128)(2,1)}) custom-call(bf16[16,24,512]{2,1,0:T(8,128)(2,1)S(1)} %all-to-all-done.1.got_ref, bf16[16,16,512]{2,1,0:T(8,128)(2,1)S(1)} %all-to-all-done.2.sums_ref.got_ref, f32[2,8,64,128]{3,2,1,0:T(8,128)S(1)} %get-tuple-element.40.own_ref, ...), custom_call_target="tpu_custom_call" | custom-call | flops 1000000000 | bytes 2000000 | tf_op jit(solution)/shard_map/pallas_call | solution.py:31
  65.3 2.4 %all-to-all-done.3.got_ref = bf16[16,8,512]{2,1,0:T(8,128)(2,1)S(1)} async-done(((bf16[16,8,512]{2,1,0:T(8,128)(2,1)}), bf16[16,8,512]{2,1,0:T(8,128)(2,1)S(1)}, u32[]{:S(2)}, u32[]{:S(2)}) %all-to-all-start.3) | async-done | bytes 131104 | tf_op jit(solution)/shard_map/all_to_all | solution.py:392
  67.7 0.7 %shard_map.83 = f32[64,864]{1,0:T(8,128)} custom-call(bf16[16,8,512]{2,1,0:T(8,128)(2,1)S(1)} %all-to-all-done.3.got_ref), custom_call_target="tpu_custom_call" | custom-call | bytes 300000 | tf_op jit(solution)/shard_map/pallas_call | solution.py:31
Async XLA Ops:
  2.4 9.7 %copy-start = (bf16[1,32,2,8,256]{4,3,2,1,0:T(8,128)(2,1)S(1)}, bf16[1,32,2,8,256]{4,3,2,1,0:T(8,128)(2,1)}, u32[]{:S(2)}) copy-start(bf16[1,32,2,8,256]{4,3,2,1,0:T(8,128)(2,1)} %param.4) | copy-start | bytes 786436
  2.5 14.6 %all-to-all-start = ((bf16[16,8,1024]{2,1,0:T(8,128)(2,1)}), bf16[16,8,1024]{2,1,0:T(8,128)(2,1)S(1)}, u32[]{:S(2)}, u32[]{:S(2)}) async-start(bf16[16,8,1024]{2,1,0:T(8,128)(2,1)} %shard_map.75), calls=%async_computation | async-start | bytes 524288 | tf_op jit(solution)/shard_map/all_to_all | solution.py:346
  12.1 5.0 %copy-start.1 = (bf16[64,864]{1,0:T(8,128)(2,1)S(1)}, bf16[64,864]{1,0:T(8,128)(2,1)}, u32[]{:S(2)}) copy-start(bf16[64,864]{1,0:T(8,128)(2,1)} %weight_ref.5) | copy-start | bytes 331780
  12.5 2.7 %collective-permute-start.1 = (bf16[8,64,128]{2,1,0:T(8,128)(2,1)S(1)}, bf16[8,64,128]{2,1,0:T(8,128)(2,1)S(1)}, u32[]{:S(2)}, u32[]{:S(2)}) collective-permute-start(bf16[8,64,128]{2,1,0:T(8,128)(2,1)S(1)} %get-tuple-element.27.inside_own), channel_id=1, source_target_pairs={{0,1},{1,0},{2,3},{3,2},{4,5},{5,4},{6,7},{7,6},{8,9},{9,8},{10,11... | collective-permute-start | bytes 393224 | tf_op jit(solution)/shard_map/ppermute | solution.py:354
  13.1 8.9 %collective-permute-start = (bf16[8,64,128]{2,1,0:T(8,128)(2,1)S(1)}, bf16[8,64,128]{2,1,0:T(8,128)(2,1)S(1)}, u32[]{:S(2)}, u32[]{:S(2)}) collective-permute-start(bf16[8,64,128]{2,1,0:T(8,128)(2,1)S(1)} %get-tuple-element.26.across_own), channel_id=1, source_target_pairs={{1,2},{2,1},{3,4},{4,3},{5,6},{6,5},{7,8},{8,7},{9,10},{10,9},{11,... | collective-permute-start | bytes 393224 | tf_op jit(solution)/shard_map/ppermute | solution.py:353
  24.5 13.2 %all-to-all-start.1 = ((bf16[16,24,512]{2,1,0:T(8,128)(2,1)}), bf16[16,24,512]{2,1,0:T(8,128)(2,1)S(1)}, u32[]{:S(2)}, u32[]{:S(2)}) async-start(bf16[16,24,512]{2,1,0:T(8,128)(2,1)} %get-tuple-element.33), calls=%async_computation.1 | async-start | bytes 786432 | tf_op jit(solution)/shard_map/all_to_all | solution.py:373
  38.5 15.4 %all-to-all-start.2 = ((bf16[16,16,512]{2,1,0:T(8,128)(2,1)}), bf16[16,16,512]{2,1,0:T(8,128)(2,1)S(1)}, u32[]{:S(2)}, u32[]{:S(2)}) async-start(bf16[16,16,512]{2,1,0:T(8,128)(2,1)} %shard_map.80), calls=%async_computation.2 | async-start | bytes 524288 | tf_op jit(solution)/shard_map/all_to_all | solution.py:387
  47.8 16.2 %collective-permute-start.2 = (bf16[8,64,128]{2,1,0:T(8,128)(2,1)S(1)}, bf16[8,64,128]{2,1,0:T(8,128)(2,1)S(1)}, u32[]{:S(2)}, u32[]{:S(2)}) collective-permute-start(bf16[8,64,128]{2,1,0:T(8,128)(2,1)S(1)} %get-tuple-element.41), channel_id=1, source_target_pairs={{1,2},{2,1},{3,4},{4,3},{5,6},{6,5},{7,8},{8,7},{9,10},{10,9},{11,... | collective-permute-start | bytes 393224 | tf_op jit(solution)/shard_map/ppermute | solution.py:383
  52.7 11.4 %collective-permute-start.3 = (bf16[8,64,128]{2,1,0:T(8,128)(2,1)S(1)}, bf16[8,64,128]{2,1,0:T(8,128)(2,1)S(1)}, u32[]{:S(2)}, u32[]{:S(2)}) collective-permute-start(bf16[8,64,128]{2,1,0:T(8,128)(2,1)S(1)} %get-tuple-element.42), channel_id=1, source_target_pairs={{0,1},{1,0},{2,3},{3,2},{4,5},{5,4},{6,7},{7,6},{8,9},{9,8},{10,11... | collective-permute-start | bytes 393224 | tf_op jit(solution)/shard_map/ppermute | solution.py:384
  54.6 13.1 %all-to-all-start.3 = ((bf16[16,8,512]{2,1,0:T(8,128)(2,1)}), bf16[16,8,512]{2,1,0:T(8,128)(2,1)S(1)}, u32[]{:S(2)}, u32[]{:S(2)}) async-start(bf16[16,8,512]{2,1,0:T(8,128)(2,1)} %shard_map.82), calls=%async_computation.3 | async-start | bytes 262144 | tf_op jit(solution)/shard_map/all_to_all | solution.py:392
